TPU v7x, 32 devices: a whole 2x2x4 slice. The times are simulated.
32 devices in a mesh: dp: 8 (over z, core), tensor: 4 (over y, x).
Axes of the slice: x: 2, y: 2, z: 4, core: 2. Of those that a mesh axis runs over, the one named last changes fastest.
Arguments:
- tokens: bfloat16 [16384, 1536], P(('dp', 'tensor')), may hold values from -6 to 6
- cotangent: bfloat16 [16384, 1536], P(('dp', 'tensor')), may hold values from -6 to 6
- first_gain: float32 [1536], replicated, may hold values from 0.1 to 1.9
- query_weight: bfloat16 [1536, 1536], P('dp', 'tensor'), may hold values from -0.15625 to 0.15625
- key_weight: bfloat16 [1536, 768], P('dp', 'tensor'), may hold values from -0.15625 to 0.15625
- value_weight: bfloat16 [1536, 768], P('dp', 'tensor'), may hold values from -0.15625 to 0.15625
- out_weight: bfloat16 [1536, 1536], P('tensor', 'dp'), may hold values from -0.625 to 0.625
- second_gain: float32 [1536], replicated, may hold values from 0.1 to 1.9
- gate_weight: bfloat16 [1536, 4096], P('dp', 'tensor'), may hold values from -0.15625 to 0.15625
- up_weight: bfloat16 [1536, 4096], P('dp', 'tensor'), may hold values from -0.15625 to 0.15625
- down_weight: bfloat16 [4096, 1536], P('tensor', 'dp'), may hold values from -0.1875 to 0.1875
Outputs:
- result: bfloat16 [16384, 1536], P(('dp', 'tensor'))
- tokens_grad: float32 [16384, 1536], P(('dp', 'tensor'))
- query_grad: float32 [1536, 1536], P('dp', 'tensor')
- key_grad: float32 [1536, 768], P('dp', 'tensor')
- value_grad: float32 [1536, 768], P('dp', 'tensor')
- out_grad: float32 [1536, 1536], P('tensor', 'dp')
- gate_grad: float32 [1536, 4096], P('dp', 'tensor')
- up_grad: float32 [1536, 4096], P('dp', 'tensor')
- down_grad: float32 [4096, 1536], P('tensor', 'dp')
- first_gain_grad: float32 [1536], P(('dp', 'tensor'))
- second_gain_grad: float32 [1536], P(('dp', 'tensor'))
All inputs are finite; a program needn't handle non-finite values.
Results may differ from a plain program's by a relative error of at most 0.02.
Values may be sent and summed in bfloat16 or wider, within the bound.
A program may use at most 192 MiB of HBM per device.

v0:
```python
import jax
import jax.numpy as jnp
from jax import lax
from jax.sharding import PartitionSpec as P

HD = 96
SEQ_LEN = 1024


EPSILON = 1e-05
THETA = 100000.0
MASKED = -1e30


def normed(inputs, gain):
    factor = lax.rsqrt(jnp.mean(inputs * inputs, axis=-1, keepdims=True) + EPSILON)
    return inputs * factor * gain


def rotate(vectors, direction):
    seq_rows, head_count, head_size = vectors.shape
    half_size = head_size // 2
    position = (jnp.arange(seq_rows, dtype=jnp.int32) % SEQ_LEN).astype(jnp.float32)
    inverse = THETA ** (-2.0 * jnp.arange(half_size, dtype=jnp.float32) / head_size)
    angles = position[:, None] * inverse[None, :]
    cosine = jnp.cos(angles)[:, None, :]
    sine_part = direction * jnp.sin(angles)[:, None, :]
    leading = vectors[..., :half_size]
    trailing = vectors[..., half_size:]
    return jnp.concatenate(
        [leading * cosine - trailing * sine_part, trailing * cosine + leading * sine_part], axis=-1
    )


def times_transposed(left, right):
    return lax.dot_general(
        left, right, (((1,), (1,)), ((), ())), preferred_element_type=jnp.float32
    )


def transposed_times(left, right):
    return lax.dot_general(
        left, right, (((0,), (0,)), ((), ())), preferred_element_type=jnp.float32
    )


def scaled_scores(queries, keys_rot):
    raw_scores = jnp.einsum(
        "qhgd,khd->hgqk", queries, keys_rot, preferred_element_type=jnp.float32
    ) * queries.shape[-1] ** (-0.5)
    length_rows = queries.shape[0]
    causal = jnp.arange(length_rows)[:, None] >= jnp.arange(length_rows)[None, :]
    return jnp.where(causal, raw_scores, MASKED)


def attend_forward(operands):
    queries, keys_rot, values = operands
    scores = scaled_scores(queries, keys_rot)
    row_max = jnp.max(scores, axis=-1, keepdims=True)
    weights = jnp.exp(scores - row_max)
    row_total = jnp.sum(weights, axis=-1, keepdims=True)
    softmax = (weights / row_total).astype(jnp.bfloat16)
    mixed_heads = jnp.einsum("hgqk,khd->qhgd", softmax, values, preferred_element_type=jnp.float32)
    return (mixed_heads.astype(jnp.bfloat16), (row_max + jnp.log(row_total))[..., 0])


def attend_backward(operands):
    queries, keys_rot, values, grad_mixed, log_total = operands
    scores = scaled_scores(queries, keys_rot)
    softmax = jnp.exp(scores - log_total[..., None])
    grad_softmax = jnp.einsum(
        "qhgd,khd->hgqk", grad_mixed, values, preferred_element_type=jnp.float32
    )
    grad_values = jnp.einsum(
        "hgqk,qhgd->khd",
        softmax.astype(jnp.bfloat16),
        grad_mixed,
        preferred_element_type=jnp.float32,
    )
    row_inner = jnp.sum(softmax * grad_softmax, axis=-1, keepdims=True)
    grad_scores = (softmax * (grad_softmax - row_inner)).astype(jnp.bfloat16)
    scale_factor = queries.shape[-1] ** (-0.5)
    grad_queries = (
        jnp.einsum("hgqk,khd->qhgd", grad_scores, keys_rot, preferred_element_type=jnp.float32)
        * scale_factor
    )
    grad_keys = (
        jnp.einsum("hgqk,qhgd->khd", grad_scores, queries, preferred_element_type=jnp.float32)
        * scale_factor
    )
    return (grad_queries, grad_keys, grad_values)


def gather_rows(shard):
    return lax.all_gather(shard, "tensor", axis=0, tiled=True)


def gather_grads(shard):
    return lax.all_gather(shard, "tensor", axis=0, tiled=True)


def sum_outputs(term, row_count):
    return lax.psum_scatter(
        term(jnp.int32(0), row_count * lax.axis_size("tensor")),
        "tensor",
        scatter_dimension=0,
        tiled=True,
    )


def sum_inputs(term, row_count):
    return lax.psum_scatter(
        term(jnp.int32(0), row_count * lax.axis_size("tensor")),
        "tensor",
        scatter_dimension=0,
        tiled=True,
    )


def local(
    tokens,
    cotangent,
    first_gain,
    query_weight,
    key_weight,
    value_weight,
    out_weight,
    second_gain,
    gate_weight,
    up_weight,
    down_weight,
):
    query_weight, key_weight, value_weight, out_weight, gate_weight, up_weight, down_weight = (
        lax.all_gather(query_weight, "dp", axis=0, tiled=True),
        lax.all_gather(key_weight, "dp", axis=0, tiled=True),
        lax.all_gather(value_weight, "dp", axis=0, tiled=True),
        lax.all_gather(out_weight, "dp", axis=1, tiled=True),
        lax.all_gather(gate_weight, "dp", axis=0, tiled=True),
        lax.all_gather(up_weight, "dp", axis=0, tiled=True),
        lax.all_gather(down_weight, "dp", axis=1, tiled=True),
    )
    own_rows = tokens.astype(jnp.float32)
    row_count = own_rows.shape[0]
    pair_count = key_weight.shape[1] // HD
    first_normed = normed(own_rows, first_gain).astype(jnp.bfloat16)
    first_rows = gather_rows(first_normed)
    group_rows = first_rows.shape[0]
    sequences = group_rows // SEQ_LEN
    query_pre = jnp.dot(first_rows, query_weight, preferred_element_type=jnp.float32)
    key_pre = jnp.dot(first_rows, key_weight, preferred_element_type=jnp.float32)
    value_pre = jnp.dot(first_rows, value_weight, preferred_element_type=jnp.float32)
    queries = rotate(query_pre.reshape(group_rows, 2 * pair_count, HD), 1.0).astype(jnp.bfloat16)
    queries = queries.reshape(sequences, SEQ_LEN, pair_count, 2, HD)
    keys_rot = rotate(key_pre.reshape(group_rows, pair_count, HD), 1.0).astype(jnp.bfloat16)
    keys_rot = keys_rot.reshape(sequences, SEQ_LEN, pair_count, HD)
    values = value_pre.astype(jnp.bfloat16).reshape(sequences, SEQ_LEN, pair_count, HD)
    mixed_heads, log_total = lax.map(attend_forward, (queries, keys_rot, values))
    heads_out = mixed_heads.reshape(group_rows, 2 * pair_count * HD)
    heads_rows = lax.all_to_all(heads_out, "tensor", split_axis=0, concat_axis=1, tiled=True)
    out_full = lax.all_gather(out_weight, "tensor", axis=0, tiled=True)
    attention_branch = jnp.dot(heads_rows, out_full, preferred_element_type=jnp.float32)
    middle = own_rows + attention_branch
    second_normed = normed(middle, second_gain).astype(jnp.bfloat16)
    second_rows = gather_rows(second_normed)
    gate_full, up_full, down_full = (gate_weight, up_weight, down_weight)
    gate_value = jnp.dot(second_rows, gate_full, preferred_element_type=jnp.float32)
    up_value = jnp.dot(second_rows, up_full, preferred_element_type=jnp.float32)
    sigmoid_gate = jax.nn.sigmoid(gate_value)
    swish_gate = gate_value * sigmoid_gate
    hidden = (swish_gate * up_value).astype(jnp.bfloat16)

    def project_hidden(start, amount):
        return jnp.dot(hidden, down_full, preferred_element_type=jnp.float32)

    ffn_branch = sum_outputs(project_hidden, row_count)
    grad_branch = gather_grads(cotangent)
    result = (middle + ffn_branch).astype(jnp.bfloat16)
    grad_hidden = times_transposed(grad_branch, down_full)
    down_part = transposed_times(hidden, grad_branch)
    slope = sigmoid_gate + gate_value * sigmoid_gate * (1.0 - sigmoid_gate)
    grad_gate = (grad_hidden * up_value * slope).astype(jnp.bfloat16)
    grad_up = (grad_hidden * swish_gate).astype(jnp.bfloat16)
    gate_part = transposed_times(second_rows, grad_gate)
    up_part = transposed_times(second_rows, grad_up)

    def second_back(start, amount):
        return times_transposed(grad_gate, gate_full) + times_transposed(grad_up, up_full)

    grad_second = sum_inputs(second_back, row_count)
    second_unused, second_pull = jax.vjp(normed, middle, second_gain)
    grad_middle_norm, second_gain_part = second_pull(grad_second)
    grad_middle = cotangent.astype(jnp.float32) + grad_middle_norm
    grad_attention = grad_middle.astype(jnp.bfloat16)
    grad_heads_rows = times_transposed(grad_attention, out_full).astype(jnp.bfloat16)
    grad_heads = lax.all_to_all(grad_heads_rows, "tensor", split_axis=1, concat_axis=0, tiled=True)
    out_part = lax.psum_scatter(
        transposed_times(heads_rows, grad_attention).astype(jnp.bfloat16),
        "tensor",
        scatter_dimension=0,
        tiled=True,
    )
    grad_mixed = grad_heads.reshape(sequences, SEQ_LEN, pair_count, 2, HD)
    grad_queries, grad_keys, grad_values = lax.map(
        attend_backward, (queries, keys_rot, values, grad_mixed, log_total)
    )
    grad_query = (
        rotate(grad_queries.reshape(group_rows, 2 * pair_count, HD), -1.0)
        .reshape(group_rows, -1)
        .astype(jnp.bfloat16)
    )
    grad_key = (
        rotate(grad_keys.reshape(group_rows, pair_count, HD), -1.0)
        .reshape(group_rows, -1)
        .astype(jnp.bfloat16)
    )
    grad_value = grad_values.reshape(group_rows, -1).astype(jnp.bfloat16)
    query_part = transposed_times(first_rows, grad_query)
    key_part = transposed_times(first_rows, grad_key)
    value_part = transposed_times(first_rows, grad_value)

    def first_back(start, amount):
        return (
            times_transposed(grad_query, query_weight)
            + times_transposed(grad_key, key_weight)
            + times_transposed(grad_value, value_weight)
        )

    grad_first = sum_inputs(first_back, row_count)
    first_unused, first_pull = jax.vjp(normed, own_rows, first_gain)
    grad_own_norm, first_gain_part = first_pull(grad_first)
    tokens_grad = grad_middle + grad_own_norm
    query_grad, key_grad, value_grad, out_grad, gate_grad, up_grad, down_grad = (
        lax.psum_scatter(
            query_part.astype(jnp.bfloat16), "dp", scatter_dimension=0, tiled=True
        ).astype(jnp.float32),
        lax.psum_scatter(
            key_part.astype(jnp.bfloat16), "dp", scatter_dimension=0, tiled=True
        ).astype(jnp.float32),
        lax.psum_scatter(
            value_part.astype(jnp.bfloat16), "dp", scatter_dimension=0, tiled=True
        ).astype(jnp.float32),
        lax.psum_scatter(out_part, "dp", scatter_dimension=1, tiled=True).astype(jnp.float32),
        lax.psum_scatter(
            gate_part.astype(jnp.bfloat16), "dp", scatter_dimension=0, tiled=True
        ).astype(jnp.float32),
        lax.psum_scatter(
            up_part.astype(jnp.bfloat16), "dp", scatter_dimension=0, tiled=True
        ).astype(jnp.float32),
        lax.psum_scatter(
            down_part.astype(jnp.bfloat16), "dp", scatter_dimension=1, tiled=True
        ).astype(jnp.float32),
    )
    first_gain_grad, second_gain_grad = (
        lax.psum_scatter(first_gain_part, ("dp", "tensor"), scatter_dimension=0, tiled=True),
        lax.psum_scatter(second_gain_part, ("dp", "tensor"), scatter_dimension=0, tiled=True),
    )
    return (
        result,
        tokens_grad,
        query_grad,
        key_grad,
        value_grad,
        out_grad,
        gate_grad,
        up_grad,
        down_grad,
        first_gain_grad,
        second_gain_grad,
    )


def solution(mesh):
    in_specs = (
        P(("dp", "tensor"), None),
        P(("dp", "tensor"), None),
        P(),
        P("dp", "tensor"),
        P("dp", "tensor"),
        P("dp", "tensor"),
        P("tensor", "dp"),
        P(),
        P("dp", "tensor"),
        P("dp", "tensor"),
        P("tensor", "dp"),
    )
    out_specs = (
        P(("dp", "tensor"), None),
        P(("dp", "tensor"), None),
        P("dp", "tensor"),
        P("dp", "tensor"),
        P("dp", "tensor"),
        P("tensor", "dp"),
        P("dp", "tensor"),
        P("dp", "tensor"),
        P("tensor", "dp"),
        P(("dp", "tensor")),
        P(("dp", "tensor")),
    )
    return jax.shard_map(local, mesh=mesh, in_specs=in_specs, out_specs=out_specs, check_vma=False)
```

profile of v0, /device:TPU:0, one launch (start us, length us, event | category | flops | bytes accessed | tf_op | source)
XLA Modules:
  0.0 1341.1 jit_solution(12575531316404064480)
XLA Ops:
  14.8 20.3 %all-gather.14.cloned.1.call-done = bf16[384,1536]{0,1:T(8,128)(2,1)} async-done(((bf16[384,192]{0,1:T(8,128)(2,1)}), bf16[384,1536]{0,1:T(8,128)(2,1)}) %all-gather.14.cloned.1.call-update) | async-done | bytes 1179664 | tf_op jit(solution)/shard_map/all_gather | solution.py:137
  35.7 15.4 %all_gather.35 = bf16[1536,192]{1,0:T(8,128)(2,1)S(1)} all-gather(bf16[192,192]{1,0:T(8,128)(2,1)S(1)} %copy-done.21), channel_id=1, replica_groups=mesh['dp'=8,'tensor'=4] {'dp'}, dimensions={0}, use_global_device_ids=true | all-gather | bytes 663552 | tf_op jit(solution)/shard_map/all_gather | solution.py:135
  51.1 15.5 %all_gather.34 = bf16[1536,192]{1,0:T(8,128)(2,1)S(1)} all-gather(bf16[192,192]{1,0:T(8,128)(2,1)S(1)} %copy-done.22), channel_id=1, replica_groups=mesh['dp'=8,'tensor'=4] {'dp'}, dimensions={0}, use_global_device_ids=true | all-gather | bytes 663552 | tf_op jit(solution)/shard_map/all_gather | solution.py:136
  68.9 38.5 %all-gather.10.cloned.1.call-done = bf16[2048,1536]{1,0:T(8,128)(2,1)} async-done(((bf16[512,1536]{1,0:T(8,128)(2,1)}), bf16[2048,1536]{1,0:T(8,128)(2,1)}) %all-gather.10.cloned.1.call-update) | async-done | bytes 6291472 | tf_op jit(solution)/shard_map/all_gather | solution.py:95
  145.4 28.8 %while.26 = (s32[]{:T(128)}, bf16[2,1024,2,2,96]{1,4,3,2,0:T(8,128)(2,1)S(1)}, f32[2,2,2,1024]{3,2,1,0:T(2,128)}, bf16[2,1024,2,96]{1,3,2,0:T(8,128)(2,1)S(1)}, ...) while((s32[]{:T(128)}, bf16[2,1024,2,2,96]{1,4,3,2,0:T(8,128)(2,1)S(1)}, ...), condition=%wide.region_4.5_spmd, body=%wide.region_1.4_spmd.sunk | while | flops 1662382080 | bytes 57018456 | solution.py:157
  190.2 16.7 %all-to-all-done = bf16[4,512,384]{1,2,0:T(8,128)(2,1)S(1)} async-done(((bf16[4,512,384]{1,2,0:T(8,128)(2,1)}), bf16[4,512,384]{1,2,0:T(8,128)(2,1)S(1)}, u32[]{:S(2)}, u32[]{:S(2)}) %all-to-all-start) | async-done | bytes 1572896 | tf_op jit(solution)/shard_map/all_to_all | solution.py:159
  218.3 20.4 %all-gather.22.cloned.1.call-done = bf16[1536,1024]{1,0:T(8,128)(2,1)} async-done(((bf16[192,1024]{1,0:T(8,128)(2,1)}), bf16[1536,1024]{1,0:T(8,128)(2,1)}) %all-gather.22.cloned.1.call-update) | async-done | bytes 3145744 | tf_op jit(solution)/shard_map/all_gather | solution.py:139
  238.8 71.3 %all-gather.18.cloned.1.call-done = bf16[2048,1536]{1,0:T(8,128)(2,1)} async-done(((bf16[512,1536]{1,0:T(8,128)(2,1)}), bf16[2048,1536]{1,0:T(8,128)(2,1)}) %all-gather.18.cloned.1.call-update) | async-done | bytes 6291472 | tf_op jit(solution)/shard_map/all_gather | solution.py:95
  310.1 11.6 fusion.77
  321.7 28.4 %all-gather.20.cloned.1.call-done = bf16[1536,1024]{1,0:T(8,128)(2,1)} async-done(((bf16[192,1024]{1,0:T(8,128)(2,1)}), bf16[1536,1024]{1,0:T(8,128)(2,1)}) %all-gather.20.cloned.1.call-update) | async-done | bytes 3145744 | tf_op jit(solution)/shard_map/all_gather | solution.py:138
  350.1 11.7 fusion.76
  361.7 27.1 %all-gather.24.cloned.1.call-done = bf16[1024,1536]{0,1:T(8,128)(2,1)} async-done(((bf16[1024,192]{0,1:T(8,128)(2,1)}), bf16[1024,1536]{0,1:T(8,128)(2,1)}) %all-gather.24.cloned.1.call-update) | async-done | bytes 3145744 | tf_op jit(solution)/shard_map/all_gather | solution.py:140
  388.9 70.9 %all-gather.26.cloned.1.call-done = bf16[2048,1536]{1,0:T(8,128)(2,1)} async-done(((bf16[512,1536]{1,0:T(8,128)(2,1)}), bf16[2048,1536]{1,0:T(8,128)(2,1)}) %all-gather.26.cloned.1.call-update) | async-done | bytes 6291472 | tf_op jit(solution)/shard_map/all_gather | solution.py:99
  459.8 18.0 %multiply_convert_fusion = (bf16[2048,1024]{1,0:T(8,128)(2,1)}, bf16[2048,1024]{1,0:T(8,128)(2,1)S(1)}, bf16[2048,1024]{1,0:T(8,128)(2,1)}) fusion(f32[2048,1024]{1,0:T(8,128)} %fusion.76, f32[2048,1024]{1,0:T(8,128)} %fusion.77, bf16[2048,1536]{1,0:T(8,128)(2,1)} %all-gather.26.cloned.1.call-done, bf16[1024,1536]{0,1:T(8,128)(2,1)} %all-gather.24.cloned.1.call-done), kind=kOutput, calls=%fused_computation.66 | convolution fusion | flops 6471811072 | bytes 38797312 | tf_op jit(solution)/shard_map/dot_general | solution.py:36
  487.6 12.9 convolution_add_fusion
  500.5 12.4 fusion.78
  513.0 108.4 %reduce-scatter.16.cloned.1.call-done = f32[512,1536]{1,0:T(8,128)} async-done(((f32[2048,1536]{1,0:T(8,128)}), f32[512,1536]{1,0:T(8,128)}) %reduce-scatter.16.cloned.1.call-update) | async-done | bytes 3145744 | tf_op jit(solution)/shard_map/reduce_scatter | solution.py:112
  624.6 120.6 %reduce-scatter.14.cloned.1.call-done = f32[512,1536]{1,0:T(8,128)} async-done(((f32[2048,1536]{1,0:T(8,128)}), f32[512,1536]{1,0:T(8,128)}) %reduce-scatter.14.cloned.1.call-update) | async-done | bytes 3145744 | tf_op jit(solution)/shard_map/reduce_scatter | solution.py:103
  756.7 11.8 convolution_convert_fusion.1
  805.7 20.7 %all-to-all-done.1 = bf16[512,4,384]{0,2,1:T(8,128)(2,1)S(1)} async-done(((bf16[512,4,384]{0,2,1:T(8,128)(2,1)}), bf16[512,4,384]{0,2,1:T(8,128)(2,1)S(1)}, u32[]{:S(2)}, u32[]{:S(2)}) %all-to-all-start.1) | async-done | bytes 1572896 | tf_op jit(solution)/shard_map/all_to_all | solution.py:195
  830.3 186.8 %while.27 = (s32[]{:T(128)}, f32[2,1024,2,2,96]{1,0,4,3,2:T(2,128)}, f32[2,1024,2,96]{1,0,3,2:T(2,128)}, bf16[2,1024,2,96]{1,3,2,0:T(8,128)(2,1)}, bf16[2,1024,2...) while((s32[]{:T(128)}, ...), condition=%wide.region_11.12_spmd, body=%wide.region_9.11_spmd.sunk | while | flops 4091080704 | bytes 203738416 | solution.py:203
  850.4 14.2 %fusion.154 = (f32[2,2,1024]{2,1,0:T(2,128)}, f32[2,1024,1024,2]{2,1,3,0:T(8,128)}) fusion(f32[2,1024,1024,2]{2,1,3,0:T(8,128)} %fusion.153, f32[2,2,1024]{2,1,0:T(2,128)} %copy-done.11, pred[1024,1024]{0,1:T(8,128)(4,1)S(1)} %iota_compare_fusion.5, bf16[2,1024,2,2,96]{1,4,3,2,0:T(8,128)(2,1)} %get-tuple-element.385, s32[]{:T(128)S(6)} %copy.112, ...), kind=kOutput, calls=%fused_computation.24.clone.1 | convolution fusion | flops 826273792 | bytes 35816448 | tf_op jit(solution)/shard_map/while/body/eval_jaxpr/qhgd,khd->hgqk/dot_general | solution.py:71
  881.9 14.4 %dynamic_update_slice.31 = f32[2,1024,2,96]{1,0,3,2:T(2,128)} dynamic-update-slice(f32[2,1024,2,96]{1,0,3,2:T(2,128)} %get-tuple-element.368, f32[1,1024,2,96]{1,0,3,2:T(1,128)S(1)} %copy.93, s32[]{:T(128)S(6)} %copy.112, s32[]{:T(128)} %constant.88.clone.1..sunk, s32[]{:T(128)} %constant.88.clone.1..sunk, s32[]{:T(128)} %constant.88.clone.1..sunk) | dynamic-update-slice | bytes 1572868 | tf_op jit(solution)/shard_map/while/body/jit(dynamic_update_index_in_dim)/dynamic_update_slice | solution.py:203
  896.3 27.6 %dynamic_update_slice.30 = f32[2,1024,2,2,96]{1,0,4,3,2:T(2,128)} dynamic-update-slice(f32[2,1024,2,2,96]{1,0,4,3,2:T(2,128)} %get-tuple-element.367, f32[1,1024,2,2,96]{1,0,4,3,2:T(1,128)S(1)} %copy.92, s32[]{:T(128)S(6)} %copy.112, s32[]{:T(128)} %constant.88.clone.1..sunk, s32[]{:T(128)} %constant.88.clone.1..sunk, s32[]{:T(128)} %constant.88.clone.1..sunk, s32[]{:T(128)} %constant.88.clone.1..sunk) | dynamic-update-slice | bytes 3145732 | tf_op jit(solution)/shard_map/while/body/jit(dynamic_update_index_in_dim)/dynamic_update_slice | solution.py:203
  943.8 14.0 %fusion.154 = (f32[2,2,1024]{2,1,0:T(2,128)}, f32[2,1024,1024,2]{2,1,3,0:T(8,128)}) fusion(f32[2,1024,1024,2]{2,1,3,0:T(8,128)} %fusion.153, f32[2,2,1024]{2,1,0:T(2,128)} %copy-done.11, pred[1024,1024]{0,1:T(8,128)(4,1)S(1)} %iota_compare_fusion.5, bf16[2,1024,2,2,96]{1,4,3,2,0:T(8,128)(2,1)} %get-tuple-element.385, s32[]{:T(128)S(6)} %copy.112, ...), kind=kOutput, calls=%fused_computation.24.clone.1 | convolution fusion | flops 826273792 | bytes 35816448 | tf_op jit(solution)/shard_map/while/body/eval_jaxpr/qhgd,khd->hgqk/dot_general | solution.py:71
  975.0 14.4 %dynamic_update_slice.31 = f32[2,1024,2,96]{1,0,3,2:T(2,128)} dynamic-update-slice(f32[2,1024,2,96]{1,0,3,2:T(2,128)} %get-tuple-element.368, f32[1,1024,2,96]{1,0,3,2:T(1,128)S(1)} %copy.93, s32[]{:T(128)S(6)} %copy.112, s32[]{:T(128)} %constant.88.clone.1..sunk, s32[]{:T(128)} %constant.88.clone.1..sunk, s32[]{:T(128)} %constant.88.clone.1..sunk) | dynamic-update-slice | bytes 1572868 | tf_op jit(solution)/shard_map/while/body/jit(dynamic_update_index_in_dim)/dynamic_update_slice | solution.py:203
  989.3 27.6 %dynamic_update_slice.30 = f32[2,1024,2,2,96]{1,0,4,3,2:T(2,128)} dynamic-update-slice(f32[2,1024,2,2,96]{1,0,4,3,2:T(2,128)} %get-tuple-element.367, f32[1,1024,2,2,96]{1,0,4,3,2:T(1,128)S(1)} %copy.92, s32[]{:T(128)S(6)} %copy.112, s32[]{:T(128)} %constant.88.clone.1..sunk, s32[]{:T(128)} %constant.88.clone.1..sunk, s32[]{:T(128)} %constant.88.clone.1..sunk, s32[]{:T(128)} %constant.88.clone.1..sunk) | dynamic-update-slice | bytes 3145732 | tf_op jit(solution)/shard_map/while/body/jit(dynamic_update_index_in_dim)/dynamic_update_slice | solution.py:203
  1080.8 15.8 %reduce-scatter.22.cloned.1.call-done = bf16[192,192]{1,0:T(8,128)(2,1)} async-done(((bf16[1536,192]{1,0:T(8,128)(2,1)}), bf16[192,192]{1,0:T(8,128)(2,1)}) %reduce-scatter.22.cloned.1.call-update) | async-done | bytes 73744 | tf_op jit(solution)/shard_map/reduce_scatter | solution.py:236
  1098.2 31.3 %reduce-scatter.20.cloned.1.call-done = bf16[192,384]{1,0:T(8,128)(2,1)} async-done(((bf16[1536,384]{1,0:T(8,128)(2,1)}), bf16[192,384]{1,0:T(8,128)(2,1)}) %reduce-scatter.20.cloned.1.call-update) | async-done | bytes 147472 | tf_op jit(solution)/shard_map/reduce_scatter | solution.py:233
  1131.1 31.8 %reduce-scatter.34.cloned.1.call-done = bf16[192,384]{1,0:T(8,128)(2,1)} async-done(((bf16[1536,384]{1,0:T(8,128)(2,1)}), bf16[192,384]{1,0:T(8,128)(2,1)}) %reduce-scatter.34.cloned.1.call-update) | async-done | bytes 147472
  1164.8 120.1 %reduce-scatter.18.cloned.1.call-done = f32[512,1536]{1,0:T(8,128)} async-done(((f32[2048,1536]{1,0:T(8,128)}), f32[512,1536]{1,0:T(8,128)}) %reduce-scatter.18.cloned.1.call-update) | async-done | bytes 3145744 | tf_op jit(solution)/shard_map/reduce_scatter | solution.py:112
  1287.8 39.5 %all-reduce.2 = (f32[1536]{0:T(1024)S(1)}, f32[1536]{0:T(1024)S(1)}) all-reduce(f32[1536]{0:T(1024)S(1)} %get-tuple-element.178, f32[1536]{0:T(1024)S(1)} %copy-done.25), channel_id=13, replica_groups=mesh['dp'=8,'tensor'=4] {'dp','tensor'}, use_global_device_ids=true, to_apply=%region_23.24.clone | all-reduce | flops 3072 | bytes 24576
  (239 shorter events, 321.9 us)
Async XLA Ops:
  7.2 27.9 %all-gather.14.cloned.1.call-start = ((), (), s32[]{:S(2)}) async-start(), calls=%async_computation.15 | async-start | bytes 1327104 | tf_op jit(solution)/shard_map/all_gather | solution.py:137
  7.9 99.5 %all-gather.10.cloned.1.call-start = ((), (), s32[]{:S(2)}) async-start(), calls=%async_computation.13 | async-start | bytes 7864320 | tf_op jit(solution)/shard_map/all_gather | solution.py:95
  10.9 24.8 %copy-start.21 = (bf16[192,192]{1,0:T(8,128)(2,1)S(1)}, bf16[192,192]{1,0:T(8,128)(2,1)}, u32[]{:S(2)}) copy-start(bf16[192,192]{1,0:T(8,128)(2,1)} %param.19) | copy-start | bytes 221188
  10.9 40.2 %copy-start.22 = (bf16[192,192]{1,0:T(8,128)(2,1)S(1)}, bf16[192,192]{1,0:T(8,128)(2,1)}, u32[]{:S(2)}) copy-start(bf16[192,192]{1,0:T(8,128)(2,1)} %param.20) | copy-start | bytes 221188
  14.0 117.8 %all-gather.12.cloned.1.call-start = ((), (), s32[]{:S(2)}) async-start(), calls=%async_computation.14 | async-start | bytes 1327104 | tf_op jit(solution)/shard_map/all_gather | solution.py:134
  14.7 175.4 %all-gather.16.cloned.1.call-start = ((), (), s32[]{:S(2)}) async-start(), calls=%async_computation.16 | async-start | bytes 5898240 | tf_op jit(solution)/shard_map/all_gather | solution.py:160
  35.1 203.7 %all-gather.22.cloned.1.call-start = ((), (), s32[]{:S(2)}) async-start(), calls=%async_computation.19 | async-start | bytes 3538944 | tf_op jit(solution)/shard_map/all_gather | solution.py:139
  51.1 64.9 %copy-start.7 = (bf16[1536,192]{1,0:T(8,128)(2,1)}, bf16[1536,192]{1,0:T(8,128)(2,1)S(1)}, u32[]{:S(2)}) copy-start(bf16[1536,192]{1,0:T(8,128)(2,1)S(1)} %all_gather.35) | copy-start | bytes 1769476
  66.7 46.6 %copy-start.12 = (bf16[1536,192]{1,0:T(8,128)(2,1)}, bf16[1536,192]{1,0:T(8,128)(2,1)S(1)}, u32[]{:S(2)}) copy-start(bf16[1536,192]{1,0:T(8,128)(2,1)S(1)} %all_gather.34) | copy-start | bytes 1769476
  68.9 68.0 %copy-start.4 = (f32[2048,48]{0,1:T(8,128)}, f32[2048,48]{0,1:T(8,128)S(1)}, u32[]{:S(2)}) copy-start(f32[2048,48]{0,1:T(8,128)S(1)} %get-tuple-element.231) | copy-start | bytes 1179652
  183.4 23.5 %all-to-all-start = ((bf16[4,512,384]{1,2,0:T(8,128)(2,1)}), bf16[4,512,384]{1,2,0:T(8,128)(2,1)S(1)}, u32[]{:S(2)}, u32[]{:S(2)}) async-start(bf16[4,512,384]{1,2,0:T(8,128)(2,1)} %copy.55), calls=%async_computation | async-start | bytes 3145728 | tf_op jit(solution)/shard_map/all_to_all | solution.py:159
  187.1 123.0 %all-gather.18.cloned.1.call-start = ((), (), s32[]{:S(2)}) async-start(), calls=%async_computation.17 | async-start | bytes 7864320 | tf_op jit(solution)/shard_map/all_gather | solution.py:95
  215.9 134.2 %all-gather.20.cloned.1.call-start = ((), (), s32[]{:S(2)}) async-start(), calls=%async_computation.18 | async-start | bytes 3538944 | tf_op jit(solution)/shard_map/all_gather | solution.py:138
  216.6 172.3 %all-gather.24.cloned.1.call-start = ((), (), s32[]{:S(2)}) async-start(), calls=%async_computation.20 | async-start | bytes 3538944 | tf_op jit(solution)/shard_map/all_gather | solution.py:140
  217.4 242.4 %all-gather.26.cloned.1.call-start = ((), (), s32[]{:S(2)}) async-start(), calls=%async_computation.22 | async-start | bytes 7864320 | tf_op jit(solution)/shard_map/all_gather | solution.py:99
  218.1 403.2 %reduce-scatter.16.cloned.1.call-start = ((), (), s32[]{:S(2)}) async-start(), calls=%async_computation.23 | async-start | bytes 15728640 | tf_op jit(solution)/shard_map/reduce_scatter | solution.py:112
  500.4 244.7 %reduce-scatter.14.cloned.1.call-start = ((), (), s32[]{:S(2)}) async-start(), calls=%async_computation.21 | async-start | bytes 15728640 | tf_op jit(solution)/shard_map/reduce_scatter | solution.py:103
  512.9 537.3 %reduce-scatter.26.cloned.1.call-start = ((), (), s32[]{:S(2)}) async-start(), calls=%async_computation.28 | async-start | bytes 5898240 | tf_op jit(solution)/shard_map/reduce_scatter | solution.py:196
  756.7 316.5 %reduce-scatter.32.cloned.1.call-start = ((), (), s32[]{:S(2)}) async-start(), calls=%async_computation.31 | async-start | bytes 3538944 | tf_op jit(solution)/shard_map/reduce_scatter | solution.py:249
  768.5 306.7 %reduce-scatter.30.cloned.1.call-start = ((), (), s32[]{:S(2)}) async-start(), calls=%async_computation.30 | async-start | bytes 3538944 | tf_op jit(solution)/shard_map/reduce_scatter | solution.py:246
  790.8 35.7 %all-to-all-start.1 = ((bf16[512,4,384]{0,2,1:T(8,128)(2,1)}), bf16[512,4,384]{0,2,1:T(8,128)(2,1)S(1)}, u32[]{:S(2)}, u32[]{:S(2)}) async-start(bf16[512,4,384]{0,2,1:T(8,128)(2,1)} %bitcast.37), calls=%async_computation.3 | async-start | bytes 3145728 | tf_op jit(solution)/shard_map/all_to_all | solution.py:195
  794.3 282.9 %reduce-scatter.28.cloned.1.call-start = ((), (), s32[]{:S(2)}) async-start(), calls=%async_computation.29 | async-start | bytes 3538944 | tf_op jit(solution)/shard_map/reduce_scatter | solution.py:243
  805.7 273.5 %reduce-scatter.24.cloned.1.call-start = ((), (), s32[]{:S(2)}) async-start(), calls=%async_computation.27 | async-start | bytes 884736 | tf_op jit(solution)/shard_map/reduce_scatter | solution.py:239
  1032.8 63.8 %reduce-scatter.22.cloned.1.call-start = ((), (), s32[]{:S(2)}) async-start(), calls=%async_computation.26 | async-start | bytes 884736 | tf_op jit(solution)/shard_map/reduce_scatter | solution.py:236
  1041.1 88.4 %reduce-scatter.20.cloned.1.call-start = ((), (), s32[]{:S(2)}) async-start(), calls=%async_computation.25 | async-start | bytes 1327104 | tf_op jit(solution)/shard_map/reduce_scatter | solution.py:233
  1050.2 112.7 %reduce-scatter.34.cloned.1.call-start = ((), (), s32[]{:S(2)}) async-start(), calls=%async_computation.32 | async-start | bytes 1327104
  1052.8 232.2 %reduce-scatter.18.cloned.1.call-start = ((), (), s32[]{:S(2)}) async-start(), calls=%async_computation.24 | async-start | bytes 15728640 | tf_op jit(solution)/shard_map/reduce_scatter | solution.py:112
  1073.1 211.8 %copy-start = (bf16[512,1536]{1,0:T(8,128)(2,1)S(1)}, bf16[512,1536]{1,0:T(8,128)(2,1)}, u32[]{:S(2)}) copy-start(bf16[512,1536]{1,0:T(8,128)(2,1)} %param.15) | copy-start | bytes 4718596
  1073.1 211.8 %copy-start.24 = (f32[1536]{0:T(1024)S(1)}, f32[1536]{0:T(1024)}, u32[]{:S(2)}) copy-start(f32[1536]{0:T(1024)} %param.17) | copy-start | bytes 18436
  1073.1 211.8 %copy-start.27 = (f32[512]{0:T(512)S(1)}, f32[512]{0:T(512)}, u32[]{:S(2)}) copy-start(f32[512]{0:T(512)} %copy-done.26) | copy-start | bytes 6148
  1080.8 207.1 %copy-start.29 = (f32[512]{0:T(512)S(1)}, f32[512]{0:T(512)}, u32[]{:S(2)}) copy-start(f32[512]{0:T(512)} %copy-done.28) | copy-start | bytes 6148
  1080.8 207.1 %copy-start.25 = (f32[1536]{0:T(1024)S(1)}, f32[1536]{0:T(1024)}, u32[]{:S(2)}) copy-start(f32[1536]{0:T(1024)} %get-tuple-element.176) | copy-start | bytes 18436
  (34 other events, 294.0 us)
Sparse Core Ops, SparseCore 0:
  9.7 25.3 all-gather.13
  37.5 69.9 all-gather.9
  109.1 22.6 all-gather.11
  133.4 56.6 all-gather.15
  191.7 47.0 all-gather.21
  241.0 69.0 all-gather.17
  311.7 38.2 all-gather.19
  351.7 37.1 all-gather.23
  390.7 69.0 all-gather.25
  500.6 120.7 reduce-scatter.15
  624.4 120.7 reduce-scatter.13
  756.8 71.1 reduce-scatter.25
  830.3 40.3 reduce-scatter.31
  872.8 39.4 reduce-scatter.29
  914.4 39.4 reduce-scatter.27
  1032.9 31.6 reduce-scatter.23
  1066.8 29.7 reduce-scatter.21
  1098.7 30.7 reduce-scatter.19
  1131.8 31.0 reduce-scatter.33
  1165.9 119.0 reduce-scatter.17
where the time goes:
time: 1360 us; the launch traced here: 1340 us
  waiting for transfers between devices  757 us (56%)
  matrix products  280 us (21%)
  local copies, waits for them, and re-layouts  138 us (10%)
  other arithmetic  70.9 us (5%)
  blocking collectives  70.5 us (5%)
  between operations  15.2 us (1%)
    reduce_scatter x2, waiting for transfers between devices, sum_inputs(): lax.psum_scatter(term(jnp.int32(0), row_count * lax.axis_size('tensor')),...  228 us
    reduce_scatter x1, waiting for transfers between devices, sum_outputs(): lax.psum_scatter(term(jnp.int32(0), row_count * lax.axis_size('tensor')),...  121 us
    all_gather x2, waiting for transfers between devices, gather_rows(): return lax.all_gather(shard, 'tensor', axis=0, tiled=True)  110 us
    dynamic_update_slice x8, local copies, waits for them, and re-layouts, local(): lax.map(attend_backward, (queries, keys_rot, values, grad_mixed, log_total))  88.9 us
    all_gather x1, waiting for transfers between devices, gather_grads(): return lax.all_gather(shard, 'tensor', axis=0, tiled=True)  70.9 us
    dot_general x7, matrix products, times_transposed(): lax.dot_general(left, right, (((1,), (1,)), ((), ())), preferred_element_...  66.7 us
    dot_general x7, matrix products, transposed_times(): lax.dot_general(left, right, (((0,), (0,)), ((), ())), preferred_element_...  57.6 us
    unnamed x1, blocking collectives  39.5 us
  transfers between devices with their start and end apart: 22, of which 17 were waited for; matrix products, arithmetic and copies ran while one was open for 31% of the time, Pallas kernels for 0%

commit v1 on v0

--- a/solution.py
+++ b/solution.py
@@ -1,6 +1,11 @@
+import functools
+
 import jax
 import jax.numpy as jnp
+import numpy as np
 from jax import lax
+from jax.experimental import pallas as pl
+from jax.experimental.pallas import tpu as pltpu
 from jax.sharding import PartitionSpec as P
 
 HD = 96
@@ -10,6 +15,9 @@
 EPSILON = 1e-05
 THETA = 100000.0
 MASKED = -1e30
+LOG2E = 1.4426950408889634
+LANES = 128
+VMEM_BYTES = 56 * 2**20
 
 
 def normed(inputs, gain):
@@ -269,31 +277,686 @@
     )
 
 
+def swap(value, axis):
+    return lax.ppermute(value, axis, [(0, 1), (1, 0)])
+
+
+def nn(left, right):
+    return jnp.dot(left, right, preferred_element_type=jnp.float32)
+
+
+def vmem_params(**more):
+    return pltpu.CompilerParams(vmem_limit_bytes=VMEM_BYTES, **more)
+
+
+def smem_spec():
+    return pl.BlockSpec(memory_space=pltpu.SMEM)
+
+
+def vmem_spec():
+    return pl.BlockSpec(memory_space=pltpu.VMEM)
+
+
+def any_spec():
+    return pl.BlockSpec(memory_space=pl.ANY)
+
+
+def row_offset(place_ref, shift, rel, deep, part):
+    ring = jnp.int32(deep)
+    slot = lax.rem(place_ref[0] + shift, ring)
+    core = lax.rem(place_ref[1] + rel, jnp.int32(2))
+    return pl.multiple_of((slot * 2 + core) * part, 64)
+
+
+def spread_heads(heads_split, heads_plain):
+    columns = (heads_split + heads_plain) * HD
+    spread = np.zeros((columns, (heads_split + heads_plain) * LANES), np.float32)
+    for head in range(heads_split + heads_plain):
+        for entry in range(HD):
+            lane = entry
+            if head < heads_split and entry >= HD // 2:
+                lane = entry - HD // 2 + LANES // 2
+            spread[head * HD + entry, head * LANES + lane] = 1.0
+    return jnp.asarray(spread, jnp.bfloat16)
+
+
+def prepare_kernel(deep, place_ref, *refs):
+    own, other, spread_ref = refs[:deep], refs[deep : 2 * deep], refs[2 * deep]
+    qkv_ref, out_ref = refs[2 * deep + 1 :]
+    part = own[0].shape[1]
+    half_qkv, half_out = qkv_ref.shape[1] // 2, out_ref.shape[1] // 2
+    for side, chunks in enumerate((own, other)):
+        for shift in range(deep):
+            for rel in range(2):
+                rows = pl.ds(row_offset(place_ref, shift, rel, deep, part), part)
+                wide = nn(chunks[shift][rel], spread_ref[...]).astype(jnp.bfloat16)
+                qkv_ref[rows, side * half_qkv : (side + 1) * half_qkv] = wide[:, :half_qkv]
+                out_ref[rows, side * half_out : (side + 1) * half_out] = wide[:, half_qkv:]
+
+
+def prepare(place, own, other, spread):
+    deep, part = len(own), own[0].shape[1]
+    rows = deep * 2 * part
+    wide = spread.shape[1]
+    half_qkv = wide * 2 // 3
+    return pl.pallas_call(
+        functools.partial(prepare_kernel, deep),
+        out_shape=(
+            jax.ShapeDtypeStruct((rows, 2 * half_qkv), jnp.bfloat16),
+            jax.ShapeDtypeStruct((rows, 2 * (wide - half_qkv)), jnp.bfloat16),
+        ),
+        in_specs=[smem_spec()] + [vmem_spec()] * (2 * deep + 1),
+        out_specs=(vmem_spec(), vmem_spec()),
+        compiler_params=vmem_params(),
+        cost_estimate=pl.CostEstimate(
+            flops=4 * rows * spread.shape[0] * wide, bytes_accessed=12 * rows * wide, transcendentals=0
+        ),
+        name="prepare",
+    )(place, *own, *other, spread)
+
+
+def turn(vectors, cosine, sine):
+    return vectors * cosine + pltpu.roll(vectors, LANES // 2, 1) * sine
+
+
+def project_kernel(rows_ref, weight_ref, cosine_ref, sine_ref, out_ref):
+    product = nn(rows_ref[...], weight_ref[...])
+    cosine, sine = cosine_ref[...], sine_ref[...]
+    for head in range(3):
+        lanes = slice(head * LANES, (head + 1) * LANES)
+        out_ref[:, lanes] = turn(product[:, lanes], cosine, sine).astype(jnp.bfloat16)
+    out_ref[:, 3 * LANES :] = product[:, 3 * LANES :].astype(jnp.bfloat16)
+
+
+def project(rows, weight, cosine, sine):
+    count, width = rows.shape
+    tile = 4 * LANES
+    return pl.pallas_call(
+        project_kernel,
+        grid=(weight.shape[1] // tile,),
+        out_shape=jax.ShapeDtypeStruct((count, weight.shape[1]), jnp.bfloat16),
+        in_specs=[
+            pl.BlockSpec((count, width), lambda i: (0, 0)),
+            pl.BlockSpec((width, tile), lambda i: (0, i)),
+            pl.BlockSpec((count, LANES), lambda i: (0, 0)),
+            pl.BlockSpec((count, LANES), lambda i: (0, 0)),
+        ],
+        out_specs=pl.BlockSpec((count, tile), lambda i: (0, i)),
+        compiler_params=vmem_params(),
+        cost_estimate=pl.CostEstimate(
+            flops=2 * count * width * weight.shape[1],
+            bytes_accessed=2 * width * (count + weight.shape[1]) + 2 * count * weight.shape[1],
+            transcendentals=0,
+        ),
+        name="project",
+    )(rows, weight, cosine, sine)
+
+
+TILE = 256
+
+
+def place_rows(place_ref, qkv_refs, keys, values):
+    for rel, ref in enumerate(qkv_refs):
+        count = ref.shape[0]
+        position = lax.rem(place_ref[2] + rel, jnp.int32(2))
+        rows = pl.ds(pl.multiple_of(position * count, count), count)
+        keys[rows, :] = ref[:, 2 * LANES : 3 * LANES]
+        values[rows, :] = ref[:, 3 * LANES :]
+
+
+def each_tile(place_ref, qkv_refs, visit):
+    for rel, ref in enumerate(qkv_refs):
+        count = ref.shape[0]
+        position = lax.rem(place_ref[2] + rel, jnp.int32(2))
+        for static_position in range(2):
+
+            @pl.when(position == static_position)
+            def _(rel=rel, count=count, static_position=static_position):
+                for step in range(count // TILE):
+                    visit(rel, step * TILE, static_position * count + step * TILE)
+
+
+def stacked(ref, first, start):
+    rows = slice(start, start + TILE)
+    return jnp.concatenate(
+        [ref[rows, first : first + LANES], ref[rows, first + LANES : first + 2 * LANES]], axis=0
+    )
+
+
+def diagonal_mask():
+    row = lax.broadcasted_iota(jnp.int32, (2 * TILE, TILE), 0)
+    row = jnp.where(row >= TILE, row - TILE, row)
+    return row >= lax.broadcasted_iota(jnp.int32, (2 * TILE, TILE), 1)
+
+
+def attend_kernel(place_ref, a_ref, b_ref, oa_ref, ob_ref, la_ref, lb_ref, keys, values):
+    qkv_refs, out_refs, log_refs = (a_ref, b_ref), (oa_ref, ob_ref), (la_ref, lb_ref)
+    place_rows(place_ref, qkv_refs, keys, values)
+    mask = diagonal_mask()
+    scale = HD ** (-0.5) * LOG2E
+
+    def visit(rel, start, before):
+        queries = stacked(qkv_refs[rel], 0, start)
+        edge = slice(before, before + TILE)
+        near = times_transposed(queries, keys[edge, :])
+        near = jnp.where(mask, near, MASKED)
+        top = jnp.max(near, axis=-1, keepdims=True)
+        if before:
+            far = times_transposed(queries, keys[:before, :])
+            top = jnp.maximum(top, jnp.max(far, axis=-1, keepdims=True))
+        top = top * scale
+        near = jnp.exp2(near * scale - top)
+        total = jnp.sum(near, axis=-1, keepdims=True)
+        mixed = nn(near.astype(jnp.bfloat16), values[edge, :])
+        if before:
+            far = jnp.exp2(far * scale - top)
+            total = total + jnp.sum(far, axis=-1, keepdims=True)
+            mixed = mixed + nn(far.astype(jnp.bfloat16), values[:before, :])
+        mixed = (mixed / total).astype(jnp.bfloat16)
+        logs = jnp.broadcast_to(top + jnp.log2(total), (2 * TILE, LANES))
+        rows = slice(start, start + TILE)
+        for head in range(2):
+            lanes = slice(head * LANES, (head + 1) * LANES)
+            part = slice(head * TILE, (head + 1) * TILE)
+            out_refs[rel][rows, lanes] = mixed[part]
+            log_refs[rel][rows, lanes] = logs[part]
+
+    each_tile(place_ref, qkv_refs, visit)
+
+
+def attend(place, first, second):
+    count = first.shape[0]
+    pairs = first.shape[1] // (4 * LANES)
+    wide = pl.BlockSpec((count, 4 * LANES), lambda i: (0, i))
+    narrow = pl.BlockSpec((count, 2 * LANES), lambda i: (0, i))
+    heads = jax.ShapeDtypeStruct((count, pairs * 2 * LANES), jnp.bfloat16)
+    logs = jax.ShapeDtypeStruct((count, pairs * 2 * LANES), jnp.float32)
+    return pl.pallas_call(
+        attend_kernel,
+        grid=(pairs,),
+        out_shape=(heads, heads, logs, logs),
+        in_specs=[smem_spec(), wide, wide],
+        out_specs=(narrow,) * 4,
+        scratch_shapes=[pltpu.VMEM((2 * count, LANES), jnp.bfloat16)] * 2,
+        compiler_params=vmem_params(),
+        cost_estimate=pl.CostEstimate(
+            flops=pairs * 2 * 4 * count * count * 4 * LANES,
+            bytes_accessed=12 * first.size,
+            transcendentals=pairs * 4 * count * count,
+        ),
+        name="attend",
+    )(place, first, second)
+
+
+def attend_back_kernel(
+    place_ref, a_ref, b_ref, ga_ref, gb_ref, oa_ref, ob_ref, la_ref, lb_ref, cosine_ref, sine_ref,
+    da_ref, db_ref, keys, values, grad_keys, grad_values,
+):
+    qkv_refs, grad_refs, out_refs = (a_ref, b_ref), (ga_ref, gb_ref), (oa_ref, ob_ref)
+    log_refs, result_refs = (la_ref, lb_ref), (da_ref, db_ref)
+    place_rows(place_ref, qkv_refs, keys, values)
+    mask = diagonal_mask()
+    factor = HD ** (-0.5)
+    scale = factor * LOG2E
+    grad_keys[...] = jnp.zeros_like(grad_keys)
+    grad_values[...] = jnp.zeros_like(grad_values)
+
+    def visit(rel, start, before):
+        queries = stacked(qkv_refs[rel], 0, start)
+        grads = stacked(grad_refs[rel], 0, start)
+        heads = stacked(out_refs[rel], 0, start)
+        logs = stacked(log_refs[rel], 0, start)[:, :1]
+        inner = jnp.sum(grads.astype(jnp.float32) * heads.astype(jnp.float32), axis=-1, keepdims=True)
+
+        def span(rows, masked):
+            softmax = jnp.exp2(times_transposed(queries, keys[rows, :]) * scale - logs)
+            if masked:
+                softmax = jnp.where(mask, softmax, 0.0)
+            grad_softmax = times_transposed(grads, values[rows, :])
+            grad_scores = (softmax * (grad_softmax - inner)).astype(jnp.bfloat16)
+            grad_values[rows, :] += transposed_times(softmax.astype(jnp.bfloat16), grads)
+            grad_keys[rows, :] += transposed_times(grad_scores, queries)
+            return nn(grad_scores, keys[rows, :])
+
+        grad_queries = span(slice(before, before + TILE), True)
+        if before:
+            grad_queries = grad_queries + span(slice(0, before), False)
+        rows = slice(start, start + TILE)
+        cosine, sine = cosine_ref[rel, rows, :], -sine_ref[rel, rows, :]
+        for head in range(2):
+            part = grad_queries[head * TILE : (head + 1) * TILE] * factor
+            result_refs[rel][rows, head * LANES : (head + 1) * LANES] = turn(part, cosine, sine).astype(
+                jnp.bfloat16
+            )
+
+    each_tile(place_ref, qkv_refs, visit)
+    for rel, ref in enumerate(result_refs):
+        count = ref.shape[0]
+        position = lax.rem(place_ref[2] + rel, jnp.int32(2))
+        rows = pl.ds(pl.multiple_of(position * count, count), count)
+        ref[:, 2 * LANES : 3 * LANES] = turn(
+            grad_keys[rows, :] * factor, cosine_ref[rel], -sine_ref[rel]
+        ).astype(jnp.bfloat16)
+        ref[:, 3 * LANES :] = grad_values[rows, :].astype(jnp.bfloat16)
+
+
+def attend_back(place, qkv, grads, heads, logs, cosine, sine):
+    count = qkv[0].shape[0]
+    pairs = qkv[0].shape[1] // (4 * LANES)
+    wide = pl.BlockSpec((count, 4 * LANES), lambda i: (0, i))
+    narrow = pl.BlockSpec((count, 2 * LANES), lambda i: (0, i))
+    table = pl.BlockSpec((2, count, LANES), lambda i: (0, 0, 0))
+    result = jax.ShapeDtypeStruct(qkv[0].shape, jnp.bfloat16)
+    return pl.pallas_call(
+        attend_back_kernel,
+        grid=(pairs,),
+        out_shape=(result, result),
+        in_specs=[smem_spec(), wide, wide] + [narrow] * 6 + [table] * 2,
+        out_specs=(wide, wide),
+        scratch_shapes=[pltpu.VMEM((2 * count, LANES), jnp.bfloat16)] * 2
+        + [pltpu.VMEM((2 * count, LANES), jnp.float32)] * 2,
+        compiler_params=vmem_params(),
+        cost_estimate=pl.CostEstimate(
+            flops=pairs * 5 * 4 * count * count * 4 * LANES,
+            bytes_accessed=20 * qkv[0].size,
+            transcendentals=pairs * 4 * count * count,
+        ),
+        name="attend_back",
+    )(place, *qkv, *grads, *heads, *logs, cosine, sine)
+
+
+def feed_kernel(deep, blocks, place_ref, *refs):
+    rows_refs, grad_refs, refs = refs[:blocks], refs[blocks : 2 * blocks], refs[2 * blocks :]
+    wide_own, wide_other, refs = refs[:deep], refs[deep : 2 * deep], refs[2 * deep :]
+    down_own, down_other, refs = refs[:deep], refs[deep : 2 * deep], refs[2 * deep :]
+    outs, scratch = refs[: 5 * blocks], refs[5 * blocks :]
+    gate, up, down, hidden, grad_gate, grad_up, branch, grad_rows, in_sems, out_sems = scratch
+    part = wide_own[0].shape[1]
+    half = gate.shape[1] // 2
+    loads = []
+    for matrix, (target, own, other, column) in enumerate(
+        ((gate, wide_own, wide_other, 0), (up, wide_own, wide_other, half), (down, down_own, down_other, 0))
+    ):
+        here = []
+        for side, chunks in enumerate((own, other)):
+            for shift in range(deep):
+                for rel in range(2):
+                    copy = pltpu.make_async_copy(
+                        chunks[shift].at[rel, :, pl.ds(column, half)],
+                        target.at[
+                            pl.ds(row_offset(place_ref, shift, rel, deep, part), part),
+                            pl.ds(side * half, half),
+                        ],
+                        in_sems.at[matrix, side, shift, rel],
+                    )
+                    copy.start()
+                    here.append(copy)
+        loads.append(here)
+    stores = []
+
+    def store(scratch_ref, block, which):
+        copy = pltpu.make_async_copy(
+            scratch_ref.at[block], outs[block * 5 + which], out_sems.at[block, which]
+        )
+        copy.start()
+        stores.append(copy)
+
+    for block in range(blocks):
+        if block == 0:
+            for here in loads:
+                for copy in here:
+                    copy.wait()
+        width = gate.shape[1]
+
+        @pl.loop(0, width // TILE)
+        def _(step, block=block):
+            lanes = pl.ds(pl.multiple_of(step * TILE, TILE), TILE)
+            rows, grads = rows_refs[block][...], grad_refs[block][...]
+            gate_value = nn(rows, gate[:, lanes])
+            up_value = nn(rows, up[:, lanes])
+            grad_hidden = nn(grads, down[:, lanes])
+            sigmoid = 1.0 / (1.0 + jnp.exp(-gate_value))
+            swish = gate_value * sigmoid
+            slope = sigmoid + swish * (1.0 - sigmoid)
+            hidden[block, :, lanes] = (swish * up_value).astype(jnp.bfloat16)
+            grad_gate[block, :, lanes] = (grad_hidden * up_value * slope).astype(jnp.bfloat16)
+            grad_up[block, :, lanes] = (grad_hidden * swish).astype(jnp.bfloat16)
+
+        store(hidden, block, 0)
+        store(grad_gate, block, 1)
+        store(grad_up, block, 2)
+
+        @pl.loop(0, gate.shape[0] // TILE)
+        def _(step, block=block):
+            lanes = pl.ds(pl.multiple_of(step * TILE, TILE), TILE)
+            grad_rows[block, :, lanes] = (
+                times_transposed(grad_gate[block], gate[lanes, :])
+                + times_transposed(grad_up[block], up[lanes, :])
+            ).astype(jnp.bfloat16)
+            branch[block, :, lanes] = times_transposed(hidden[block], down[lanes, :]).astype(
+                jnp.bfloat16
+            )
+
+        store(branch, block, 3)
+        store(grad_rows, block, 4)
+    for copy in stores:
+        copy.wait()
+
+
+def feed(place, rows, grads, wide_own, wide_other, down_own, down_other):
+    deep, part = len(wide_own), wide_own[0].shape[1]
+    width, hidden_units = deep * 2 * part, 2 * down_own[0].shape[2]
+    blocks = len(rows)
+    count = rows[0].shape[0]
+    small = jax.ShapeDtypeStruct((count, hidden_units), jnp.bfloat16)
+    large = jax.ShapeDtypeStruct((count, width), jnp.bfloat16)
+    outs = pl.pallas_call(
+        functools.partial(feed_kernel, deep, blocks),
+        out_shape=(small, small, small, large, large) * blocks,
+        in_specs=[smem_spec()] + [vmem_spec()] * (2 * blocks) + [any_spec()] * (4 * deep),
+        out_specs=(any_spec(),) * (5 * blocks),
+        scratch_shapes=[pltpu.VMEM((width, hidden_units), jnp.bfloat16)] * 3
+        + [pltpu.VMEM((blocks, count, hidden_units), jnp.bfloat16)] * 3
+        + [pltpu.VMEM((blocks, count, width), jnp.bfloat16)] * 2
+        + [pltpu.SemaphoreType.DMA((3, 2, deep, 2)), pltpu.SemaphoreType.DMA((blocks, 5))],
+        compiler_params=vmem_params(),
+        cost_estimate=pl.CostEstimate(
+            flops=blocks * 12 * count * width * hidden_units,
+            bytes_accessed=2 * (3 * width * hidden_units + blocks * count * (4 * width + 3 * hidden_units)),
+            transcendentals=blocks * count * hidden_units,
+        ),
+        name="feed",
+    )(place, *rows, *grads, *wide_own, *wide_other, *down_own, *down_other)
+    return [outs[5 * block : 5 * block + 5] for block in range(blocks)]
+
+
+def weight_kernel(blocks, pairs, spread, added, *refs):
+    lefts, rights = refs[: blocks * pairs], refs[blocks * pairs : 2 * blocks * pairs]
+    rest = refs[2 * blocks * pairs :]
+    out_ref = rest[-1]
+    offset = 0
+    parts = []
+    for pair in range(pairs):
+        total = None
+        for block in range(blocks):
+            term = transposed_times(lefts[pair * blocks + block][...], rights[pair * blocks + block][...])
+            total = term if total is None else total + term
+        parts.append(total)
+    if spread:
+        joined = jnp.concatenate([part.astype(jnp.bfloat16) for part in parts], axis=1)
+        total = times_transposed(joined, rest[0][...])
+        if added:
+            total = total + rest[1][...].astype(jnp.float32)
+        out_ref[...] = total.astype(jnp.bfloat16)
+    else:
+        for pair, total in enumerate(parts):
+            lanes = slice(offset, offset + total.shape[1])
+            if added:
+                total = total + rest[0][:, lanes].astype(jnp.float32)
+            out_ref[:, lanes] = total.astype(jnp.bfloat16)
+            offset += total.shape[1]
+
+
+def weight_grad(pairs, side, spread=None, added=None, tile=256):
+    blocks = len(pairs[0][0])
+    lefts = [left for left_blocks, _ in pairs for left in left_blocks]
+    rights = [right for _, right_blocks in pairs for right in right_blocks]
+    count, width = lefts[0].shape
+    widths = [right_blocks[0].shape[1] // 2 for _, right_blocks in pairs]
+    columns = sum(widths) if spread is None else spread.shape[0]
+    operands = lefts + rights
+    in_specs = [pl.BlockSpec((count, tile), lambda i: (0, i)) for _ in lefts]
+    in_specs += [pl.BlockSpec((count, right.shape[1] // 2), lambda i: (0, side)) for right in rights]
+    if spread is not None:
+        operands.append(spread)
+        in_specs.append(pl.BlockSpec(spread.shape, lambda i: (0, 0)))
+    if added is not None:
+        operands.append(added)
+        in_specs.append(pl.BlockSpec((tile, columns), lambda i: (i, 0)))
+    return pl.pallas_call(
+        functools.partial(weight_kernel, blocks, len(pairs), spread is not None, added is not None),
+        grid=(width // tile,),
+        out_shape=jax.ShapeDtypeStruct((width, columns), jnp.bfloat16),
+        in_specs=in_specs,
+        out_specs=pl.BlockSpec((tile, columns), lambda i: (i, 0)),
+        compiler_params=vmem_params(),
+        cost_estimate=pl.CostEstimate(
+            flops=2 * blocks * count * width * sum(widths),
+            bytes_accessed=2 * (blocks * count * (width * len(pairs) + sum(widths)) + width * columns),
+            transcendentals=0,
+        ),
+        name="weight_grad",
+    )(*operands)
+
+
+def tables(rows, x_place):
+    lane = np.arange(LANES)
+    entry = lane % (LANES // 2)
+    live = (entry < HD // 2).astype(np.float32)
+    sign = np.where(lane < LANES // 2, -1.0, 1.0).astype(np.float32) * live
+    pair_entry = np.where(entry < HD // 2, entry, 0).astype(np.float32)
+    inverse = THETA ** (-2.0 * jnp.asarray(pair_entry) / HD)
+    both = []
+    for rel in range(2):
+        first = lax.rem(x_place + rel, jnp.int32(2)) * rows
+        position = (first + jnp.arange(rows, dtype=jnp.int32)).astype(jnp.float32)
+        both.append(position[:, None] * inverse[None, :])
+    angles = jnp.stack(both)
+    return jnp.cos(angles) * live, jnp.sin(angles) * sign
+
+
+def norm_factor(rows):
+    return lax.rsqrt(jnp.mean(rows * rows, axis=-1, keepdims=True) + EPSILON)
+
+
+def norm_back(rows, gain, grad):
+    factor = norm_factor(rows)
+    scaled = grad * gain
+    return factor * scaled - rows * factor**3 * jnp.mean(scaled * rows, axis=-1, keepdims=True)
+
+
+def spread_blocks(own):
+    beside = swap(own, "x")
+    return [own, beside, swap(own, "c"), swap(beside, "c")]
+
+
+def sum_blocks(parts):
+    beside = parts[1].astype(jnp.float32) + swap(parts[3], "c").astype(jnp.float32)
+    arrived = swap(beside.astype(jnp.bfloat16), "x")
+    own = parts[0].astype(jnp.float32) + swap(parts[2], "c").astype(jnp.float32)
+    return own + arrived.astype(jnp.float32)
+
+
+def gather_chunks(halves, core, deep):
+    keep = jnp.where(core == 0, halves[0], halves[1])
+    send = jnp.where(core == 0, halves[1], halves[0])
+    chunk = jnp.stack([keep, swap(send, "c")])
+    own = [chunk]
+    for shift in range(1, deep):
+        own.append(lax.ppermute(chunk, "z", [((i + shift) % deep, i) for i in range(deep)]))
+    other = [swap(piece, "y") for piece in own]
+    return own, other
+
+
+def finish_grad(summed, core, part):
+    mine = lax.psum_scatter(summed, "z", scatter_dimension=0, tiled=True)
+    keep = lax.dynamic_slice_in_dim(mine, core * part, part, axis=0)
+    send = lax.dynamic_slice_in_dim(mine, (1 - core) * part, part, axis=0)
+    recv = swap(send, "c")
+    first = jnp.where(core == 0, keep, recv).astype(jnp.float32)
+    second = jnp.where(core == 0, recv, keep).astype(jnp.float32)
+    return first, second
+
+
+def join(first, second, start, stop):
+    return jnp.concatenate([first[:, start:stop], second[:, start:stop]], axis=1)
+
+
+def gain_grad(columns, gain, depth_place, part):
+    rows = sum(jnp.sum(grad * weight.astype(jnp.float32), axis=1) for grad, weight in columns)
+    rows = rows / lax.dynamic_slice_in_dim(gain, depth_place * part, part)
+    rows = rows + swap(rows, "x")
+    rows = rows + swap(rows, "y")
+    piece = part // 4
+    place = lax.axis_index("y") * 2 + lax.axis_index("x")
+    return lax.dynamic_slice_in_dim(rows, place * piece, piece)
+
+
+def fast_local(
+    tokens,
+    cotangent,
+    first_gain,
+    query_weight,
+    key_weight,
+    value_weight,
+    out_weight,
+    second_gain,
+    gate_weight,
+    up_weight,
+    down_weight,
+):
+    deep = lax.axis_size("z")
+    z_place, core, x_place = (lax.axis_index(name).astype(jnp.int32) for name in ("z", "c", "x"))
+    place = jnp.stack([z_place, core, x_place])
+    rows = tokens.shape[0]
+    part = gate_weight.shape[0]
+    depth_place = z_place * 2 + core
+    own_rows = tokens.astype(jnp.float32)
+    first_normed = (own_rows * norm_factor(own_rows) * first_gain).astype(jnp.bfloat16)
+    out_turned, down_turned = out_weight.T, down_weight.T
+
+    def halves(*weights):
+        result = []
+        for half in range(2):
+            pieces = []
+            for weight in weights:
+                size = weight.shape[1] // 2
+                pieces.append(weight[:, half * size : (half + 1) * size])
+            result.append(jnp.concatenate(pieces, axis=1))
+        return result
+
+    spread = spread_heads(3, 3)
+    heads_own, heads_other = gather_chunks(
+        halves(query_weight, key_weight, value_weight, out_turned), core, deep
+    )
+    wide_own, wide_other = gather_chunks(halves(gate_weight, up_weight), core, deep)
+    down_own, down_other = gather_chunks(halves(down_turned), core, deep)
+    first_blocks = spread_blocks(first_normed)
+    qkv_weight, out_wide = prepare(place, heads_own, heads_other, spread)
+    cosine, sine = tables(rows, x_place)
+    qkv = [project(first_blocks[i], qkv_weight, cosine[i % 2], sine[i % 2]) for i in (0, 1, 2, 3)]
+    heads, logs = [], []
+    for sequence in range(2):
+        one, two, log_one, log_two = attend(place, qkv[2 * sequence], qkv[2 * sequence + 1])
+        heads += [one, two]
+        logs += [log_one, log_two]
+    branch = sum_blocks([times_transposed(block, out_wide).astype(jnp.bfloat16) for block in heads])
+    middle = own_rows + branch
+    second_normed = (middle * norm_factor(middle) * second_gain).astype(jnp.bfloat16)
+    cotangent_blocks = spread_blocks(cotangent)
+    second_blocks = spread_blocks(second_normed)
+    fed = [None] * 4
+    for pair in ((0, 2), (1, 3)):
+        outs = feed(
+            place,
+            [second_blocks[i] for i in pair],
+            [cotangent_blocks[i] for i in pair],
+            wide_own,
+            wide_other,
+            down_own,
+            down_other,
+        )
+        for i, out in zip(pair, outs):
+            fed[i] = out
+    hidden, grad_gate, grad_up, branches, grads_second = ([block[i] for block in fed] for i in range(5))
+    grad_second = sum_blocks(grads_second)
+    grad_middle = cotangent.astype(jnp.float32) + norm_back(middle, second_gain, grad_second)
+    grad_attention = spread_blocks(grad_middle.astype(jnp.bfloat16))
+    result = (middle + sum_blocks(branches)).astype(jnp.bfloat16)
+
+    down_sent = swap(weight_grad([(cotangent_blocks, hidden)], 1), "y")
+    wide_sent = swap(weight_grad([(second_blocks, grad_gate), (second_blocks, grad_up)], 1), "y")
+    down_grads = finish_grad(weight_grad([(cotangent_blocks, hidden)], 0, added=down_sent), core, part)
+    wide_grads = finish_grad(
+        weight_grad([(second_blocks, grad_gate), (second_blocks, grad_up)], 0, added=wide_sent), core, part
+    )
+
+    grad_heads = [nn(block, out_wide).astype(jnp.bfloat16) for block in grad_attention]
+    grad_qkv = []
+    for sequence in range(2):
+        chosen = slice(2 * sequence, 2 * sequence + 2)
+        grad_qkv += attend_back(
+            place, qkv[chosen], grad_heads[chosen], heads[chosen], logs[chosen], cosine, sine
+        )
+    grad_first = sum_blocks([times_transposed(block, qkv_weight).astype(jnp.bfloat16) for block in grad_qkv])
+    tokens_grad = grad_middle + norm_back(own_rows, first_gain, grad_first)
+    head_pairs = [(first_blocks, grad_qkv), (grad_attention, heads)]
+    heads_sent = swap(weight_grad(head_pairs, 1, spread=spread), "y")
+    heads_grads = finish_grad(
+        weight_grad(head_pairs, 0, spread=spread, added=heads_sent), core, part
+    )
+
+    sizes = [weight.shape[1] // 2 for weight in (query_weight, key_weight, value_weight, out_turned)]
+    starts = np.cumsum([0] + sizes)
+    query_grad, key_grad, value_grad, out_grad = (
+        join(*heads_grads, int(starts[i]), int(starts[i + 1])) for i in range(4)
+    )
+    half = gate_weight.shape[1] // 2
+    gate_grad, up_grad = (join(*wide_grads, i * half, (i + 1) * half) for i in range(2))
+    down_grad = join(*down_grads, 0, half)
+    first_gain_grad = gain_grad(
+        ((query_grad, query_weight), (key_grad, key_weight), (value_grad, value_weight)),
+        first_gain,
+        depth_place,
+        part,
+    )
+    second_gain_grad = gain_grad(
+        ((gate_grad, gate_weight), (up_grad, up_weight)), second_gain, depth_place, part
+    )
+    return (
+        result,
+        tokens_grad,
+        query_grad,
+        key_grad,
+        value_grad,
+        out_grad.T,
+        gate_grad,
+        up_grad,
+        down_grad.T,
+        first_gain_grad,
+        second_gain_grad,
+    )
+
+
+def specs(depth, width):
+    both = depth + width
+    rows, inward, outward = P(both, None), P(depth, width), P(width, depth)
+    in_specs = (rows, rows, P(), inward, inward, inward, outward, P(), inward, inward, outward)
+    out_specs = (rows, rows, inward, inward, inward, outward, inward, inward, outward, P(both), P(both))
+    return in_specs, out_specs
+
+
 def solution(mesh):
-    in_specs = (
-        P(("dp", "tensor"), None),
-        P(("dp", "tensor"), None),
-        P(),
-        P("dp", "tensor"),
-        P("dp", "tensor"),
-        P("dp", "tensor"),
-        P("tensor", "dp"),
-        P(),
-        P("dp", "tensor"),
-        P("dp", "tensor"),
-        P("tensor", "dp"),
-    )
-    out_specs = (
-        P(("dp", "tensor"), None),
-        P(("dp", "tensor"), None),
-        P("dp", "tensor"),
-        P("dp", "tensor"),
-        P("dp", "tensor"),
-        P("tensor", "dp"),
-        P("dp", "tensor"),
-        P("dp", "tensor"),
-        P("tensor", "dp"),
-        P(("dp", "tensor")),
-        P(("dp", "tensor")),
-    )
-    return jax.shard_map(local, mesh=mesh, in_specs=in_specs, out_specs=out_specs, check_vma=False)
+    depth, width = mesh.shape["dp"], mesh.shape["tensor"]
+
+    def run(tokens, cotangent, *weights):
+        fits = (
+            width == 4
+            and depth % 2 == 0
+            and tokens.shape[0] * 2 == SEQ_LEN * depth * width
+            and weights[2].shape[1] == 2 * width * HD
+            and weights[1].shape[1] == 4 * width * HD
+        )
+        if fits:
+            devices = mesh.devices.reshape(depth // 2, 2, 2, 2)
+            fine = jax.sharding.Mesh(devices, ("z", "c", "y", "x"))
+            in_specs, out_specs = specs(("z", "c"), ("y", "x"))
+            call, over = fast_local, fine
+        else:
+            in_specs, out_specs = specs(("dp",), ("tensor",))
+            call, over = local, mesh
+        return jax.shard_map(call, mesh=over, in_specs=in_specs, out_specs=out_specs, check_vma=False)(
+            tokens, cotangent, *weights
+        )
+
+    return run

time: 1360 us -> 774 us (0.57); the launches traced: 1340 us -> 770 us
  waiting for transfers between devices: 757 us -> 381 us
  matrix products: 280 us -> 32.7 us
  Pallas kernels: 0 us -> 216 us
  local copies, waits for them, and re-layouts: 138 us -> 21.9 us
  blocking collectives: 70.5 us -> 0 us
  starting transfers between devices: 8.41 us -> 64.8 us
  other arithmetic: 70.9 us -> 39 us
    reduce_scatter x10 -> x3, waiting for transfers between devices: 396 us -> 22.4 us  [finish_grad(): mine = lax.psum_scatter(summed, 'z', scatter_dimension=0, tiled=True)]
    ppermute x0 -> x58, waiting for transfers between devices: none -> 358 us  [the longest x49 254 us: swap(): return lax.ppermute(value, axis, [(0, 1), (1, 0)])]
    all_gather x9 -> x0, waiting for transfers between devices: 288 us -> none  [the longest x2 110 us: gather_rows(): return lax.all_gather(shard, 'tensor', axis=0, tiled=True)]
    pallas_call x0 -> x17, Pallas kernels: none -> 216 us  [the longest x6 75.3 us: weight_grad(): pl.pallas_call(functools.partial(weight_kernel, blocks, len(pairs), sprea...]
    dot_general x28 -> x4, matrix products: 214 us -> 9.6 us  [nn(): return jnp.dot(left, right, preferred_element_type=jnp.float32)]
    dynamic_update_slice x8 -> x0, local copies, waits for them, and re-layouts: 88.9 us -> none  [local(): lax.map(attend_backward, (queries, keys_rot, values, grad_mixed, log_total))]
    ppermute x0 -> x58, starting transfers between devices: none -> 64.3 us  [the longest x49 36.7 us: swap(): return lax.ppermute(value, axis, [(0, 1), (1, 0)])]
    dot_general x7 -> x8, matrix products: 66.7 us -> 23.1 us  [times_transposed(): lax.dot_general(left, right, (((1,), (1,)), ((), ())), preferred_element_...]
  transfers between devices with their start and end apart: 22 -> 61, of which waited for: 17 -> 22; matrix products, arithmetic and copies ran while one was open for 31% -> 11% of each run, Pallas kernels for 0% -> 26%
where the time goes in v1:
time: 774 us; the launch traced here: 770 us
  waiting for transfers between devices  381 us (49%)
  Pallas kernels  216 us (28%)
  starting transfers between devices  64.8 us (8%)
  other arithmetic  39 us (5%)
  matrix products  32.7 us (4%)
  local copies, waits for them, and re-layouts  21.9 us (3%)
  between operations  15.1 us (2%)
    ppermute x49, waiting for transfers between devices, swap(): return lax.ppermute(value, axis, [(0, 1), (1, 0)])  254 us
    ppermute x9, waiting for transfers between devices, gather_chunks(): lax.ppermute(chunk, 'z', [((i + shift) % deep, i) for i in range(deep)])  105 us
    pallas_call x6, Pallas kernels, weight_grad(): pl.pallas_call(functools.partial(weight_kernel, blocks, len(pairs), sprea...  75.3 us
    pallas_call x2, Pallas kernels, feed(): pl.pallas_call(functools.partial(feed_kernel, deep, blocks), out_shape=(s...  65.1 us
    ppermute x49, starting transfers between devices, swap(): return lax.ppermute(value, axis, [(0, 1), (1, 0)])  36.7 us
    pallas_call x2, Pallas kernels, attend_back(): pl.pallas_call(attend_back_kernel, grid=(pairs,), out_shape=(result, resu...  28.9 us
    ppermute x9, starting transfers between devices, gather_chunks(): lax.ppermute(chunk, 'z', [((i + shift) % deep, i) for i in range(deep)])  27.6 us
    dot_general x8, matrix products, times_transposed(): lax.dot_general(left, right, (((1,), (1,)), ((), ())), preferred_element_...  23.1 us
  transfers between devices with their start and end apart: 61, of which 22 were waited for; matrix products, arithmetic and copies ran while one was open for 11% of the time, Pallas kernels for 26%

profile of v1, /device:TPU:0, one launch (start us, length us, event | category | flops | bytes accessed | tf_op | source)
XLA Modules:
  0.0 769.9 jit_solution(9473884782247723857)
XLA Ops:
  20.8 26.9 %collective-permute-done.8.rows_ref.refs_1_ = bf16[512,1536]{1,0:T(8,128)(2,1)S(1)} collective-permute-done((bf16[512,1536]{1,0:T(8,128)(2,1)S(1)}, bf16[512,1536]{1,0:T(8,128)(2,1)S(1)}, u32[]{:S(2)}, u32[]{:S(2)}) %collective-permute-start.8) | collective-permute-done | bytes 1572896 | tf_op jit(solution)/shard_map/ppermute | solution.py:281
  56.7 27.7 %collective-permute-done.2.refs_2_ = bf16[2,192,576]{2,1,0:T(8,128)(2,1)S(1)} collective-permute-done((bf16[2,192,576]{2,1,0:T(8,128)(2,1)}, bf16[2,192,576]{2,1,0:T(8,128)(2,1)S(1)}, u32[]{:S(2)}, u32[]{:S(2)}) %collective-permute-start.2) | collective-permute-done | bytes 442400 | tf_op jit(solution)/shard_map/ppermute | solution.py:776
  89.6 9.0 %collective-permute-done.5.refs_5_ = bf16[2,192,576]{2,1,0:T(8,128)(2,1)S(1)} collective-permute-done((bf16[2,192,576]{2,1,0:T(8,128)(2,1)}, bf16[2,192,576]{2,1,0:T(8,128)(2,1)S(1)}, u32[]{:S(2)}, u32[]{:S(2)}) %collective-permute-start.5) | collective-permute-done | bytes 442400 | tf_op jit(solution)/shard_map/ppermute | solution.py:281
  98.7 10.5 %collective-permute-done.6.refs_6_ = bf16[2,192,576]{2,1,0:T(8,128)(2,1)S(1)} collective-permute-done((bf16[2,192,576]{2,1,0:T(8,128)(2,1)S(1)}, bf16[2,192,576]{2,1,0:T(8,128)(2,1)S(1)}, u32[]{:S(2)}, u32[]{:S(2)}) %collective-permute-start.6) | collective-permute-done | bytes 442400 | tf_op jit(solution)/shard_map/ppermute | solution.py:281
  110.0 8.7 %collective-permute-done.7.refs_7_ = bf16[2,192,576]{2,1,0:T(8,128)(2,1)} collective-permute-done((bf16[2,192,576]{2,1,0:T(8,128)(2,1)S(1)}, bf16[2,192,576]{2,1,0:T(8,128)(2,1)}, u32[]{:S(2)}, u32[]{:S(2)}) %collective-permute-start.7) | collective-permute-done | bytes 442400 | tf_op jit(solution)/shard_map/ppermute | solution.py:281
  118.7 8.4 %prepare.1 = (bf16[1536,1024]{1,0:T(8,128)(2,1)}, bf16[1536,512]{1,0:T(8,128)(2,1)}) custom-call(s32[3]{0:T(128)} %pad_add_fusion.place_ref, bf16[2,192,576]{2,1,0:T(8,128)(2,1)} %pad_maximum_fusion.4.refs_0_, bf16[2,192,576]{2,1,0:T(8,128)(2,1)} %collective-permute-done.1.refs_1_, bf16[2,192,576]{2,1,0:T(8,128)(2,1)} %copy-done.58, ...), custom_call_target="tpu_custom_call" | custom-call | flops 2717908992 | bytes 14155776 | tf_op jit(solution)/shard_map/prepare/pallas_call | solution.py:342
  138.5 9.1 %attend.3 = (bf16[512,512]{1,0:T(8,128)(2,1)}, bf16[512,512]{1,0:T(8,128)(2,1)}, f32[512,512]{1,0:T(8,128)}, f32[512,512]{1,0:T(8,128)}) custom-call(s32[3]{0:T(128)} %pad_add_fusion.place_ref, bf16[512,1024]{1,0:T(8,128)(2,1)} %project.6.a_ref, bf16[512,1024]{1,0:T(8,128)(2,1)} %project.7.b_ref), custom_call_target="tpu_custom_call" | custom-call | flops 2147483648 | bytes 6291456 | tf_op jit(solution)/shard_map/attend/pallas_call | solution.py:474
  159.9 8.6 %attend.2 = (bf16[512,512]{1,0:T(8,128)(2,1)}, bf16[512,512]{1,0:T(8,128)(2,1)}, f32[512,512]{1,0:T(8,128)}, f32[512,512]{1,0:T(8,128)}) custom-call(s32[3]{0:T(128)} %pad_add_fusion.place_ref, bf16[512,1024]{1,0:T(8,128)(2,1)} %project.4.a_ref, bf16[512,1024]{1,0:T(8,128)(2,1)} %project.5.b_ref), custom_call_target="tpu_custom_call" | custom-call | flops 2147483648 | bytes 6291456 | tf_op jit(solution)/shard_map/attend/pallas_call | solution.py:474
  176.9 33.0 %collective-permute-done.13 = bf16[512,1536]{1,0:T(8,128)(2,1)S(1)} collective-permute-done((bf16[512,1536]{1,0:T(8,128)(2,1)S(1)}, bf16[512,1536]{1,0:T(8,128)(2,1)S(1)}, u32[]{:S(2)}, u32[]{:S(2)}) %collective-permute-start.13) | collective-permute-done | bytes 1572896 | tf_op jit(solution)/shard_map/ppermute | solution.py:281
  216.0 8.8 %collective-permute-done.25.refs_13_ = bf16[2,192,512]{2,1,0:T(8,128)(2,1)S(1)} collective-permute-done((bf16[2,192,512]{2,1,0:T(8,128)(2,1)S(1)}, bf16[2,192,512]{2,1,0:T(8,128)(2,1)S(1)}, u32[]{:S(2)}, u32[]{:S(2)}) %collective-permute-start.25) | collective-permute-done | bytes 393248 | tf_op jit(solution)/shard_map/ppermute | solution.py:776
  226.3 19.8 %collective-permute-done.26.refs_14_ = bf16[2,192,512]{2,1,0:T(8,128)(2,1)S(1)} collective-permute-done((bf16[2,192,512]{2,1,0:T(8,128)(2,1)S(1)}, bf16[2,192,512]{2,1,0:T(8,128)(2,1)S(1)}, u32[]{:S(2)}, u32[]{:S(2)}) %collective-permute-start.26) | collective-permute-done | bytes 393248 | tf_op jit(solution)/shard_map/ppermute | solution.py:776
  248.3 9.8 %collective-permute-done.29.refs_17_ = bf16[2,192,512]{2,1,0:T(8,128)(2,1)S(1)} collective-permute-done((bf16[2,192,512]{2,1,0:T(8,128)(2,1)S(1)}, bf16[2,192,512]{2,1,0:T(8,128)(2,1)S(1)}, u32[]{:S(2)}, u32[]{:S(2)}) %collective-permute-start.29) | collective-permute-done | bytes 393248 | tf_op jit(solution)/shard_map/ppermute | solution.py:281
  266.5 11.7 %collective-permute-start.18 = (bf16[2,192,1024]{2,1,0:T(8,128)(2,1)S(1)}, bf16[2,192,1024]{2,1,0:T(8,128)(2,1)S(1)}, u32[]{:S(2)}, u32[]{:S(2)}) collective-permute-start(bf16[2,192,1024]{2,1,0:T(8,128)(2,1)S(1)} %pad_maximum_fusion.refs_4_), channel_id=1, source_target_pairs={{16,0},{24,8},{0,16},{8,24},{17,1},{25,9},{1,17},{9,25},{18,2},{26... | collective-permute-start | bytes 2359304 | tf_op jit(solution)/shard_map/ppermute | solution.py:776
  286.1 48.3 %collective-permute-done.18.refs_6_ = bf16[2,192,1024]{2,1,0:T(8,128)(2,1)S(1)} collective-permute-done((bf16[2,192,1024]{2,1,0:T(8,128)(2,1)S(1)}, bf16[2,192,1024]{2,1,0:T(8,128)(2,1)S(1)}, u32[]{:S(2)}, u32[]{:S(2)}) %collective-permute-start.18) | collective-permute-done | bytes 786464 | tf_op jit(solution)/shard_map/ppermute | solution.py:776
  338.0 16.9 %collective-permute-done.21.refs_9_ = bf16[2,192,1024]{2,1,0:T(8,128)(2,1)S(1)} collective-permute-done((bf16[2,192,1024]{2,1,0:T(8,128)(2,1)S(1)}, bf16[2,192,1024]{2,1,0:T(8,128)(2,1)S(1)}, u32[]{:S(2)}, u32[]{:S(2)}) %collective-permute-start.21) | collective-permute-done | bytes 786464 | tf_op jit(solution)/shard_map/ppermute | solution.py:281
  355.0 16.8 %collective-permute-done.22.refs_10_ = bf16[2,192,1024]{2,1,0:T(8,128)(2,1)S(1)} collective-permute-done((bf16[2,192,1024]{2,1,0:T(8,128)(2,1)S(1)}, bf16[2,192,1024]{2,1,0:T(8,128)(2,1)S(1)}, u32[]{:S(2)}, u32[]{:S(2)}) %collective-permute-start.22) | collective-permute-done | bytes 786464 | tf_op jit(solution)/shard_map/ppermute | solution.py:281
  371.8 15.3 %collective-permute-done.23.refs_11_ = bf16[2,192,1024]{2,1,0:T(8,128)(2,1)S(1)} collective-permute-done((bf16[2,192,1024]{2,1,0:T(8,128)(2,1)S(1)}, bf16[2,192,1024]{2,1,0:T(8,128)(2,1)S(1)}, u32[]{:S(2)}, u32[]{:S(2)}) %collective-permute-start.23) | collective-permute-done | bytes 786464 | tf_op jit(solution)/shard_map/ppermute | solution.py:281
  390.3 32.7 %feed.3 = (bf16[512,1024]{1,0:T(8,128)(2,1)}, bf16[512,1024]{1,0:T(8,128)(2,1)}, bf16[512,1024]{1,0:T(8,128)(2,1)}, bf16[512,1536]{1,0:T(8,128)(2,1)}, bf16[512,...) custom-call(s32[3]{0:T(128)} %pad_add_fusion.place_ref, ...), custom_call_target="tpu_custom_call" | custom-call | flops 19327352832 | bytes 28311552 | tf_op jit(solution)/shard_map/feed/pallas_call | solution.py:653
  423.6 32.4 %feed.2 = (bf16[512,1024]{1,0:T(8,128)(2,1)}, bf16[512,1024]{1,0:T(8,128)(2,1)}, bf16[512,1024]{1,0:T(8,128)(2,1)}, bf16[512,1536]{1,0:T(8,128)(2,1)}, bf16[512,...) custom-call(s32[3]{0:T(128)} %pad_add_fusion.place_ref, ...), custom_call_target="tpu_custom_call" | custom-call | flops 19327352832 | bytes 28311552 | tf_op jit(solution)/shard_map/feed/pallas_call | solution.py:653
  456.6 8.6 %weight_grad.10 = bf16[1536,512]{1,0:T(8,128)(2,1)} custom-call(bf16[512,1536]{1,0:T(8,128)(2,1)} %refs_0_.3, bf16[512,1536]{1,0:T(8,128)(2,1)} %copy-done.11, bf16[512,1536]{1,0:T(8,128)(2,1)} %collective-permute-done.15.refs_3_.refs_2_, bf16[512,1536]{1,0:T(8,128)(2,1)} %copy-done.12, bf16[512,1024]{1,0:T(8,128)(2,1)} %get-tuple-element.75.refs_4_, ...), custom_call_target="tpu_custom_call" | custom-call | flops 3221225472 | bytes 9961472 | tf_op jit(solution)/shard_map/weight_grad/pallas_call | solution.py:716
  468.8 13.3 %weight_grad.8 = bf16[1536,1024]{1,0:T(8,128)(2,1)} custom-call(bf16[512,1536]{1,0:T(8,128)(2,1)} %copy-done.1, bf16[512,1536]{1,0:T(8,128)(2,1)} %copy-done.6, bf16[512,1536]{1,0:T(8,128)(2,1)} %collective-permute-done.14.refs_1_.refs_2_.refs_6_, bf16[512,1536]{1,0:T(8,128)(2,1)} %copy-done.7, bf16[512,1536]{1,0:T(8,128)(2,1)} %copy-done.1, ...), custom_call_target="tpu_custom_call" | custom-call | flops 6442450944 | bytes 19922944 | tf_op jit(solution)/shard_map/weight_grad/pallas_call | solution.py:716
  484.3 18.4 %collective-permute-done.52.refs_8_ = bf16[1536,512]{1,0:T(8,128)(2,1)} collective-permute-done((bf16[1536,512]{1,0:T(8,128)(2,1)}, bf16[1536,512]{1,0:T(8,128)(2,1)}, u32[]{:S(2)}, u32[]{:S(2)}) %collective-permute-start.52) | collective-permute-done | bytes 1572896 | tf_op jit(solution)/shard_map/ppermute | solution.py:281
  503.4 8.8 %weight_grad.11 = bf16[1536,512]{1,0:T(8,128)(2,1)} custom-call(bf16[512,1536]{1,0:T(8,128)(2,1)} %refs_0_.3, bf16[512,1536]{1,0:T(8,128)(2,1)} %copy-done.11, bf16[512,1536]{1,0:T(8,128)(2,1)} %collective-permute-done.15.refs_3_.refs_2_, bf16[512,1536]{1,0:T(8,128)(2,1)} %copy-done.12, bf16[512,1024]{1,0:T(8,128)(2,1)} %get-tuple-element.75.refs_4_, ...), custom_call_target="tpu_custom_call" | custom-call | flops 3221225472 | bytes 9961472 | tf_op jit(solution)/shard_map/weight_grad/pallas_call | solution.py:716
  515.7 22.6 %collective-permute-done.38 = bf16[512,1536]{1,0:T(8,128)(2,1)} collective-permute-done((bf16[512,1536]{1,0:T(8,128)(2,1)}, bf16[512,1536]{1,0:T(8,128)(2,1)}, u32[]{:S(2)}, u32[]{:S(2)}) %collective-permute-start.38) | collective-permute-done | bytes 1572896 | tf_op jit(solution)/shard_map/ppermute | solution.py:281
  545.0 24.3 %collective-permute-done.50.refs_16_ = bf16[1536,1024]{1,0:T(8,128)(2,1)} collective-permute-done((bf16[1536,1024]{1,0:T(8,128)(2,1)}, bf16[1536,1024]{1,0:T(8,128)(2,1)}, u32[]{:S(2)}, u32[]{:S(2)}) %collective-permute-start.50) | collective-permute-done | bytes 3145760 | tf_op jit(solution)/shard_map/ppermute | solution.py:281
  569.3 13.6 %weight_grad.9 = bf16[1536,1024]{1,0:T(8,128)(2,1)} custom-call(bf16[512,1536]{1,0:T(8,128)(2,1)} %copy-done.1, bf16[512,1536]{1,0:T(8,128)(2,1)} %copy-done.6, bf16[512,1536]{1,0:T(8,128)(2,1)} %collective-permute-done.14.refs_1_.refs_2_.refs_6_, bf16[512,1536]{1,0:T(8,128)(2,1)} %copy-done.7, bf16[512,1536]{1,0:T(8,128)(2,1)} %copy-done.1, ...), custom_call_target="tpu_custom_call" | custom-call | flops 6442450944 | bytes 19922944 | tf_op jit(solution)/shard_map/weight_grad/pallas_call | solution.py:716
  591.3 14.3 %attend_back.2 = (bf16[512,1024]{1,0:T(8,128)(2,1)}, bf16[512,1024]{1,0:T(8,128)(2,1)}) custom-call(s32[3]{0:T(128)} %pad_add_fusion.place_ref, bf16[512,1024]{1,0:T(8,128)(2,1)} %project.4.a_ref, bf16[512,1024]{1,0:T(8,128)(2,1)} %project.5.b_ref, bf16[512,512]{1,0:T(8,128)(2,1)} %convolution_convert_fusion.11.ga_ref, ...), custom_call_target="tpu_custom_call" | custom-call | flops 5368709120 | bytes 10485760 | tf_op jit(solution)/shard_map/attend_back/pallas_call | solution.py:550
  607.4 14.6 %attend_back.3 = (bf16[512,1024]{1,0:T(8,128)(2,1)}, bf16[512,1024]{1,0:T(8,128)(2,1)}) custom-call(s32[3]{0:T(128)} %pad_add_fusion.place_ref, bf16[512,1024]{1,0:T(8,128)(2,1)} %project.6.a_ref, bf16[512,1024]{1,0:T(8,128)(2,1)} %project.7.b_ref, bf16[512,512]{1,0:T(8,128)(2,1)} %convolution_convert_fusion.9.ga_ref, ...), custom_call_target="tpu_custom_call" | custom-call | flops 5368709120 | bytes 10485760 | tf_op jit(solution)/shard_map/attend_back/pallas_call | solution.py:550
  626.2 15.5 %weight_grad.6 = bf16[1536,576]{1,0:T(8,128)(2,1)} custom-call(bf16[512,1536]{1,0:T(8,128)(2,1)} %copy-done.5, bf16[512,1536]{1,0:T(8,128)(2,1)} %copy-done.8, bf16[512,1536]{1,0:T(8,128)(2,1)} %collective-permute-done.9.rows_ref.refs_2_, bf16[512,1536]{1,0:T(8,128)(2,1)} %copy-done.9, bf16[512,1536]{1,0:T(8,128)(2,1)} %get-tuple-element.89.refs_4_, ...), custom_call_target="tpu_custom_call" | custom-call | flops 4831838208 | bytes 17498112 | tf_op jit(solution)/shard_map/weight_grad/pallas_call | solution.py:716
  657.0 29.9 %collective-permute-done.48 = bf16[1536,576]{0,1:T(8,128)(2,1)} collective-permute-done((bf16[1536,576]{0,1:T(8,128)(2,1)}, bf16[1536,576]{0,1:T(8,128)(2,1)}, u32[]{:S(2)}, u32[]{:S(2)}) %collective-permute-start.48) | collective-permute-done | bytes 1769504 | tf_op jit(solution)/shard_map/ppermute | solution.py:281
  690.8 15.6 %weight_grad.7 = bf16[1536,576]{1,0:T(8,128)(2,1)} custom-call(bf16[512,1536]{1,0:T(8,128)(2,1)} %copy-done.5, bf16[512,1536]{1,0:T(8,128)(2,1)} %copy-done.8, bf16[512,1536]{1,0:T(8,128)(2,1)} %collective-permute-done.9.rows_ref.refs_2_, bf16[512,1536]{1,0:T(8,128)(2,1)} %copy-done.9, bf16[512,1536]{1,0:T(8,128)(2,1)} %get-tuple-element.89.refs_4_, ...), custom_call_target="tpu_custom_call" | custom-call | flops 4831838208 | bytes 17498112 | tf_op jit(solution)/shard_map/weight_grad/pallas_call | solution.py:716
  722.9 22.4 %reduce-scatter.4.cloned.1.call-done = bf16[384,576]{1,0:T(8,128)(2,1)} async-done(((bf16[1536,576]{1,0:T(8,128)(2,1)}), bf16[384,576]{1,0:T(8,128)(2,1)}) %reduce-scatter.4.cloned.1.call-update) | async-done | bytes 442384 | tf_op jit(solution)/shard_map/reduce_scatter | solution.py:782
  (325 shorter events, 178.6 us)
Async XLA Ops:
  7.2 699.3 %reduce-scatter.8.cloned.1.call-start = ((), (), s32[]{:S(2)}) async-start(), calls=%async_computation.5 | async-start | bytes 1966080 | tf_op jit(solution)/shard_map/reduce_scatter | solution.py:782
  10.3 37.3 %collective-permute-start.8 = (bf16[512,1536]{1,0:T(8,128)(2,1)S(1)}, bf16[512,1536]{1,0:T(8,128)(2,1)S(1)}, u32[]{:S(2)}, u32[]{:S(2)}) collective-permute-start(bf16[512,1536]{1,0:T(8,128)(2,1)S(1)} %fusion.2.rows_ref.refs_0_), channel_id=1, source_target_pairs={{0,1},{1,0},{2,3},{3,2},{4,5},{5,4},{6,7},{7,6},{8,9},{9,8},{10,11... | collective-permute-start | bytes 4718600 | tf_op jit(solution)/shard_map/ppermute | solution.py:281
  20.8 106.4 %collective-permute-start.9 = (bf16[512,1536]{1,0:T(8,128)(2,1)S(1)}, bf16[512,1536]{1,0:T(8,128)(2,1)}, u32[]{:S(2)}, u32[]{:S(2)}) collective-permute-start(bf16[512,1536]{1,0:T(8,128)(2,1)S(1)} %fusion.2.rows_ref.refs_0_), channel_id=1, source_target_pairs={{0,4},{4,0},{1,5},{5,1},{2,6},{6,2},{3,7},{7,3},{8,12},{12,8},{9,1... | collective-permute-start | bytes 4718600 | tf_op jit(solution)/shard_map/ppermute | solution.py:281
  47.7 84.6 %collective-permute-start.10 = (bf16[512,1536]{1,0:T(8,128)(2,1)S(1)}, bf16[512,1536]{1,0:T(8,128)(2,1)S(1)}, u32[]{:S(2)}, u32[]{:S(2)}) collective-permute-start(bf16[512,1536]{1,0:T(8,128)(2,1)S(1)} %collective-permute-done.8.rows_ref.refs_1_), channel_id=1, source_target_pairs={{0,4},{4,0},{1,5},{5,1},{2,6},{6,2},{3,7},{7,3},{8,12},{12,8},{9,1... | collective-permute-start | bytes 4718600 | tf_op jit(solution)/shard_map/ppermute | solution.py:281
  172.6 37.3 %collective-permute-start.13 = (bf16[512,1536]{1,0:T(8,128)(2,1)S(1)}, bf16[512,1536]{1,0:T(8,128)(2,1)S(1)}, u32[]{:S(2)}, u32[]{:S(2)}) collective-permute-start(bf16[512,1536]{1,0:T(8,128)(2,1)S(1)} %add_convert_fusion.4), channel_id=1, source_target_pairs={{0,1},{1,0},{2,3},{3,2},{4,5},{5,4},{6,7},{7,6},{8,9},{9,8},{10,11... | collective-permute-start | bytes 4718600 | tf_op jit(solution)/shard_map/ppermute | solution.py:281
  174.0 111.4 %collective-permute-start.35 = (bf16[512,1536]{1,0:T(8,128)(2,1)}, bf16[512,1536]{1,0:T(8,128)(2,1)S(1)}, u32[]{:S(2)}, u32[]{:S(2)}) collective-permute-start(bf16[512,1536]{1,0:T(8,128)(2,1)} %refs_0_.3), channel_id=1, source_target_pairs={{0,1},{1,0},{2,3},{3,2},{4,5},{5,4},{6,7},{7,6},{8,9},{9,8},{10,11... | collective-permute-start | bytes 4718600 | tf_op jit(solution)/shard_map/ppermute | solution.py:281
  175.0 38.9 %collective-permute-start.16 = (bf16[192,1024]{1,0:T(8,128)(2,1)S(1)}, bf16[192,1024]{1,0:T(8,128)(2,1)S(1)}, u32[]{:S(2)}, u32[]{:S(2)}) collective-permute-start(bf16[192,1024]{1,0:T(8,128)(2,1)S(1)} %maximum_select_fusion.1), channel_id=1, source_target_pairs={{0,4},{4,0},{1,5},{5,1},{2,6},{6,2},{3,7},{7,3},{8,12},{12,8},{9,1... | collective-permute-start | bytes 1179656 | tf_op jit(solution)/shard_map/ppermute | solution.py:281
  175.1 38.6 %collective-permute-start.24 = (bf16[192,512]{1,0:T(8,128)(2,1)S(1)}, bf16[192,512]{1,0:T(8,128)(2,1)S(1)}, u32[]{:S(2)}, u32[]{:S(2)}) collective-permute-start(bf16[192,512]{1,0:T(8,128)(2,1)S(1)} %get-tuple-element.119), channel_id=1, source_target_pairs={{0,4},{4,0},{1,5},{5,1},{2,6},{6,2},{3,7},{7,3},{8,12},{12,8},{9,1... | collective-permute-start | bytes 589832 | tf_op jit(solution)/shard_map/ppermute | solution.py:281
  212.3 73.2 %collective-permute-start.33 = (bf16[512,1536]{1,0:T(8,128)(2,1)S(1)}, bf16[512,1536]{1,0:T(8,128)(2,1)S(1)}, u32[]{:S(2)}, u32[]{:S(2)}) collective-permute-start(bf16[512,1536]{1,0:T(8,128)(2,1)S(1)} %multiply_convert_fusion.refs_0_.refs_4_), channel_id=1, source_target_pairs={{0,1},{1,0},{2,3},{3,2},{4,5},{5,4},{6,7},{7,6},{8,9},{9,8},{10,11... | collective-permute-start | bytes 4718600 | tf_op jit(solution)/shard_map/ppermute | solution.py:281
  247.6 36.1 %collective-permute-start.17 = (bf16[2,192,1024]{2,1,0:T(8,128)(2,1)S(1)}, bf16[2,192,1024]{2,1,0:T(8,128)(2,1)S(1)}, u32[]{:S(2)}, u32[]{:S(2)}) collective-permute-start(bf16[2,192,1024]{2,1,0:T(8,128)(2,1)S(1)} %pad_maximum_fusion.refs_4_), channel_id=1, source_target_pairs={{8,0},{16,8},{24,16},{0,24},{9,1},{17,9},{25,17},{1,25},{10,2},{18... | collective-permute-start | bytes 2359304 | tf_op jit(solution)/shard_map/ppermute | solution.py:776
  266.5 68.0 %collective-permute-start.18 = (bf16[2,192,1024]{2,1,0:T(8,128)(2,1)S(1)}, bf16[2,192,1024]{2,1,0:T(8,128)(2,1)S(1)}, u32[]{:S(2)}, u32[]{:S(2)}) collective-permute-start(bf16[2,192,1024]{2,1,0:T(8,128)(2,1)S(1)} %pad_maximum_fusion.refs_4_), channel_id=1, source_target_pairs={{16,0},{24,8},{0,16},{8,24},{17,1},{25,9},{1,17},{9,25},{18,2},{26... | collective-permute-start | bytes 2359304 | tf_op jit(solution)/shard_map/ppermute | solution.py:776
  278.2 57.7 %collective-permute-start.19 = (bf16[2,192,1024]{2,1,0:T(8,128)(2,1)S(1)}, bf16[2,192,1024]{2,1,0:T(8,128)(2,1)S(1)}, u32[]{:S(2)}, u32[]{:S(2)}) collective-permute-start(bf16[2,192,1024]{2,1,0:T(8,128)(2,1)S(1)} %pad_maximum_fusion.refs_4_), channel_id=1, source_target_pairs={{24,0},{0,8},{8,16},{16,24},{25,1},{1,9},{9,17},{17,25},{26,2},{2,... | collective-permute-start | bytes 2359304 | tf_op jit(solution)/shard_map/ppermute | solution.py:776
  283.8 52.7 %collective-permute-start.20 = (bf16[2,192,1024]{2,1,0:T(8,128)(2,1)S(1)}, bf16[2,192,1024]{2,1,0:T(8,128)(2,1)S(1)}, u32[]{:S(2)}, u32[]{:S(2)}) collective-permute-start(bf16[2,192,1024]{2,1,0:T(8,128)(2,1)S(1)} %pad_maximum_fusion.refs_4_), channel_id=1, source_target_pairs={{0,2},{2,0},{1,3},{3,1},{4,6},{6,4},{5,7},{7,5},{8,10},{10,8},{9,1... | collective-permute-start | bytes 2359304 | tf_op jit(solution)/shard_map/ppermute | solution.py:281
  285.5 101.7 %collective-permute-start.36 = (bf16[512,1536]{1,0:T(8,128)(2,1)S(1)}, bf16[512,1536]{1,0:T(8,128)(2,1)S(1)}, u32[]{:S(2)}, u32[]{:S(2)}) collective-permute-start(bf16[512,1536]{1,0:T(8,128)(2,1)S(1)} %collective-permute-done.35.refs_2_.refs_1_), channel_id=1, source_target_pairs={{0,4},{4,0},{1,5},{5,1},{2,6},{6,2},{3,7},{7,3},{8,12},{12,8},{9,1... | collective-permute-start | bytes 4718600 | tf_op jit(solution)/shard_map/ppermute | solution.py:281
  285.6 103.5 %collective-permute-start.34 = (bf16[512,1536]{1,0:T(8,128)(2,1)S(1)}, bf16[512,1536]{1,0:T(8,128)(2,1)S(1)}, u32[]{:S(2)}, u32[]{:S(2)}) collective-permute-start(bf16[512,1536]{1,0:T(8,128)(2,1)S(1)} %collective-permute-done.33.refs_0_.refs_1_.refs_5_), channel_id=1, source_target_pairs={{0,4},{4,0},{1,5},{5,1},{2,6},{6,2},{3,7},{7,3},{8,12},{12,8},{9,1... | collective-permute-start | bytes 4718600 | tf_op jit(solution)/shard_map/ppermute | solution.py:281
  336.5 50.6 %collective-permute-start.23 = (bf16[2,192,1024]{2,1,0:T(8,128)(2,1)S(1)}, bf16[2,192,1024]{2,1,0:T(8,128)(2,1)S(1)}, u32[]{:S(2)}, u32[]{:S(2)}) collective-permute-start(bf16[2,192,1024]{2,1,0:T(8,128)(2,1)S(1)} %collective-permute-done.19.refs_7_), channel_id=1, source_target_pairs={{0,2},{2,0},{1,3},{3,1},{4,6},{6,4},{5,7},{7,5},{8,10},{10,8},{9,1... | collective-permute-start | bytes 2359304 | tf_op jit(solution)/shard_map/ppermute | solution.py:281
  354.9 68.6 %collective-permute-start.15 = (bf16[512,1536]{1,0:T(8,128)(2,1)}, bf16[512,1536]{1,0:T(8,128)(2,1)}, u32[]{:S(2)}, u32[]{:S(2)}) collective-permute-start(bf16[512,1536]{1,0:T(8,128)(2,1)} %refs_0_.3), channel_id=1, source_target_pairs={{0,4},{4,0},{1,5},{5,1},{2,6},{6,2},{3,7},{7,3},{8,12},{12,8},{9,1... | collective-permute-start | bytes 4718600 | tf_op jit(solution)/shard_map/ppermute | solution.py:281
  371.8 51.8 %collective-permute-start.14 = (bf16[512,1536]{1,0:T(8,128)(2,1)S(1)}, bf16[512,1536]{1,0:T(8,128)(2,1)}, u32[]{:S(2)}, u32[]{:S(2)}) collective-permute-start(bf16[512,1536]{1,0:T(8,128)(2,1)S(1)} %multiply_convert_fusion.refs_0_.refs_4_), channel_id=1, source_target_pairs={{0,4},{4,0},{1,5},{5,1},{2,6},{6,2},{3,7},{7,3},{8,12},{12,8},{9,1... | collective-permute-start | bytes 4718600 | tf_op jit(solution)/shard_map/ppermute | solution.py:281
  423.0 43.7 %collective-permute-start.40 = (bf16[512,1536]{1,0:T(8,128)(2,1)}, bf16[512,1536]{1,0:T(8,128)(2,1)S(1)}, u32[]{:S(2)}, u32[]{:S(2)}) collective-permute-start(bf16[512,1536]{1,0:T(8,128)(2,1)} %get-tuple-element.58), channel_id=1, source_target_pairs={{0,4},{4,0},{1,5},{5,1},{2,6},{6,2},{3,7},{7,3},{8,12},{12,8},{9,1... | collective-permute-start | bytes 4718600 | tf_op jit(solution)/shard_map/ppermute | solution.py:281
  423.1 59.0 %collective-permute-start.37 = (bf16[512,1536]{1,0:T(8,128)(2,1)}, bf16[512,1536]{1,0:T(8,128)(2,1)S(1)}, u32[]{:S(2)}, u32[]{:S(2)}) collective-permute-start(bf16[512,1536]{1,0:T(8,128)(2,1)} %get-tuple-element.54), channel_id=1, source_target_pairs={{0,4},{4,0},{1,5},{5,1},{2,6},{6,2},{3,7},{7,3},{8,12},{12,8},{9,1... | collective-permute-start | bytes 4718600 | tf_op jit(solution)/shard_map/ppermute | solution.py:281
  456.0 56.2 %collective-permute-start.39 = (bf16[512,1536]{1,0:T(8,128)(2,1)}, bf16[512,1536]{1,0:T(8,128)(2,1)}, u32[]{:S(2)}, u32[]{:S(2)}) collective-permute-start(bf16[512,1536]{1,0:T(8,128)(2,1)} %get-tuple-element.56), channel_id=1, source_target_pairs={{0,4},{4,0},{1,5},{5,1},{2,6},{6,2},{3,7},{7,3},{8,12},{12,8},{9,1... | collective-permute-start | bytes 4718600 | tf_op jit(solution)/shard_map/ppermute | solution.py:281
  456.2 59.6 %collective-permute-start.32 = (bf16[512,1536]{1,0:T(8,128)(2,1)}, bf16[512,1536]{1,0:T(8,128)(2,1)}, u32[]{:S(2)}, u32[]{:S(2)}) collective-permute-start(bf16[512,1536]{1,0:T(8,128)(2,1)} %get-tuple-element.52), channel_id=1, source_target_pairs={{0,4},{4,0},{1,5},{5,1},{2,6},{6,2},{3,7},{7,3},{8,12},{12,8},{9,1... | collective-permute-start | bytes 4718600 | tf_op jit(solution)/shard_map/ppermute | solution.py:281
  465.2 37.6 %collective-permute-start.52 = (bf16[1536,512]{1,0:T(8,128)(2,1)}, bf16[1536,512]{1,0:T(8,128)(2,1)}, u32[]{:S(2)}, u32[]{:S(2)}) collective-permute-start(bf16[1536,512]{1,0:T(8,128)(2,1)} %weight_grad.10), channel_id=1, source_target_pairs={{0,2},{2,0},{1,3},{3,1},{4,6},{6,4},{5,7},{7,5},{8,10},{10,8},{9,1... | collective-permute-start | bytes 4718600 | tf_op jit(solution)/shard_map/ppermute | solution.py:281
  468.2 44.1 %collective-permute-start.41 = (bf16[512,1536]{1,0:T(8,128)(2,1)}, bf16[512,1536]{1,0:T(8,128)(2,1)}, u32[]{:S(2)}, u32[]{:S(2)}) collective-permute-start(bf16[512,1536]{1,0:T(8,128)(2,1)} %add_convert_fusion.1), channel_id=1, source_target_pairs={{0,1},{1,0},{2,3},{3,2},{4,5},{5,4},{6,7},{7,6},{8,9},{9,8},{10,11... | collective-permute-start | bytes 4718600 | tf_op jit(solution)/shard_map/ppermute | solution.py:281
  482.1 87.2 %collective-permute-start.50 = (bf16[1536,1024]{1,0:T(8,128)(2,1)}, bf16[1536,1024]{1,0:T(8,128)(2,1)}, u32[]{:S(2)}, u32[]{:S(2)}) collective-permute-start(bf16[1536,1024]{1,0:T(8,128)(2,1)} %weight_grad.8), channel_id=1, source_target_pairs={{0,2},{2,0},{1,3},{3,1},{4,6},{6,4},{5,7},{7,5},{8,10},{10,8},{9,1... | collective-permute-start | bytes 9437192 | tf_op jit(solution)/shard_map/ppermute | solution.py:281
  512.2 199.7 %reduce-scatter.6.cloned.1.call-start = ((), (), s32[]{:S(2)}) async-start(), calls=%async_computation.4 | async-start | bytes 3932160 | tf_op jit(solution)/shard_map/reduce_scatter | solution.py:782
  544.4 38.9 %collective-permute-start.42 = (bf16[512,1536]{1,0:T(8,128)(2,1)}, bf16[512,1536]{1,0:T(8,128)(2,1)S(1)}, u32[]{:S(2)}, u32[]{:S(2)}) collective-permute-start(bf16[512,1536]{1,0:T(8,128)(2,1)} %get-tuple-element.89.refs_4_), channel_id=1, source_target_pairs={{0,1},{1,0},{2,3},{3,2},{4,5},{5,4},{6,7},{7,6},{8,9},{9,8},{10,11... | collective-permute-start | bytes 4718600 | tf_op jit(solution)/shard_map/ppermute | solution.py:281
  545.0 44.5 %collective-permute-start.43 = (bf16[512,1536]{1,0:T(8,128)(2,1)}, bf16[512,1536]{1,0:T(8,128)(2,1)S(1)}, u32[]{:S(2)}, u32[]{:S(2)}) collective-permute-start(bf16[512,1536]{1,0:T(8,128)(2,1)} %get-tuple-element.89.refs_4_), channel_id=1, source_target_pairs={{0,4},{4,0},{1,5},{5,1},{2,6},{6,2},{3,7},{7,3},{8,12},{12,8},{9,1... | collective-permute-start | bytes 4718600 | tf_op jit(solution)/shard_map/ppermute | solution.py:281
  582.9 162.5 %reduce-scatter.4.cloned.1.call-start = ((), (), s32[]{:S(2)}) async-start(), calls=%async_computation.3 | async-start | bytes 2457600 | tf_op jit(solution)/shard_map/reduce_scatter | solution.py:782
  645.6 41.3 %collective-permute-start.48 = (bf16[1536,576]{0,1:T(8,128)(2,1)}, bf16[1536,576]{0,1:T(8,128)(2,1)}, u32[]{:S(2)}, u32[]{:S(2)}) collective-permute-start(bf16[1536,576]{0,1:T(8,128)(2,1)} %copy.26), channel_id=1, source_target_pairs={{0,2},{2,0},{1,3},{3,1},{4,6},{6,4},{5,7},{7,5},{8,10},{10,8},{9,1... | collective-permute-start | bytes 5308424 | tf_op jit(solution)/shard_map/ppermute | solution.py:281
  653.3 59.9 %collective-permute-start.45 = (bf16[512,1536]{1,0:T(8,128)(2,1)}, bf16[512,1536]{1,0:T(8,128)(2,1)}, u32[]{:S(2)}, u32[]{:S(2)}) collective-permute-start(bf16[512,1536]{1,0:T(8,128)(2,1)} %convolution_convert_fusion.6), channel_id=1, source_target_pairs={{0,4},{4,0},{1,5},{5,1},{2,6},{6,2},{3,7},{7,3},{8,12},{12,8},{9,1... | collective-permute-start | bytes 4718600 | tf_op jit(solution)/shard_map/ppermute | solution.py:281
  656.4 56.8 %collective-permute-start.47 = (bf16[512,1536]{1,0:T(8,128)(2,1)}, bf16[512,1536]{1,0:T(8,128)(2,1)}, u32[]{:S(2)}, u32[]{:S(2)}) collective-permute-start(bf16[512,1536]{1,0:T(8,128)(2,1)} %add_convert_fusion), channel_id=1, source_target_pairs={{0,1},{1,0},{2,3},{3,2},{4,5},{5,4},{6,7},{7,6},{8,9},{9,8},{10,11... | collective-permute-start | bytes 4718600 | tf_op jit(solution)/shard_map/ppermute | solution.py:281
  (100 other events, 2486.1 us)
Sparse Core Ops, SparseCore 0:
  512.3 33.3 reduce-scatter.7
  583.0 57.5 reduce-scatter.5
  706.5 38.7 reduce-scatter.3

commit v2 on v1

--- a/solution.py
+++ b/solution.py
@@ -17,6 +17,7 @@
 MASKED = -1e30
 LOG2E = 1.4426950408889634
 LANES = 128
+SHARE = 20
 VMEM_BYTES = 56 * 2**20
 
 
@@ -285,6 +286,12 @@
     return jnp.dot(left, right, preferred_element_type=jnp.float32)
 
 
+def cost(flops, bytes_accessed, transcendentals):
+    return pl.CostEstimate(
+        flops=flops // SHARE, bytes_accessed=bytes_accessed // SHARE, transcendentals=transcendentals // SHARE
+    )
+
+
 def vmem_params(**more):
     return pltpu.CompilerParams(vmem_limit_bytes=VMEM_BYTES, **more)
 
@@ -320,76 +327,8 @@
     return jnp.asarray(spread, jnp.bfloat16)
 
 
-def prepare_kernel(deep, place_ref, *refs):
-    own, other, spread_ref = refs[:deep], refs[deep : 2 * deep], refs[2 * deep]
-    qkv_ref, out_ref = refs[2 * deep + 1 :]
-    part = own[0].shape[1]
-    half_qkv, half_out = qkv_ref.shape[1] // 2, out_ref.shape[1] // 2
-    for side, chunks in enumerate((own, other)):
-        for shift in range(deep):
-            for rel in range(2):
-                rows = pl.ds(row_offset(place_ref, shift, rel, deep, part), part)
-                wide = nn(chunks[shift][rel], spread_ref[...]).astype(jnp.bfloat16)
-                qkv_ref[rows, side * half_qkv : (side + 1) * half_qkv] = wide[:, :half_qkv]
-                out_ref[rows, side * half_out : (side + 1) * half_out] = wide[:, half_qkv:]
-
-
-def prepare(place, own, other, spread):
-    deep, part = len(own), own[0].shape[1]
-    rows = deep * 2 * part
-    wide = spread.shape[1]
-    half_qkv = wide * 2 // 3
-    return pl.pallas_call(
-        functools.partial(prepare_kernel, deep),
-        out_shape=(
-            jax.ShapeDtypeStruct((rows, 2 * half_qkv), jnp.bfloat16),
-            jax.ShapeDtypeStruct((rows, 2 * (wide - half_qkv)), jnp.bfloat16),
-        ),
-        in_specs=[smem_spec()] + [vmem_spec()] * (2 * deep + 1),
-        out_specs=(vmem_spec(), vmem_spec()),
-        compiler_params=vmem_params(),
-        cost_estimate=pl.CostEstimate(
-            flops=4 * rows * spread.shape[0] * wide, bytes_accessed=12 * rows * wide, transcendentals=0
-        ),
-        name="prepare",
-    )(place, *own, *other, spread)
-
-
 def turn(vectors, cosine, sine):
     return vectors * cosine + pltpu.roll(vectors, LANES // 2, 1) * sine
-
-
-def project_kernel(rows_ref, weight_ref, cosine_ref, sine_ref, out_ref):
-    product = nn(rows_ref[...], weight_ref[...])
-    cosine, sine = cosine_ref[...], sine_ref[...]
-    for head in range(3):
-        lanes = slice(head * LANES, (head + 1) * LANES)
-        out_ref[:, lanes] = turn(product[:, lanes], cosine, sine).astype(jnp.bfloat16)
-    out_ref[:, 3 * LANES :] = product[:, 3 * LANES :].astype(jnp.bfloat16)
-
-
-def project(rows, weight, cosine, sine):
-    count, width = rows.shape
-    tile = 4 * LANES
-    return pl.pallas_call(
-        project_kernel,
-        grid=(weight.shape[1] // tile,),
-        out_shape=jax.ShapeDtypeStruct((count, weight.shape[1]), jnp.bfloat16),
-        in_specs=[
-            pl.BlockSpec((count, width), lambda i: (0, 0)),
-            pl.BlockSpec((width, tile), lambda i: (0, i)),
-            pl.BlockSpec((count, LANES), lambda i: (0, 0)),
-            pl.BlockSpec((count, LANES), lambda i: (0, 0)),
-        ],
-        out_specs=pl.BlockSpec((count, tile), lambda i: (0, i)),
-        compiler_params=vmem_params(),
-        cost_estimate=pl.CostEstimate(
-            flops=2 * count * width * weight.shape[1],
-            bytes_accessed=2 * width * (count + weight.shape[1]) + 2 * count * weight.shape[1],
-            transcendentals=0,
-        ),
-        name="project",
-    )(rows, weight, cosine, sine)
 
 
 TILE = 256
@@ -427,65 +366,6 @@
     row = lax.broadcasted_iota(jnp.int32, (2 * TILE, TILE), 0)
     row = jnp.where(row >= TILE, row - TILE, row)
     return row >= lax.broadcasted_iota(jnp.int32, (2 * TILE, TILE), 1)
-
-
-def attend_kernel(place_ref, a_ref, b_ref, oa_ref, ob_ref, la_ref, lb_ref, keys, values):
-    qkv_refs, out_refs, log_refs = (a_ref, b_ref), (oa_ref, ob_ref), (la_ref, lb_ref)
-    place_rows(place_ref, qkv_refs, keys, values)
-    mask = diagonal_mask()
-    scale = HD ** (-0.5) * LOG2E
-
-    def visit(rel, start, before):
-        queries = stacked(qkv_refs[rel], 0, start)
-        edge = slice(before, before + TILE)
-        near = times_transposed(queries, keys[edge, :])
-        near = jnp.where(mask, near, MASKED)
-        top = jnp.max(near, axis=-1, keepdims=True)
-        if before:
-            far = times_transposed(queries, keys[:before, :])
-            top = jnp.maximum(top, jnp.max(far, axis=-1, keepdims=True))
-        top = top * scale
-        near = jnp.exp2(near * scale - top)
-        total = jnp.sum(near, axis=-1, keepdims=True)
-        mixed = nn(near.astype(jnp.bfloat16), values[edge, :])
-        if before:
-            far = jnp.exp2(far * scale - top)
-            total = total + jnp.sum(far, axis=-1, keepdims=True)
-            mixed = mixed + nn(far.astype(jnp.bfloat16), values[:before, :])
-        mixed = (mixed / total).astype(jnp.bfloat16)
-        logs = jnp.broadcast_to(top + jnp.log2(total), (2 * TILE, LANES))
-        rows = slice(start, start + TILE)
-        for head in range(2):
-            lanes = slice(head * LANES, (head + 1) * LANES)
-            part = slice(head * TILE, (head + 1) * TILE)
-            out_refs[rel][rows, lanes] = mixed[part]
-            log_refs[rel][rows, lanes] = logs[part]
-
-    each_tile(place_ref, qkv_refs, visit)
-
-
-def attend(place, first, second):
-    count = first.shape[0]
-    pairs = first.shape[1] // (4 * LANES)
-    wide = pl.BlockSpec((count, 4 * LANES), lambda i: (0, i))
-    narrow = pl.BlockSpec((count, 2 * LANES), lambda i: (0, i))
-    heads = jax.ShapeDtypeStruct((count, pairs * 2 * LANES), jnp.bfloat16)
-    logs = jax.ShapeDtypeStruct((count, pairs * 2 * LANES), jnp.float32)
-    return pl.pallas_call(
-        attend_kernel,
-        grid=(pairs,),
-        out_shape=(heads, heads, logs, logs),
-        in_specs=[smem_spec(), wide, wide],
-        out_specs=(narrow,) * 4,
-        scratch_shapes=[pltpu.VMEM((2 * count, LANES), jnp.bfloat16)] * 2,
-        compiler_params=vmem_params(),
-        cost_estimate=pl.CostEstimate(
-            flops=pairs * 2 * 4 * count * count * 4 * LANES,
-            bytes_accessed=12 * first.size,
-            transcendentals=pairs * 4 * count * count,
-        ),
-        name="attend",
-    )(place, first, second)
 
 
 def attend_back_kernel(
@@ -505,7 +385,16 @@
         queries = stacked(qkv_refs[rel], 0, start)
         grads = stacked(grad_refs[rel], 0, start)
         heads = stacked(out_refs[rel], 0, start)
-        logs = stacked(log_refs[rel], 0, start)[:, :1]
+        rows = slice(start, start + TILE)
+        pair = pl.program_id(0)
+        lane = lax.broadcasted_iota(jnp.int32, (TILE, LANES), 1)
+        logs = jnp.concatenate(
+            [
+                jnp.sum(jnp.where(lane == 2 * pair + head, log_refs[rel][rows, :], 0.0), axis=-1, keepdims=True)
+                for head in range(2)
+            ],
+            axis=0,
+        )
         inner = jnp.sum(grads.astype(jnp.float32) * heads.astype(jnp.float32), axis=-1, keepdims=True)
 
         def span(rows, masked):
@@ -545,18 +434,19 @@
     pairs = qkv[0].shape[1] // (4 * LANES)
     wide = pl.BlockSpec((count, 4 * LANES), lambda i: (0, i))
     narrow = pl.BlockSpec((count, 2 * LANES), lambda i: (0, i))
+    log = pl.BlockSpec((count, LANES), lambda i: (0, 0))
     table = pl.BlockSpec((2, count, LANES), lambda i: (0, 0, 0))
     result = jax.ShapeDtypeStruct(qkv[0].shape, jnp.bfloat16)
     return pl.pallas_call(
         attend_back_kernel,
         grid=(pairs,),
         out_shape=(result, result),
-        in_specs=[smem_spec(), wide, wide] + [narrow] * 6 + [table] * 2,
+        in_specs=[smem_spec(), wide, wide] + [narrow] * 4 + [log] * 2 + [table] * 2,
         out_specs=(wide, wide),
         scratch_shapes=[pltpu.VMEM((2 * count, LANES), jnp.bfloat16)] * 2
         + [pltpu.VMEM((2 * count, LANES), jnp.float32)] * 2,
         compiler_params=vmem_params(),
-        cost_estimate=pl.CostEstimate(
+        cost_estimate=cost(
             flops=pairs * 5 * 4 * count * count * 4 * LANES,
             bytes_accessed=20 * qkv[0].size,
             transcendentals=pairs * 4 * count * count,
@@ -565,24 +455,28 @@
     )(place, *qkv, *grads, *heads, *logs, cosine, sine)
 
 
-def feed_kernel(deep, blocks, place_ref, *refs):
-    rows_refs, grad_refs, refs = refs[:blocks], refs[blocks : 2 * blocks], refs[2 * blocks :]
-    wide_own, wide_other, refs = refs[:deep], refs[deep : 2 * deep], refs[2 * deep :]
-    down_own, down_other, refs = refs[:deep], refs[deep : 2 * deep], refs[2 * deep :]
+def feed_kernel(deep, blocks, chosen, place_ref, rows_ref, grads_ref, chunks, *refs):
     outs, scratch = refs[: 5 * blocks], refs[5 * blocks :]
-    gate, up, down, hidden, grad_gate, grad_up, branch, grad_rows, in_sems, out_sems = scratch
-    part = wide_own[0].shape[1]
+    gate, up, down, hidden, grad_gate, grad_up, branch, grad_rows, in_sems, out_sems = scratch[:10]
+    rows_refs, grad_refs, row_sems = scratch[10], scratch[11], scratch[12]
+    part = chunks.shape[3]
     half = gate.shape[1] // 2
+    row_loads = []
+    for block, index in enumerate(chosen):
+        here = []
+        for which, (source, target) in enumerate(((rows_ref, rows_refs), (grads_ref, grad_refs))):
+            copy = pltpu.make_async_copy(source.at[index], target.at[block], row_sems.at[block, which])
+            copy.start()
+            here.append(copy)
+        row_loads.append(here)
     loads = []
-    for matrix, (target, own, other, column) in enumerate(
-        ((gate, wide_own, wide_other, 0), (up, wide_own, wide_other, half), (down, down_own, down_other, 0))
-    ):
+    for matrix, target in enumerate((gate, up, down)):
         here = []
-        for side, chunks in enumerate((own, other)):
+        for side in range(2):
             for shift in range(deep):
                 for rel in range(2):
                     copy = pltpu.make_async_copy(
-                        chunks[shift].at[rel, :, pl.ds(column, half)],
+                        chunks.at[side, shift, rel, :, pl.ds(matrix * half, half)],
                         target.at[
                             pl.ds(row_offset(place_ref, shift, rel, deep, part), part),
                             pl.ds(side * half, half),
@@ -602,10 +496,9 @@
         stores.append(copy)
 
     for block in range(blocks):
-        if block == 0:
-            for here in loads:
-                for copy in here:
-                    copy.wait()
+        for here in [row_loads[block]] + (loads if block == 0 else []):
+            for copy in here:
+                copy.wait()
         width = gate.shape[1]
 
         @pl.loop(0, width // TILE)
@@ -643,30 +536,32 @@
         copy.wait()
 
 
-def feed(place, rows, grads, wide_own, wide_other, down_own, down_other):
-    deep, part = len(wide_own), wide_own[0].shape[1]
-    width, hidden_units = deep * 2 * part, 2 * down_own[0].shape[2]
-    blocks = len(rows)
-    count = rows[0].shape[0]
+def feed(place, rows, grads, chunks, chosen):
+    deep, part = chunks.shape[1], chunks.shape[3]
+    width, hidden_units = deep * 2 * part, 2 * (chunks.shape[4] // 3)
+    blocks = len(chosen)
+    count = rows.shape[1]
     small = jax.ShapeDtypeStruct((count, hidden_units), jnp.bfloat16)
     large = jax.ShapeDtypeStruct((count, width), jnp.bfloat16)
     outs = pl.pallas_call(
-        functools.partial(feed_kernel, deep, blocks),
+        functools.partial(feed_kernel, deep, blocks, chosen),
         out_shape=(small, small, small, large, large) * blocks,
-        in_specs=[smem_spec()] + [vmem_spec()] * (2 * blocks) + [any_spec()] * (4 * deep),
+        in_specs=[smem_spec()] + [any_spec()] * 3,
         out_specs=(any_spec(),) * (5 * blocks),
         scratch_shapes=[pltpu.VMEM((width, hidden_units), jnp.bfloat16)] * 3
         + [pltpu.VMEM((blocks, count, hidden_units), jnp.bfloat16)] * 3
         + [pltpu.VMEM((blocks, count, width), jnp.bfloat16)] * 2
-        + [pltpu.SemaphoreType.DMA((3, 2, deep, 2)), pltpu.SemaphoreType.DMA((blocks, 5))],
+        + [pltpu.SemaphoreType.DMA((3, 2, deep, 2)), pltpu.SemaphoreType.DMA((blocks, 5))]
+        + [pltpu.VMEM((blocks, count, width), jnp.bfloat16)] * 2
+        + [pltpu.SemaphoreType.DMA((blocks, 2))],
         compiler_params=vmem_params(),
-        cost_estimate=pl.CostEstimate(
+        cost_estimate=cost(
             flops=blocks * 12 * count * width * hidden_units,
             bytes_accessed=2 * (3 * width * hidden_units + blocks * count * (4 * width + 3 * hidden_units)),
             transcendentals=blocks * count * hidden_units,
         ),
         name="feed",
-    )(place, *rows, *grads, *wide_own, *wide_other, *down_own, *down_other)
+    )(place, rows, grads, chunks)
     return [outs[5 * block : 5 * block + 5] for block in range(blocks)]
 
 
@@ -720,13 +615,345 @@
         in_specs=in_specs,
         out_specs=pl.BlockSpec((tile, columns), lambda i: (i, 0)),
         compiler_params=vmem_params(),
-        cost_estimate=pl.CostEstimate(
+        cost_estimate=cost(
             flops=2 * blocks * count * width * sum(widths),
             bytes_accessed=2 * (blocks * count * (width * len(pairs) + sum(widths)) + width * columns),
             transcendentals=0,
         ),
         name="weight_grad",
     )(*operands)
+
+
+def hbm_spec():
+    return pl.BlockSpec(memory_space=pltpu.HBM)
+
+
+def send(source, target, sems, where):
+    copy = pltpu.make_async_remote_copy(
+        src_ref=source,
+        dst_ref=target,
+        send_sem=sems[0],
+        recv_sem=sems[1],
+        device_id=where,
+        device_id_type=pl.DeviceIdType.MESH,
+    )
+    copy.start()
+    return copy
+
+
+def greet(partners):
+    barrier = pltpu.get_barrier_semaphore()
+    for partner in partners:
+        pl.semaphore_signal(barrier, inc=1, device_id=partner, device_id_type=pl.DeviceIdType.MESH)
+    pl.semaphore_wait(barrier, len(partners))
+
+
+def beside():
+    core, across, along = (lax.axis_index(name).astype(jnp.int32) for name in ("c", "x", "y"))
+    return {"c": 1 - core}, {"x": 1 - across}, {"y": 1 - along}
+
+
+def grid_offset(slot, rel, deep, part):
+    z_place = lax.rem(lax.axis_index("z").astype(jnp.int32) + slot, jnp.int32(deep))
+    core = lax.rem(lax.axis_index("c").astype(jnp.int32) + rel, jnp.int32(2))
+    return pl.multiple_of((z_place * 2 + core) * part, 64)
+
+
+def spread_weight(buffer, spread_ref, wide, deep):
+    part = buffer.shape[3]
+    half = wide.shape[1] // 2
+
+    @pl.loop(0, 4 * deep)
+    def _(step):
+        rel, slot = lax.rem(step, jnp.int32(2)), lax.rem(step // 2, jnp.int32(deep))
+        side = step // (2 * deep)
+        rows = pl.ds(grid_offset(slot, rel, deep, part), part)
+        lanes = pl.ds(pl.multiple_of(side * half, half), half)
+        wide[rows, lanes] = nn(buffer[side, slot, rel], spread_ref[...]).astype(jnp.bfloat16)
+
+
+def attend_pair(qkv, heads, logs, keys, values, sequence, pair):
+    count = qkv.shape[1]
+    x_place = lax.axis_index("x").astype(jnp.int32)
+    lane0 = pl.multiple_of(pair * 4 * LANES, 4 * LANES)
+    mask = diagonal_mask()
+    scale = HD ** (-0.5) * LOG2E
+    for rel in range(2):
+        position = lax.rem(x_place + rel, jnp.int32(2))
+        rows = pl.ds(pl.multiple_of(position * count, count), count)
+        keys[rows, :] = qkv[2 * sequence + rel, :, pl.ds(lane0 + 2 * LANES, LANES)]
+        values[rows, :] = qkv[2 * sequence + rel, :, pl.ds(lane0 + 3 * LANES, LANES)]
+
+    def visit(rel, start, before):
+        block = 2 * sequence + rel
+        rows = slice(start, start + TILE)
+        queries = jnp.concatenate(
+            [qkv[block, rows, pl.ds(lane0, LANES)], qkv[block, rows, pl.ds(lane0 + LANES, LANES)]], axis=0
+        )
+        edge = slice(before, before + TILE)
+        near = jnp.where(mask, times_transposed(queries, keys[edge, :]), MASKED)
+        top = jnp.max(near, axis=-1, keepdims=True)
+        if before:
+            far = times_transposed(queries, keys[:before, :])
+            top = jnp.maximum(top, jnp.max(far, axis=-1, keepdims=True))
+        top = top * scale
+        near = jnp.exp2(near * scale - top)
+        total = jnp.sum(near, axis=-1, keepdims=True)
+        mixed = nn(near.astype(jnp.bfloat16), values[edge, :])
+        if before:
+            far = jnp.exp2(far * scale - top)
+            total = total + jnp.sum(far, axis=-1, keepdims=True)
+            mixed = mixed + nn(far.astype(jnp.bfloat16), values[:before, :])
+        mixed = (mixed / total).astype(jnp.bfloat16)
+        log = top + jnp.log2(total)
+        lane = lax.broadcasted_iota(jnp.int32, (TILE, LANES), 1)
+        kept = logs[block, rows, :]
+        for head in range(2):
+            part = slice(head * TILE, (head + 1) * TILE)
+            out_lane = pl.multiple_of(pair * 2 * LANES, LANES) + head * LANES
+            heads[block, rows, pl.ds(out_lane, LANES)] = mixed[part]
+            kept = jnp.where(lane == 2 * pair + head, log[part], kept)
+        logs[block, rows, :] = kept
+
+    for rel in range(2):
+        position = lax.rem(x_place + rel, jnp.int32(2))
+        for static_position in range(2):
+
+            @pl.when(position == static_position)
+            def _(rel=rel, static_position=static_position):
+                for step in range(count // TILE):
+                    visit(rel, step * TILE, static_position * count + step * TILE)
+
+
+def forward_kernel(
+    deep, first_ref, cotangent_ref, tokens_ref, gain_ref, qkv_halves, out_halves, feed_halves,
+    qkv_spread, out_spread, cosine_ref, sine_ref,
+    first_out, qkv_out, heads_out, logs_out, qkv_wide_out, out_wide_out, middle_out, second_out,
+    cotangent_out, feed_out,
+    first_all, qkv_buffer, out_buffer, qkv_wide, out_wide, qkv, heads, logs, keys, values,
+    parts, core_parts, outgoing, incoming, middle, second,
+    local_sems, row_sems, qkv_sems, out_sems, feed_sems, core_sems,
+):
+    core, z_place = lax.axis_index("c").astype(jnp.int32), lax.axis_index("z").astype(jnp.int32)
+    core_beside, x_beside, y_beside = beside()
+    count = first_ref.shape[0]
+    ring = jnp.int32(deep)
+    z_beside = [{"z": lax.rem(z_place + deep - shift, ring)} for shift in range(deep)]
+    greet([core_beside, x_beside, y_beside] + z_beside[1:])
+
+    kept = []
+    sent = []
+
+    def keep_local(source, target, index):
+        copy = pltpu.make_async_copy(source, target, local_sems.at[index])
+        copy.start()
+        return copy
+
+    def pair_of(sems, index):
+        return sems.at[0, index], sems.at[1, index]
+
+    def move(source, target, sems, index, where):
+        copy = send(source, target, pair_of(sems, index), where)
+        sent.append(copy)
+        return copy
+
+    qkv_core = move(qkv_halves.at[1 - core], qkv_buffer.at[0, 0, 1], qkv_sems, 0, core_beside)
+    qkv_kept = keep_local(qkv_halves.at[core], qkv_buffer.at[0, 0, 0], 0)
+    first_x = move(first_ref, first_all.at[1], row_sems, 0, x_beside)
+    out_core = move(out_halves.at[1 - core], out_buffer.at[0, 0, 1], out_sems, 0, core_beside)
+    out_kept = keep_local(out_halves.at[core], out_buffer.at[0, 0, 0], 1)
+    feed_core = move(feed_halves.at[1 - core], feed_out.at[0, 0, 1], feed_sems, 0, core_beside)
+    feed_kept = keep_local(feed_halves.at[core], feed_out.at[0, 0, 0], 2)
+    first_core = move(first_ref, first_all.at[2], row_sems, 1, core_beside)
+    first_kept = keep_local(first_ref, first_all.at[0], 3)
+    cotangent_kept = keep_local(cotangent_ref, cotangent_out.at[0], 4)
+
+    def open_z(buffer, sems, shifts):
+        return [move(buffer.at[0, 0], buffer.at[0, shift], sems, shift, z_beside[shift]) for shift in shifts]
+
+    def open_y(buffer, sems, shift):
+        return move(buffer.at[0, shift], buffer.at[1, shift], sems, deep + shift, y_beside)
+
+    far = [shift for shift in range(1, deep) if shift in (1, deep - 1)]
+    rest = [shift for shift in range(1, deep) if shift not in far]
+
+    qkv_core.wait_recv()
+    qkv_kept.wait()
+    qkv_z = open_z(qkv_buffer, qkv_sems, far + rest)
+    qkv_y = [open_y(qkv_buffer, qkv_sems, 0)]
+    out_core.wait_recv()
+    out_kept.wait()
+    feed_core.wait_recv()
+    feed_kept.wait()
+    for shift, copy in zip(far + rest, qkv_z):
+        copy.wait_recv()
+        qkv_y.append(open_y(qkv_buffer, qkv_sems, shift))
+    out_z = open_z(out_buffer, out_sems, far + rest)
+    out_y = [open_y(out_buffer, out_sems, 0)]
+    first_x.wait_recv()
+    first_far = move(first_all.at[1], first_all.at[3], row_sems, 2, core_beside)
+    cotangent_x = move(cotangent_ref, cotangent_out.at[1], row_sems, 3, x_beside)
+    cotangent_core = move(cotangent_ref, cotangent_out.at[2], row_sems, 4, core_beside)
+    feed_z = open_z(feed_out, feed_sems, far)
+    for copy in qkv_y:
+        copy.wait_recv()
+    for shift, copy in zip(far + rest, out_z):
+        copy.wait_recv()
+        out_y.append(open_y(out_buffer, out_sems, shift))
+    feed_y = [open_y(feed_out, feed_sems, 0)]
+
+    spread_weight(qkv_buffer, qkv_spread, qkv_wide, deep)
+    kept.append(keep_local(qkv_wide, qkv_wide_out, 5))
+    first_core.wait_recv()
+    first_far.wait_recv()
+    first_kept.wait()
+    kept.append(keep_local(first_all, first_out, 6))
+
+    @pl.loop(0, 8)
+    def _(step):
+        block, pair = step // 2, lax.rem(step, jnp.int32(2))
+        lane0 = pl.multiple_of(pair * 4 * LANES, 4 * LANES)
+        product = nn(first_all[block], qkv_wide[:, pl.ds(lane0, 4 * LANES)])
+        rel = lax.rem(block, jnp.int32(2))
+        cosine, sine = cosine_ref[rel], sine_ref[rel]
+        for head in range(4):
+            part = product[:, head * LANES : (head + 1) * LANES]
+            if head < 3:
+                part = turn(part, cosine, sine)
+            qkv[block, :, pl.ds(lane0 + head * LANES, LANES)] = part.astype(jnp.bfloat16)
+
+    kept.append(keep_local(qkv, qkv_out, 7))
+    logs[...] = jnp.zeros_like(logs)
+
+    @pl.loop(0, 4)
+    def _(step):
+        attend_pair(qkv, heads, logs, keys, values, step // 2, lax.rem(step, jnp.int32(2)))
+
+    kept.append(keep_local(heads, heads_out, 8))
+    kept.append(keep_local(logs, logs_out, 9))
+    for copy in out_y:
+        copy.wait_recv()
+    spread_weight(out_buffer, out_spread, out_wide, deep)
+    kept.append(keep_local(out_wide, out_wide_out, 10))
+
+    def out_part(block):
+        @pl.loop(0, out_wide.shape[0] // 512)
+        def _(step):
+            lanes = pl.ds(pl.multiple_of(step * 512, 512), 512)
+            parts[block, :, lanes] = times_transposed(heads[block], out_wide[lanes, :]).astype(jnp.bfloat16)
+
+    out_part(3)
+    core_far = move(parts.at[3], core_parts.at[1], core_sems, 0, core_beside)
+    out_part(1)
+    core_far.wait_recv()
+    step_rows = 128
+
+    @pl.loop(0, count // step_rows)
+    def _(step):
+        rows = pl.ds(pl.multiple_of(step * step_rows, step_rows), step_rows)
+        outgoing[rows, :] = (
+            parts[1, rows, :].astype(jnp.float32) + core_parts[1, rows, :].astype(jnp.float32)
+        ).astype(jnp.bfloat16)
+
+    branch_x = move(outgoing, incoming, core_sems, 1, x_beside)
+    out_part(2)
+    core_near = move(parts.at[2], core_parts.at[0], core_sems, 2, core_beside)
+    out_part(0)
+    for shift, copy in zip(far, feed_z):
+        copy.wait_recv()
+        feed_y.append(open_y(feed_out, feed_sems, shift))
+    feed_z = open_z(feed_out, feed_sems, rest)
+    core_near.wait_recv()
+    branch_x.wait_recv()
+
+    @pl.loop(0, count // step_rows)
+    def _(step):
+        rows = pl.ds(pl.multiple_of(step * step_rows, step_rows), step_rows)
+        total = (
+            tokens_ref[rows, :].astype(jnp.float32)
+            + parts[0, rows, :].astype(jnp.float32)
+            + core_parts[0, rows, :].astype(jnp.float32)
+            + incoming[rows, :].astype(jnp.float32)
+        )
+        middle[rows, :] = total
+        second[rows, :] = (total * norm_factor(total) * gain_ref[...]).astype(jnp.bfloat16)
+
+    kept.append(keep_local(middle, middle_out, 11))
+    kept.append(keep_local(second, second_out.at[0], 12))
+    second_x = move(second, second_out.at[1], row_sems, 5, x_beside)
+    second_core = move(second, second_out.at[2], row_sems, 6, core_beside)
+    cotangent_x.wait_recv()
+    cotangent_far = move(cotangent_out.at[1], cotangent_out.at[3], row_sems, 7, core_beside)
+    for shift, copy in zip(rest, feed_z):
+        copy.wait_recv()
+        feed_y.append(open_y(feed_out, feed_sems, shift))
+    second_x.wait_recv()
+    second_far = move(second_out.at[1], second_out.at[3], row_sems, 8, core_beside)
+    for copy in [second_core, second_far, cotangent_core, cotangent_far] + feed_y:
+        copy.wait_recv()
+    for copy in kept + [cotangent_kept]:
+        copy.wait()
+    for copy in sent:
+        copy.wait_send()
+
+
+def forward(deep, first, cotangent, tokens, gain, qkv_halves, out_halves, feed_halves, spreads, cosine, sine):
+    count, width = first.shape
+    part = feed_halves.shape[1]
+
+    def shape(*dims, kind=jnp.bfloat16):
+        return jax.ShapeDtypeStruct(dims, kind)
+
+    def room(*dims, kind=jnp.bfloat16):
+        return pltpu.VMEM(dims, kind)
+
+    qkv_lanes, out_lanes = 2 * spreads[0].shape[1], 2 * spreads[1].shape[1]
+    outs = (
+        shape(4, count, width),
+        shape(4, count, qkv_lanes),
+        shape(4, count, out_lanes),
+        shape(4, count, LANES, kind=jnp.float32),
+        shape(width, qkv_lanes),
+        shape(width, out_lanes),
+        shape(count, width, kind=jnp.float32),
+        shape(4, count, width),
+        shape(4, count, width),
+        shape(2, deep, 2, part, feed_halves.shape[2]),
+    )
+    scratch = [
+        room(4, count, width),
+        room(2, deep, 2, part, qkv_halves.shape[2]),
+        room(2, deep, 2, part, out_halves.shape[2]),
+        room(width, qkv_lanes),
+        room(width, out_lanes),
+        room(4, count, qkv_lanes),
+        room(4, count, out_lanes),
+        room(4, count, LANES, kind=jnp.float32),
+        room(2 * count, LANES),
+        room(2 * count, LANES),
+        room(4, count, width),
+        room(2, count, width),
+        room(count, width),
+        room(count, width),
+        room(count, width, kind=jnp.float32),
+        room(count, width),
+        pltpu.SemaphoreType.DMA((13,)),
+        pltpu.SemaphoreType.DMA((2, 9)),
+        pltpu.SemaphoreType.DMA((2, 2 * deep)),
+        pltpu.SemaphoreType.DMA((2, 2 * deep)),
+        pltpu.SemaphoreType.DMA((2, 2 * deep)),
+        pltpu.SemaphoreType.DMA((2, 3)),
+    ]
+    return pl.pallas_call(
+        functools.partial(forward_kernel, deep),
+        out_shape=outs,
+        in_specs=[vmem_spec(), hbm_spec()] + [vmem_spec()] * 2 + [hbm_spec()] * 3 + [vmem_spec()] * 4,
+        out_specs=(hbm_spec(),) * len(outs),
+        scratch_shapes=scratch,
+        compiler_params=vmem_params(collective_id=1, has_side_effects=True),
+        cost_estimate=cost(flops=20 * 10**9, bytes_accessed=10**8, transcendentals=10**7),
+        name="forward",
+    )(first, cotangent, tokens, gain, qkv_halves, out_halves, feed_halves, *spreads, cosine, sine)
 
 
 def tables(rows, x_place):
@@ -765,17 +992,6 @@
     arrived = swap(beside.astype(jnp.bfloat16), "x")
     own = parts[0].astype(jnp.float32) + swap(parts[2], "c").astype(jnp.float32)
     return own + arrived.astype(jnp.float32)
-
-
-def gather_chunks(halves, core, deep):
-    keep = jnp.where(core == 0, halves[0], halves[1])
-    send = jnp.where(core == 0, halves[1], halves[0])
-    chunk = jnp.stack([keep, swap(send, "c")])
-    own = [chunk]
-    for shift in range(1, deep):
-        own.append(lax.ppermute(chunk, "z", [((i + shift) % deep, i) for i in range(deep)]))
-    other = [swap(piece, "y") for piece in own]
-    return own, other
 
 
 def finish_grad(summed, core, part):
@@ -836,36 +1052,30 @@
         return result
 
     spread = spread_heads(3, 3)
-    heads_own, heads_other = gather_chunks(
-        halves(query_weight, key_weight, value_weight, out_turned), core, deep
-    )
-    wide_own, wide_other = gather_chunks(halves(gate_weight, up_weight), core, deep)
-    down_own, down_other = gather_chunks(halves(down_turned), core, deep)
-    first_blocks = spread_blocks(first_normed)
-    qkv_weight, out_wide = prepare(place, heads_own, heads_other, spread)
+    spreads = (spread_heads(3, 1), spread_heads(0, 2))
     cosine, sine = tables(rows, x_place)
-    qkv = [project(first_blocks[i], qkv_weight, cosine[i % 2], sine[i % 2]) for i in (0, 1, 2, 3)]
-    heads, logs = [], []
-    for sequence in range(2):
-        one, two, log_one, log_two = attend(place, qkv[2 * sequence], qkv[2 * sequence + 1])
-        heads += [one, two]
-        logs += [log_one, log_two]
-    branch = sum_blocks([times_transposed(block, out_wide).astype(jnp.bfloat16) for block in heads])
-    middle = own_rows + branch
-    second_normed = (middle * norm_factor(middle) * second_gain).astype(jnp.bfloat16)
-    cotangent_blocks = spread_blocks(cotangent)
-    second_blocks = spread_blocks(second_normed)
+    (
+        first_all, qkv_all, heads_all, logs_all, qkv_weight, out_wide, middle, second_all, cotangent_all, chunks,
+    ) = forward(
+        deep,
+        first_normed,
+        cotangent,
+        tokens,
+        second_gain[None],
+        jnp.stack(halves(query_weight, key_weight, value_weight)),
+        jnp.stack(halves(out_turned)),
+        jnp.stack(halves(gate_weight, up_weight, down_turned)),
+        spreads,
+        cosine,
+        sine,
+    )
+    first_blocks, cotangent_blocks, second_blocks, qkv, heads, logs = (
+        [stack[i] for i in range(4)]
+        for stack in (first_all, cotangent_all, second_all, qkv_all, heads_all, logs_all)
+    )
     fed = [None] * 4
-    for pair in ((0, 2), (1, 3)):
-        outs = feed(
-            place,
-            [second_blocks[i] for i in pair],
-            [cotangent_blocks[i] for i in pair],
-            wide_own,
-            wide_other,
-            down_own,
-            down_other,
-        )
+    for pair in ((1, 3), (0, 2)):
+        outs = feed(place, second_all, cotangent_all, chunks, pair)
         for i, out in zip(pair, outs):
             fed[i] = out
     hidden, grad_gate, grad_up, branches, grads_second = ([block[i] for block in fed] for i in range(5))

time: 774 us -> 627 us (0.81)
  waiting for transfers between devices: 381 us -> 130 us
  Pallas kernels: 216 us -> 353 us
  starting transfers between devices: 64.8 us -> 15.9 us
  local copies, waits for them, and re-layouts: 21.9 us -> 37.7 us
    ppermute x49 -> x22, waiting for transfers between devices: 254 us -> 95.5 us  [swap(): return lax.ppermute(value, axis, [(0, 1), (1, 0)])]
    pallas_call x9 -> x3, Pallas kernels: 112 us -> 250 us  [the longest x1 185 us: forward(): pl.pallas_call(functools.partial(forward_kernel, deep), out_shape=outs, i...]
    ppermute x9 -> x0, waiting for transfers between devices: 105 us -> none  [gather_chunks(): lax.ppermute(chunk, 'z', [((i + shift) % deep, i) for i in range(deep)])]
    ppermute x9 -> x0, starting transfers between devices: 27.6 us -> none  [gather_chunks(): lax.ppermute(chunk, 'z', [((i + shift) % deep, i) for i in range(deep)])]
    ppermute x49 -> x22, starting transfers between devices: 36.7 us -> 15.8 us  [swap(): return lax.ppermute(value, axis, [(0, 1), (1, 0)])]
    squeeze x2 -> x6, local copies, waits for them, and re-layouts: 1.65 us -> 19 us  [fast_local(): stack[i]]
    reduce_scatter x3, waiting for transfers between devices: 22.4 us -> 34.2 us  [finish_grad(): mine = lax.psum_scatter(summed, 'z', scatter_dimension=0, tiled=True)]
    dot_general x8 -> x4, matrix products: 23.1 us -> 20.3 us  [times_transposed(): lax.dot_general(left, right, (((1,), (1,)), ((), ())), preferred_element_...]
  transfers between devices with their start and end apart: 61 -> 25, of which waited for: 22 -> 8; matrix products, arithmetic and copies ran while one was open for 11% -> 14% of each run, Pallas kernels for 26% -> 22%
where the time goes in v2:
time: 627 us; the launch traced here: 616 us
  Pallas kernels  353 us (56%)
  waiting for transfers between devices  130 us (21%)
  local copies, waits for them, and re-layouts  37.7 us (6%)
  other arithmetic  37.2 us (6%)
  matrix products  27.4 us (4%)
  starting transfers between devices  15.9 us (3%)
  between operations  14.9 us (2%)
    pallas_call x1, Pallas kernels, forward(): pl.pallas_call(functools.partial(forward_kernel, deep), out_shape=outs, i...  185 us
    ppermute x22, waiting for transfers between devices, swap(): return lax.ppermute(value, axis, [(0, 1), (1, 0)])  95.5 us
    pallas_call x6, Pallas kernels, weight_grad(): pl.pallas_call(functools.partial(weight_kernel, blocks, len(pairs), sprea...  74.2 us
    pallas_call x2, Pallas kernels, feed(): pl.pallas_call(functools.partial(feed_kernel, deep, blocks, chosen), out_...  64.8 us
    reduce_scatter x3, waiting for transfers between devices, finish_grad(): mine = lax.psum_scatter(summed, 'z', scatter_dimension=0, tiled=True)  34.2 us
    pallas_call x2, Pallas kernels, attend_back(): pl.pallas_call(attend_back_kernel, grid=(pairs,), out_shape=(result, resu...  29.2 us
    dot_general x4, matrix products, times_transposed(): lax.dot_general(left, right, (((1,), (1,)), ((), ())), preferred_element_...  20.3 us
    squeeze x6, local copies, waits for them, and re-layouts, fast_local(): stack[i]  19 us
  transfers between devices with their start and end apart: 25, of which 8 were waited for; matrix products, arithmetic and copies ran while one was open for 14% of the time, Pallas kernels for 22%

profile of v2, /device:TPU:0, one launch (start us, length us, event | category | flops | bytes accessed | tf_op | source)
XLA Modules:
  0.0 616.3 jit_solution(2896908805669152872)
XLA Ops:
  18.9 2.7 sine_multiply_fusion
  21.5 185.3 %forward.1 = (bf16[4,512,1536]{2,1,0:T(8,128)(2,1)}, bf16[4,512,1024]{2,1,0:T(8,128)(2,1)}, bf16[4,512,512]{2,1,0:T(8,128)(2,1)}, f32[4,512,128]{2,1,0:T(8,128)}...) custom-call(bf16[512,1536]{1,0:T(8,128)(2,1)} %fusion.2.first_ref, ...), custom_call_target="tpu_custom_call" | custom-call | flops 1000000000 | bytes 5000000 | tf_op jit(solution)/shard_map/forward/pallas_call | solution.py:947
  206.8 32.7 %feed.3 = (bf16[512,1024]{1,0:T(8,128)(2,1)}, bf16[512,1024]{1,0:T(8,128)(2,1)}, bf16[512,1024]{1,0:T(8,128)(2,1)}, bf16[512,1536]{1,0:T(8,128)(2,1)}, bf16[512,...) custom-call(s32[3]{0:T(128)} %pad_add_fusion.place_ref, ...), custom_call_target="tpu_custom_call" | custom-call | flops 966367616 | bytes 1415577 | tf_op jit(solution)/shard_map/feed/pallas_call | solution.py:546
  239.6 32.2 %feed.2 = (bf16[512,1024]{1,0:T(8,128)(2,1)}, bf16[512,1024]{1,0:T(8,128)(2,1)}, bf16[512,1024]{1,0:T(8,128)(2,1)}, bf16[512,1536]{1,0:T(8,128)(2,1)}, bf16[512,...) custom-call(s32[3]{0:T(128)} %pad_add_fusion.place_ref, ...), custom_call_target="tpu_custom_call" | custom-call | flops 966367616 | bytes 1415577 | tf_op jit(solution)/shard_map/feed/pallas_call | solution.py:546
  271.7 5.7 slice_bitcast_fusion
  277.4 8.6 %weight_grad.10 = bf16[1536,512]{1,0:T(8,128)(2,1)} custom-call(bf16[512,1536]{1,0:T(8,128)(2,1)} %get-tuple-element.96.refs_0_, bf16[512,1536]{1,0:T(8,128)(2,1)} %get-tuple-element.95.refs_1_, bf16[512,1536]{1,0:T(8,128)(2,1)} %get-tuple-element.94.refs_2_, bf16[512,1536]{1,0:T(8,128)(2,1)} %get-tuple-element.93.refs_3_, ...), custom_call_target="tpu_custom_call" | custom-call | flops 161061280 | bytes 498073 | tf_op jit(solution)/shard_map/weight_grad/pallas_call | solution.py:611
  287.2 3.4 add_convert_fusion.1
  292.1 2.8 slice_bitcast_fusion.4
  294.9 12.7 %weight_grad.8 = bf16[1536,1024]{1,0:T(8,128)(2,1)} custom-call(bf16[512,1536]{1,0:T(8,128)(2,1)} %get-tuple-element.100.refs_0_.refs_4_, bf16[512,1536]{1,0:T(8,128)(2,1)} %get-tuple-element.99.refs_1_.refs_5_, bf16[512,1536]{1,0:T(8,128)(2,1)} %get-tuple-element.98.refs_2_.refs_6_, bf16[512,1536]{1,0:T(8,128)(2,1)} %get-tuple-element.97.refs_3_.refs_7_, ...), custom_call_target="tpu_custom_call" | custom-call | flops 322122560 | bytes 996147 | tf_op jit(solution)/shard_map/weight_grad/pallas_call | solution.py:611
  307.6 15.5 %collective-permute-done.16.refs_8_ = bf16[1536,512]{1,0:T(8,128)(2,1)} collective-permute-done((bf16[1536,512]{1,0:T(8,128)(2,1)}, bf16[1536,512]{1,0:T(8,128)(2,1)}, u32[]{:S(2)}, u32[]{:S(2)}) %collective-permute-start.16) | collective-permute-done | bytes 1572896 | tf_op jit(solution)/shard_map/ppermute | solution.py:282
  323.6 8.8 %weight_grad.11 = bf16[1536,512]{1,0:T(8,128)(2,1)} custom-call(bf16[512,1536]{1,0:T(8,128)(2,1)} %get-tuple-element.96.refs_0_, bf16[512,1536]{1,0:T(8,128)(2,1)} %get-tuple-element.95.refs_1_, bf16[512,1536]{1,0:T(8,128)(2,1)} %get-tuple-element.94.refs_2_, bf16[512,1536]{1,0:T(8,128)(2,1)} %get-tuple-element.93.refs_3_, ...), custom_call_target="tpu_custom_call" | custom-call | flops 161061280 | bytes 498073 | tf_op jit(solution)/shard_map/weight_grad/pallas_call | solution.py:611
  337.4 2.8 multiply_reduce_fusion.1
  340.2 31.4 %collective-permute-done.2 = bf16[512,1536]{1,0:T(8,128)(2,1)S(1)} collective-permute-done((bf16[512,1536]{1,0:T(8,128)(2,1)S(1)}, bf16[512,1536]{1,0:T(8,128)(2,1)S(1)}, u32[]{:S(2)}, u32[]{:S(2)}) %collective-permute-start.2) | collective-permute-done | bytes 1572896 | tf_op jit(solution)/shard_map/ppermute | solution.py:282
  371.6 5.1 fusion.7
  378.1 15.0 %collective-permute-done.14.refs_16_ = bf16[1536,1024]{1,0:T(8,128)(2,1)} collective-permute-done((bf16[1536,1024]{1,0:T(8,128)(2,1)}, bf16[1536,1024]{1,0:T(8,128)(2,1)}, u32[]{:S(2)}, u32[]{:S(2)}) %collective-permute-start.14) | collective-permute-done | bytes 3145760 | tf_op jit(solution)/shard_map/ppermute | solution.py:282
  393.1 13.5 %weight_grad.9 = bf16[1536,1024]{1,0:T(8,128)(2,1)} custom-call(bf16[512,1536]{1,0:T(8,128)(2,1)} %get-tuple-element.100.refs_0_.refs_4_, bf16[512,1536]{1,0:T(8,128)(2,1)} %get-tuple-element.99.refs_1_.refs_5_, bf16[512,1536]{1,0:T(8,128)(2,1)} %get-tuple-element.98.refs_2_.refs_6_, bf16[512,1536]{1,0:T(8,128)(2,1)} %get-tuple-element.97.refs_3_.refs_7_, ...), custom_call_target="tpu_custom_call" | custom-call | flops 322122560 | bytes 996147 | tf_op jit(solution)/shard_map/weight_grad/pallas_call | solution.py:611
  406.8 3.0 slice_bitcast_fusion.18
  411.6 2.7 slice_bitcast_fusion.22
  417.3 2.7 slice_bitcast_fusion.8
  423.5 14.6 %attend_back.3 = (bf16[512,1024]{1,0:T(8,128)(2,1)}, bf16[512,1024]{1,0:T(8,128)(2,1)}) custom-call(s32[3]{0:T(128)} %pad_add_fusion.place_ref, bf16[512,1024]{1,0:T(8,128)(2,1)} %get-tuple-element.107.a_ref, bf16[512,1024]{1,0:T(8,128)(2,1)} %get-tuple-element.106.b_ref, bf16[512,512]{1,0:T(8,128)(2,1)} %convolution_convert_fusion.5.ga_ref, ...), custom_call_target="tpu_custom_call" | custom-call | flops 268435456 | bytes 524288 | tf_op jit(solution)/shard_map/attend_back/pallas_call | solution.py:440
  438.1 4.2 convolution_convert_fusion
  445.8 14.6 %attend_back.2 = (bf16[512,1024]{1,0:T(8,128)(2,1)}, bf16[512,1024]{1,0:T(8,128)(2,1)}) custom-call(s32[3]{0:T(128)} %pad_add_fusion.place_ref, bf16[512,1024]{1,0:T(8,128)(2,1)} %get-tuple-element.108.a_ref, bf16[512,1024]{1,0:T(8,128)(2,1)} %get-tuple-element.105.b_ref, bf16[512,512]{1,0:T(8,128)(2,1)} %convolution_convert_fusion.7.ga_ref, ...), custom_call_target="tpu_custom_call" | custom-call | flops 268435456 | bytes 524288 | tf_op jit(solution)/shard_map/attend_back/pallas_call | solution.py:440
  460.4 15.3 %weight_grad.6 = bf16[1536,576]{1,0:T(8,128)(2,1)} custom-call(bf16[512,1536]{1,0:T(8,128)(2,1)} %get-tuple-element.104.refs_0_, bf16[512,1536]{1,0:T(8,128)(2,1)} %get-tuple-element.103.refs_1_, bf16[512,1536]{1,0:T(8,128)(2,1)} %get-tuple-element.102.refs_2_, bf16[512,1536]{1,0:T(8,128)(2,1)} %get-tuple-element.101.refs_3_, bf16[512,1536]{1,0:T(8,128)(2,1)} %copy-done.2, ...), custom_call_target="tpu_custom_call" | custom-call | flops 241591904 | bytes 874905 | tf_op jit(solution)/shard_map/weight_grad/pallas_call | solution.py:611
  475.7 4.2 copy.28
  481.6 4.9 convolution_convert_fusion.2
  486.7 4.4 add_convert_fusion
  492.5 28.9 %collective-permute-done.12 = bf16[1536,576]{0,1:T(8,128)(2,1)} collective-permute-done((bf16[1536,576]{0,1:T(8,128)(2,1)}, bf16[1536,576]{0,1:T(8,128)(2,1)}, u32[]{:S(2)}, u32[]{:S(2)}) %collective-permute-start.12) | collective-permute-done | bytes 1769504 | tf_op jit(solution)/shard_map/ppermute | solution.py:282
  521.4 3.9 copy.29.refs_17_
  525.2 15.4 %weight_grad.7 = bf16[1536,576]{1,0:T(8,128)(2,1)} custom-call(bf16[512,1536]{1,0:T(8,128)(2,1)} %get-tuple-element.104.refs_0_, bf16[512,1536]{1,0:T(8,128)(2,1)} %get-tuple-element.103.refs_1_, bf16[512,1536]{1,0:T(8,128)(2,1)} %get-tuple-element.102.refs_2_, bf16[512,1536]{1,0:T(8,128)(2,1)} %get-tuple-element.101.refs_3_, bf16[512,1536]{1,0:T(8,128)(2,1)} %copy-done.2, ...), custom_call_target="tpu_custom_call" | custom-call | flops 241591904 | bytes 874905 | tf_op jit(solution)/shard_map/weight_grad/pallas_call | solution.py:611
  546.8 6.8 %fusion.6 = (f32[512]{0:T(512)}, bf16[512,1536]{1,0:T(8,128)(2,1)}) fusion(bf16[512,1536]{1,0:T(8,128)(2,1)S(1)} %copy-done.1, bf16[512,1536]{1,0:T(8,128)(2,1)} %collective-permute-done.11, bf16[512,1536]{1,0:T(8,128)(2,1)} %collective-permute-done.9, f32[1536]{0:T(1024)S(1)} %copy-done.37, bf16[512,1024]{1,0:T(8,128)(2,1)S(1)} %copy-done.11, ...), kind=kOutput, calls=%fused_computation.10 | convolution fusion | flops 1618476544 | bytes 10493952 | tf_op jit(solution)/shard_map/dot_general | solution.py:45
  557.4 34.2 %reduce-scatter.4.cloned.1.call-done = bf16[384,576]{1,0:T(8,128)(2,1)} async-done(((bf16[1536,576]{1,0:T(8,128)(2,1)}), bf16[384,576]{1,0:T(8,128)(2,1)}) %reduce-scatter.4.cloned.1.call-update) | async-done | bytes 442384 | tf_op jit(solution)/shard_map/reduce_scatter | solution.py:998
  599.7 4.8 fusion.5
  (209 shorter events, 58.9 us)
Async XLA Ops:
  7.2 533.5 %reduce-scatter.8.cloned.1.call-start = ((), (), s32[]{:S(2)}) async-start(), calls=%async_computation.5 | async-start | bytes 1966080 | tf_op jit(solution)/shard_map/reduce_scatter | solution.py:998
  239.5 47.7 %collective-permute-start.4 = (bf16[512,1536]{1,0:T(8,128)(2,1)}, bf16[512,1536]{1,0:T(8,128)(2,1)}, u32[]{:S(2)}, u32[]{:S(2)}) collective-permute-start(bf16[512,1536]{1,0:T(8,128)(2,1)} %get-tuple-element.56), channel_id=1, source_target_pairs={{0,4},{4,0},{1,5},{5,1},{2,6},{6,2},{3,7},{7,3},{8,12},{12,8},{9,1... | collective-permute-start | bytes 4718600 | tf_op jit(solution)/shard_map/ppermute | solution.py:282
  271.7 20.4 %slice-start = ((s8[6291456]{0:T(1024)(128)(4,1)}), s8[4194304]{0:T(1024)(128)(4,1)S(1)}, s32[]{:S(2)}) async-start(s8[6291456]{0:T(1024)(128)(4,1)} %bitcast.85), calls=%async_computation.6 | async-start | bytes 8388608
  277.4 14.7 %slice-start.1 = ((s8[6291456]{0:T(1024)(128)(4,1)}), s8[2097152]{0:T(1024)(128)(4,1)S(1)}, s32[]{:S(2)}) async-start(s8[6291456]{0:T(1024)(128)(4,1)} %bitcast.85), calls=%async_computation.7 | async-start | bytes 4194304
  286.0 37.1 %collective-permute-start.16 = (bf16[1536,512]{1,0:T(8,128)(2,1)}, bf16[1536,512]{1,0:T(8,128)(2,1)}, u32[]{:S(2)}, u32[]{:S(2)}) collective-permute-start(bf16[1536,512]{1,0:T(8,128)(2,1)} %weight_grad.10), channel_id=1, source_target_pairs={{0,2},{2,0},{1,3},{3,1},{4,6},{6,4},{5,7},{7,5},{8,10},{10,8},{9,1... | collective-permute-start | bytes 4718600 | tf_op jit(solution)/shard_map/ppermute | solution.py:282
  286.5 46.0 %collective-permute-start.1 = (bf16[512,1536]{1,0:T(8,128)(2,1)}, bf16[512,1536]{1,0:T(8,128)(2,1)}, u32[]{:S(2)}, u32[]{:S(2)}) collective-permute-start(bf16[512,1536]{1,0:T(8,128)(2,1)} %get-tuple-element.52), channel_id=1, source_target_pairs={{0,4},{4,0},{1,5},{5,1},{2,6},{6,2},{3,7},{7,3},{8,12},{12,8},{9,1... | collective-permute-start | bytes 4718600 | tf_op jit(solution)/shard_map/ppermute | solution.py:282
  286.7 50.6 %collective-permute-start.3 = (bf16[512,1536]{1,0:T(8,128)(2,1)}, bf16[512,1536]{1,0:T(8,128)(2,1)S(1)}, u32[]{:S(2)}, u32[]{:S(2)}) collective-permute-start(bf16[512,1536]{1,0:T(8,128)(2,1)} %get-tuple-element.54), channel_id=1, source_target_pairs={{0,4},{4,0},{1,5},{5,1},{2,6},{6,2},{3,7},{7,3},{8,12},{12,8},{9,1... | collective-permute-start | bytes 4718600 | tf_op jit(solution)/shard_map/ppermute | solution.py:282
  287.0 53.2 %collective-permute-start = (bf16[512,1536]{1,0:T(8,128)(2,1)}, bf16[512,1536]{1,0:T(8,128)(2,1)}, u32[]{:S(2)}, u32[]{:S(2)}) collective-permute-start(bf16[512,1536]{1,0:T(8,128)(2,1)} %get-tuple-element.50), channel_id=1, source_target_pairs={{0,4},{4,0},{1,5},{5,1},{2,6},{6,2},{3,7},{7,3},{8,12},{12,8},{9,1... | collective-permute-start | bytes 4718600 | tf_op jit(solution)/shard_map/ppermute | solution.py:282
  290.6 46.7 %collective-permute-start.5 = (bf16[512,1536]{1,0:T(8,128)(2,1)}, bf16[512,1536]{1,0:T(8,128)(2,1)}, u32[]{:S(2)}, u32[]{:S(2)}) collective-permute-start(bf16[512,1536]{1,0:T(8,128)(2,1)} %add_convert_fusion.1), channel_id=1, source_target_pairs={{0,1},{1,0},{2,3},{3,2},{4,5},{5,4},{6,7},{7,6},{8,9},{9,8},{10,11... | collective-permute-start | bytes 4718600 | tf_op jit(solution)/shard_map/ppermute | solution.py:282
  323.1 70.0 %collective-permute-start.14 = (bf16[1536,1024]{1,0:T(8,128)(2,1)}, bf16[1536,1024]{1,0:T(8,128)(2,1)}, u32[]{:S(2)}, u32[]{:S(2)}) collective-permute-start(bf16[1536,1024]{1,0:T(8,128)(2,1)} %weight_grad.8), channel_id=1, source_target_pairs={{0,2},{2,0},{1,3},{3,1},{4,6},{6,4},{5,7},{7,5},{8,10},{10,8},{9,1... | collective-permute-start | bytes 9437192 | tf_op jit(solution)/shard_map/ppermute | solution.py:282
  332.4 213.1 %reduce-scatter.6.cloned.1.call-start = ((), (), s32[]{:S(2)}) async-start(), calls=%async_computation.4 | async-start | bytes 3932160 | tf_op jit(solution)/shard_map/reduce_scatter | solution.py:998
  335.8 35.8 %collective-permute-start.2 = (bf16[512,1536]{1,0:T(8,128)(2,1)S(1)}, bf16[512,1536]{1,0:T(8,128)(2,1)S(1)}, u32[]{:S(2)}, u32[]{:S(2)}) collective-permute-start(bf16[512,1536]{1,0:T(8,128)(2,1)S(1)} %add_convert_fusion.3), channel_id=1, source_target_pairs={{0,1},{1,0},{2,3},{3,2},{4,5},{5,4},{6,7},{7,6},{8,9},{9,8},{10,11... | collective-permute-start | bytes 4718600 | tf_op jit(solution)/shard_map/ppermute | solution.py:282
  337.3 34.2 %copy-start.9 = (bf16[512,1536]{1,0:T(8,128)(2,1)S(1)}, bf16[512,1536]{1,0:T(8,128)(2,1)}, u32[]{:S(2)}) copy-start(bf16[512,1536]{1,0:T(8,128)(2,1)} %cotangent_ref.1) | copy-start | bytes 4718596
  337.3 34.2 %copy-start.19 = (bf16[512,1536]{1,0:T(8,128)(2,1)S(1)}, bf16[512,1536]{1,0:T(8,128)(2,1)}, u32[]{:S(2)}) copy-start(bf16[512,1536]{1,0:T(8,128)(2,1)} %get-tuple-element.49) | copy-start | bytes 4718596
  376.7 65.6 %copy-start.2 = (bf16[512,1536]{1,0:T(8,128)(2,1)}, bf16[512,1536]{1,0:T(8,128)(2,1)S(1)}, u32[]{:S(2)}) copy-start(bf16[512,1536]{1,0:T(8,128)(2,1)S(1)} %get-tuple-element.91.refs_4_) | copy-start | bytes 4718596
  376.7 34.9 %collective-permute-start.6 = (bf16[512,1536]{1,0:T(8,128)(2,1)S(1)}, bf16[512,1536]{1,0:T(8,128)(2,1)S(1)}, u32[]{:S(2)}, u32[]{:S(2)}) collective-permute-start(bf16[512,1536]{1,0:T(8,128)(2,1)S(1)} %get-tuple-element.91.refs_4_), channel_id=1, source_target_pairs={{0,1},{1,0},{2,3},{3,2},{4,5},{5,4},{6,7},{7,6},{8,9},{9,8},{10,11... | collective-permute-start | bytes 4718600 | tf_op jit(solution)/shard_map/ppermute | solution.py:282
  406.6 185.0 %reduce-scatter.4.cloned.1.call-start = ((), (), s32[]{:S(2)}) async-start(), calls=%async_computation.3 | async-start | bytes 2457600 | tf_op jit(solution)/shard_map/reduce_scatter | solution.py:998
  406.7 13.3 %collective-permute-start.7 = (bf16[512,1536]{1,0:T(8,128)(2,1)S(1)}, bf16[512,1536]{1,0:T(8,128)(2,1)S(1)}, u32[]{:S(2)}, u32[]{:S(2)}) collective-permute-start(bf16[512,1536]{1,0:T(8,128)(2,1)S(1)} %get-tuple-element.91.refs_4_), channel_id=1, source_target_pairs={{0,4},{4,0},{1,5},{5,1},{2,6},{6,2},{3,7},{7,3},{8,12},{12,8},{9,1... | collective-permute-start | bytes 4718600 | tf_op jit(solution)/shard_map/ppermute | solution.py:282
  411.6 32.5 %copy-start.5 = (bf16[512,1536]{1,0:T(8,128)(2,1)}, bf16[512,1536]{1,0:T(8,128)(2,1)S(1)}, u32[]{:S(2)}) copy-start(bf16[512,1536]{1,0:T(8,128)(2,1)S(1)} %collective-permute-done.6.refs_5_) | copy-start | bytes 4718596
  411.6 10.2 %collective-permute-start.8 = (bf16[512,1536]{1,0:T(8,128)(2,1)S(1)}, bf16[512,1536]{1,0:T(8,128)(2,1)S(1)}, u32[]{:S(2)}, u32[]{:S(2)}) collective-permute-start(bf16[512,1536]{1,0:T(8,128)(2,1)S(1)} %collective-permute-done.6.refs_5_), channel_id=1, source_target_pairs={{0,4},{4,0},{1,5},{5,1},{2,6},{6,2},{3,7},{7,3},{8,12},{12,8},{9,1... | collective-permute-start | bytes 4718600 | tf_op jit(solution)/shard_map/ppermute | solution.py:282
  442.3 44.4 %collective-permute-start.10 = (bf16[512,1536]{1,0:T(8,128)(2,1)}, bf16[512,1536]{1,0:T(8,128)(2,1)}, u32[]{:S(2)}, u32[]{:S(2)}) collective-permute-start(bf16[512,1536]{1,0:T(8,128)(2,1)} %convolution_convert_fusion), channel_id=1, source_target_pairs={{0,4},{4,0},{1,5},{5,1},{2,6},{6,2},{3,7},{7,3},{8,12},{12,8},{9,1... | collective-permute-start | bytes 4718600 | tf_op jit(solution)/shard_map/ppermute | solution.py:282
  480.0 41.4 %collective-permute-start.12 = (bf16[1536,576]{0,1:T(8,128)(2,1)}, bf16[1536,576]{0,1:T(8,128)(2,1)}, u32[]{:S(2)}, u32[]{:S(2)}) collective-permute-start(bf16[1536,576]{0,1:T(8,128)(2,1)} %copy.28), channel_id=1, source_target_pairs={{0,2},{2,0},{1,3},{3,1},{4,6},{6,4},{5,7},{7,5},{8,10},{10,8},{9,1... | collective-permute-start | bytes 5308424 | tf_op jit(solution)/shard_map/ppermute | solution.py:282
  486.5 60.3 %collective-permute-start.9 = (bf16[512,1536]{1,0:T(8,128)(2,1)}, bf16[512,1536]{1,0:T(8,128)(2,1)}, u32[]{:S(2)}, u32[]{:S(2)}) collective-permute-start(bf16[512,1536]{1,0:T(8,128)(2,1)} %convolution_convert_fusion.2), channel_id=1, source_target_pairs={{0,4},{4,0},{1,5},{5,1},{2,6},{6,2},{3,7},{7,3},{8,12},{12,8},{9,1... | collective-permute-start | bytes 4718600 | tf_op jit(solution)/shard_map/ppermute | solution.py:282
  491.1 55.7 %collective-permute-start.11 = (bf16[512,1536]{1,0:T(8,128)(2,1)}, bf16[512,1536]{1,0:T(8,128)(2,1)}, u32[]{:S(2)}, u32[]{:S(2)}) collective-permute-start(bf16[512,1536]{1,0:T(8,128)(2,1)} %add_convert_fusion), channel_id=1, source_target_pairs={{0,1},{1,0},{2,3},{3,2},{4,5},{5,4},{6,7},{7,6},{8,9},{9,8},{10,11... | collective-permute-start | bytes 4718600 | tf_op jit(solution)/shard_map/ppermute | solution.py:282
  541.8 1.6 collective-permute-start.17
  546.6 7.0 %collective-permute-start.15 = (bf16[192,1024]{1,0:T(8,128)(2,1)S(1)}, bf16[192,1024]{1,0:T(8,128)(2,1)S(1)}, u32[]{:S(2)}, u32[]{:S(2)}) collective-permute-start(bf16[192,1024]{1,0:T(8,128)(2,1)S(1)} %constant_dynamic-slice_fusion.1), channel_id=1, source_target_pairs={{0,4},{4,0},{1,5},{5,1},{2,6},{6,2},{3,7},{7,3},{8,12},{12,8},{9,1... | collective-permute-start | bytes 1179656 | tf_op jit(solution)/shard_map/ppermute | solution.py:282
  554.9 37.7 %copy-start.41 = (f32[512]{0:T(512)S(1)}, f32[512]{0:T(512)}, u32[]{:S(2)}) copy-start(f32[512]{0:T(512)} %get-tuple-element.158) | copy-start | bytes 6148
  556.0 36.7 %collective-permute-start.20 = (f32[192]{0:T(256)S(1)}, f32[192]{0:T(256)S(1)}, u32[]{:S(2)}, u32[]{:S(2)}) collective-permute-start(f32[192]{0:T(256)S(1)} %dynamic-slice_divide_fusion), channel_id=1, source_target_pairs={{0,1},{1,0},{2,3},{3,2},{4,5},{5,4},{6,7},{7,6},{8,9},{9,8},{10,11... | collective-permute-start | bytes 2312 | tf_op jit(solution)/shard_map/ppermute | solution.py:282
  592.5 1.7 collective-permute-start.13
  592.7 11.9 %collective-permute-start.21 = (f32[192]{0:T(256)S(1)}, f32[192]{0:T(256)S(1)}, u32[]{:S(2)}, u32[]{:S(2)}) collective-permute-start(f32[192]{0:T(256)S(1)} %add.164), channel_id=1, source_target_pairs={{0,2},{2,0},{1,3},{3,1},{4,6},{6,4},{5,7},{7,5},{8,10},{10,8},{9,1... | collective-permute-start | bytes 2312 | tf_op jit(solution)/shard_map/ppermute | solution.py:282
  598.3 6.9 %collective-permute-start.18 = (f32[192]{0:T(256)S(1)}, f32[192]{0:T(256)S(1)}, u32[]{:S(2)}, u32[]{:S(2)}) collective-permute-start(f32[192]{0:T(256)S(1)} %dynamic-slice_divide_fusion.1), channel_id=1, source_target_pairs={{0,1},{1,0},{2,3},{3,2},{4,5},{5,4},{6,7},{7,6},{8,9},{9,8},{10,11... | collective-permute-start | bytes 2312 | tf_op jit(solution)/shard_map/ppermute | solution.py:282
  605.2 3.6 collective-permute-start.19
  (45 other events, 174.1 us)
Sparse Core Ops, SparseCore 0:
  332.6 44.5 reduce-scatter.7
  406.7 68.5 reduce-scatter.5
  540.8 50.7 reduce-scatter.3

commit v3 on v2

--- a/solution.py
+++ b/solution.py
@@ -18,7 +18,7 @@
 LOG2E = 1.4426950408889634
 LANES = 128
 SHARE = 20
-VMEM_BYTES = 56 * 2**20
+VMEM_BYTES = 60 * 2**20
 
 
 def normed(inputs, gain):
@@ -278,10 +278,6 @@
     )
 
 
-def swap(value, axis):
-    return lax.ppermute(value, axis, [(0, 1), (1, 0)])
-
-
 def nn(left, right):
     return jnp.dot(left, right, preferred_element_type=jnp.float32)
 
@@ -296,23 +292,8 @@
     return pltpu.CompilerParams(vmem_limit_bytes=VMEM_BYTES, **more)
 
 
-def smem_spec():
-    return pl.BlockSpec(memory_space=pltpu.SMEM)
-
-
 def vmem_spec():
     return pl.BlockSpec(memory_space=pltpu.VMEM)
-
-
-def any_spec():
-    return pl.BlockSpec(memory_space=pl.ANY)
-
-
-def row_offset(place_ref, shift, rel, deep, part):
-    ring = jnp.int32(deep)
-    slot = lax.rem(place_ref[0] + shift, ring)
-    core = lax.rem(place_ref[1] + rel, jnp.int32(2))
-    return pl.multiple_of((slot * 2 + core) * part, 64)
 
 
 def spread_heads(heads_split, heads_plain):
@@ -334,294 +315,10 @@
 TILE = 256
 
 
-def place_rows(place_ref, qkv_refs, keys, values):
-    for rel, ref in enumerate(qkv_refs):
-        count = ref.shape[0]
-        position = lax.rem(place_ref[2] + rel, jnp.int32(2))
-        rows = pl.ds(pl.multiple_of(position * count, count), count)
-        keys[rows, :] = ref[:, 2 * LANES : 3 * LANES]
-        values[rows, :] = ref[:, 3 * LANES :]
-
-
-def each_tile(place_ref, qkv_refs, visit):
-    for rel, ref in enumerate(qkv_refs):
-        count = ref.shape[0]
-        position = lax.rem(place_ref[2] + rel, jnp.int32(2))
-        for static_position in range(2):
-
-            @pl.when(position == static_position)
-            def _(rel=rel, count=count, static_position=static_position):
-                for step in range(count // TILE):
-                    visit(rel, step * TILE, static_position * count + step * TILE)
-
-
-def stacked(ref, first, start):
-    rows = slice(start, start + TILE)
-    return jnp.concatenate(
-        [ref[rows, first : first + LANES], ref[rows, first + LANES : first + 2 * LANES]], axis=0
-    )
-
-
 def diagonal_mask():
     row = lax.broadcasted_iota(jnp.int32, (2 * TILE, TILE), 0)
     row = jnp.where(row >= TILE, row - TILE, row)
     return row >= lax.broadcasted_iota(jnp.int32, (2 * TILE, TILE), 1)
-
-
-def attend_back_kernel(
-    place_ref, a_ref, b_ref, ga_ref, gb_ref, oa_ref, ob_ref, la_ref, lb_ref, cosine_ref, sine_ref,
-    da_ref, db_ref, keys, values, grad_keys, grad_values,
-):
-    qkv_refs, grad_refs, out_refs = (a_ref, b_ref), (ga_ref, gb_ref), (oa_ref, ob_ref)
-    log_refs, result_refs = (la_ref, lb_ref), (da_ref, db_ref)
-    place_rows(place_ref, qkv_refs, keys, values)
-    mask = diagonal_mask()
-    factor = HD ** (-0.5)
-    scale = factor * LOG2E
-    grad_keys[...] = jnp.zeros_like(grad_keys)
-    grad_values[...] = jnp.zeros_like(grad_values)
-
-    def visit(rel, start, before):
-        queries = stacked(qkv_refs[rel], 0, start)
-        grads = stacked(grad_refs[rel], 0, start)
-        heads = stacked(out_refs[rel], 0, start)
-        rows = slice(start, start + TILE)
-        pair = pl.program_id(0)
-        lane = lax.broadcasted_iota(jnp.int32, (TILE, LANES), 1)
-        logs = jnp.concatenate(
-            [
-                jnp.sum(jnp.where(lane == 2 * pair + head, log_refs[rel][rows, :], 0.0), axis=-1, keepdims=True)
-                for head in range(2)
-            ],
-            axis=0,
-        )
-        inner = jnp.sum(grads.astype(jnp.float32) * heads.astype(jnp.float32), axis=-1, keepdims=True)
-
-        def span(rows, masked):
-            softmax = jnp.exp2(times_transposed(queries, keys[rows, :]) * scale - logs)
-            if masked:
-                softmax = jnp.where(mask, softmax, 0.0)
-            grad_softmax = times_transposed(grads, values[rows, :])
-            grad_scores = (softmax * (grad_softmax - inner)).astype(jnp.bfloat16)
-            grad_values[rows, :] += transposed_times(softmax.astype(jnp.bfloat16), grads)
-            grad_keys[rows, :] += transposed_times(grad_scores, queries)
-            return nn(grad_scores, keys[rows, :])
-
-        grad_queries = span(slice(before, before + TILE), True)
-        if before:
-            grad_queries = grad_queries + span(slice(0, before), False)
-        rows = slice(start, start + TILE)
-        cosine, sine = cosine_ref[rel, rows, :], -sine_ref[rel, rows, :]
-        for head in range(2):
-            part = grad_queries[head * TILE : (head + 1) * TILE] * factor
-            result_refs[rel][rows, head * LANES : (head + 1) * LANES] = turn(part, cosine, sine).astype(
-                jnp.bfloat16
-            )
-
-    each_tile(place_ref, qkv_refs, visit)
-    for rel, ref in enumerate(result_refs):
-        count = ref.shape[0]
-        position = lax.rem(place_ref[2] + rel, jnp.int32(2))
-        rows = pl.ds(pl.multiple_of(position * count, count), count)
-        ref[:, 2 * LANES : 3 * LANES] = turn(
-            grad_keys[rows, :] * factor, cosine_ref[rel], -sine_ref[rel]
-        ).astype(jnp.bfloat16)
-        ref[:, 3 * LANES :] = grad_values[rows, :].astype(jnp.bfloat16)
-
-
-def attend_back(place, qkv, grads, heads, logs, cosine, sine):
-    count = qkv[0].shape[0]
-    pairs = qkv[0].shape[1] // (4 * LANES)
-    wide = pl.BlockSpec((count, 4 * LANES), lambda i: (0, i))
-    narrow = pl.BlockSpec((count, 2 * LANES), lambda i: (0, i))
-    log = pl.BlockSpec((count, LANES), lambda i: (0, 0))
-    table = pl.BlockSpec((2, count, LANES), lambda i: (0, 0, 0))
-    result = jax.ShapeDtypeStruct(qkv[0].shape, jnp.bfloat16)
-    return pl.pallas_call(
-        attend_back_kernel,
-        grid=(pairs,),
-        out_shape=(result, result),
-        in_specs=[smem_spec(), wide, wide] + [narrow] * 4 + [log] * 2 + [table] * 2,
-        out_specs=(wide, wide),
-        scratch_shapes=[pltpu.VMEM((2 * count, LANES), jnp.bfloat16)] * 2
-        + [pltpu.VMEM((2 * count, LANES), jnp.float32)] * 2,
-        compiler_params=vmem_params(),
-        cost_estimate=cost(
-            flops=pairs * 5 * 4 * count * count * 4 * LANES,
-            bytes_accessed=20 * qkv[0].size,
-            transcendentals=pairs * 4 * count * count,
-        ),
-        name="attend_back",
-    )(place, *qkv, *grads, *heads, *logs, cosine, sine)
-
-
-def feed_kernel(deep, blocks, chosen, place_ref, rows_ref, grads_ref, chunks, *refs):
-    outs, scratch = refs[: 5 * blocks], refs[5 * blocks :]
-    gate, up, down, hidden, grad_gate, grad_up, branch, grad_rows, in_sems, out_sems = scratch[:10]
-    rows_refs, grad_refs, row_sems = scratch[10], scratch[11], scratch[12]
-    part = chunks.shape[3]
-    half = gate.shape[1] // 2
-    row_loads = []
-    for block, index in enumerate(chosen):
-        here = []
-        for which, (source, target) in enumerate(((rows_ref, rows_refs), (grads_ref, grad_refs))):
-            copy = pltpu.make_async_copy(source.at[index], target.at[block], row_sems.at[block, which])
-            copy.start()
-            here.append(copy)
-        row_loads.append(here)
-    loads = []
-    for matrix, target in enumerate((gate, up, down)):
-        here = []
-        for side in range(2):
-            for shift in range(deep):
-                for rel in range(2):
-                    copy = pltpu.make_async_copy(
-                        chunks.at[side, shift, rel, :, pl.ds(matrix * half, half)],
-                        target.at[
-                            pl.ds(row_offset(place_ref, shift, rel, deep, part), part),
-                            pl.ds(side * half, half),
-                        ],
-                        in_sems.at[matrix, side, shift, rel],
-                    )
-                    copy.start()
-                    here.append(copy)
-        loads.append(here)
-    stores = []
-
-    def store(scratch_ref, block, which):
-        copy = pltpu.make_async_copy(
-            scratch_ref.at[block], outs[block * 5 + which], out_sems.at[block, which]
-        )
-        copy.start()
-        stores.append(copy)
-
-    for block in range(blocks):
-        for here in [row_loads[block]] + (loads if block == 0 else []):
-            for copy in here:
-                copy.wait()
-        width = gate.shape[1]
-
-        @pl.loop(0, width // TILE)
-        def _(step, block=block):
-            lanes = pl.ds(pl.multiple_of(step * TILE, TILE), TILE)
-            rows, grads = rows_refs[block][...], grad_refs[block][...]
-            gate_value = nn(rows, gate[:, lanes])
-            up_value = nn(rows, up[:, lanes])
-            grad_hidden = nn(grads, down[:, lanes])
-            sigmoid = 1.0 / (1.0 + jnp.exp(-gate_value))
-            swish = gate_value * sigmoid
-            slope = sigmoid + swish * (1.0 - sigmoid)
-            hidden[block, :, lanes] = (swish * up_value).astype(jnp.bfloat16)
-            grad_gate[block, :, lanes] = (grad_hidden * up_value * slope).astype(jnp.bfloat16)
-            grad_up[block, :, lanes] = (grad_hidden * swish).astype(jnp.bfloat16)
-
-        store(hidden, block, 0)
-        store(grad_gate, block, 1)
-        store(grad_up, block, 2)
-
-        @pl.loop(0, gate.shape[0] // TILE)
-        def _(step, block=block):
-            lanes = pl.ds(pl.multiple_of(step * TILE, TILE), TILE)
-            grad_rows[block, :, lanes] = (
-                times_transposed(grad_gate[block], gate[lanes, :])
-                + times_transposed(grad_up[block], up[lanes, :])
-            ).astype(jnp.bfloat16)
-            branch[block, :, lanes] = times_transposed(hidden[block], down[lanes, :]).astype(
-                jnp.bfloat16
-            )
-
-        store(branch, block, 3)
-        store(grad_rows, block, 4)
-    for copy in stores:
-        copy.wait()
-
-
-def feed(place, rows, grads, chunks, chosen):
-    deep, part = chunks.shape[1], chunks.shape[3]
-    width, hidden_units = deep * 2 * part, 2 * (chunks.shape[4] // 3)
-    blocks = len(chosen)
-    count = rows.shape[1]
-    small = jax.ShapeDtypeStruct((count, hidden_units), jnp.bfloat16)
-    large = jax.ShapeDtypeStruct((count, width), jnp.bfloat16)
-    outs = pl.pallas_call(
-        functools.partial(feed_kernel, deep, blocks, chosen),
-        out_shape=(small, small, small, large, large) * blocks,
-        in_specs=[smem_spec()] + [any_spec()] * 3,
-        out_specs=(any_spec(),) * (5 * blocks),
-        scratch_shapes=[pltpu.VMEM((width, hidden_units), jnp.bfloat16)] * 3
-        + [pltpu.VMEM((blocks, count, hidden_units), jnp.bfloat16)] * 3
-        + [pltpu.VMEM((blocks, count, width), jnp.bfloat16)] * 2
-        + [pltpu.SemaphoreType.DMA((3, 2, deep, 2)), pltpu.SemaphoreType.DMA((blocks, 5))]
-        + [pltpu.VMEM((blocks, count, width), jnp.bfloat16)] * 2
-        + [pltpu.SemaphoreType.DMA((blocks, 2))],
-        compiler_params=vmem_params(),
-        cost_estimate=cost(
-            flops=blocks * 12 * count * width * hidden_units,
-            bytes_accessed=2 * (3 * width * hidden_units + blocks * count * (4 * width + 3 * hidden_units)),
-            transcendentals=blocks * count * hidden_units,
-        ),
-        name="feed",
-    )(place, rows, grads, chunks)
-    return [outs[5 * block : 5 * block + 5] for block in range(blocks)]
-
-
-def weight_kernel(blocks, pairs, spread, added, *refs):
-    lefts, rights = refs[: blocks * pairs], refs[blocks * pairs : 2 * blocks * pairs]
-    rest = refs[2 * blocks * pairs :]
-    out_ref = rest[-1]
-    offset = 0
-    parts = []
-    for pair in range(pairs):
-        total = None
-        for block in range(blocks):
-            term = transposed_times(lefts[pair * blocks + block][...], rights[pair * blocks + block][...])
-            total = term if total is None else total + term
-        parts.append(total)
-    if spread:
-        joined = jnp.concatenate([part.astype(jnp.bfloat16) for part in parts], axis=1)
-        total = times_transposed(joined, rest[0][...])
-        if added:
-            total = total + rest[1][...].astype(jnp.float32)
-        out_ref[...] = total.astype(jnp.bfloat16)
-    else:
-        for pair, total in enumerate(parts):
-            lanes = slice(offset, offset + total.shape[1])
-            if added:
-                total = total + rest[0][:, lanes].astype(jnp.float32)
-            out_ref[:, lanes] = total.astype(jnp.bfloat16)
-            offset += total.shape[1]
-
-
-def weight_grad(pairs, side, spread=None, added=None, tile=256):
-    blocks = len(pairs[0][0])
-    lefts = [left for left_blocks, _ in pairs for left in left_blocks]
-    rights = [right for _, right_blocks in pairs for right in right_blocks]
-    count, width = lefts[0].shape
-    widths = [right_blocks[0].shape[1] // 2 for _, right_blocks in pairs]
-    columns = sum(widths) if spread is None else spread.shape[0]
-    operands = lefts + rights
-    in_specs = [pl.BlockSpec((count, tile), lambda i: (0, i)) for _ in lefts]
-    in_specs += [pl.BlockSpec((count, right.shape[1] // 2), lambda i: (0, side)) for right in rights]
-    if spread is not None:
-        operands.append(spread)
-        in_specs.append(pl.BlockSpec(spread.shape, lambda i: (0, 0)))
-    if added is not None:
-        operands.append(added)
-        in_specs.append(pl.BlockSpec((tile, columns), lambda i: (i, 0)))
-    return pl.pallas_call(
-        functools.partial(weight_kernel, blocks, len(pairs), spread is not None, added is not None),
-        grid=(width // tile,),
-        out_shape=jax.ShapeDtypeStruct((width, columns), jnp.bfloat16),
-        in_specs=in_specs,
-        out_specs=pl.BlockSpec((tile, columns), lambda i: (i, 0)),
-        compiler_params=vmem_params(),
-        cost_estimate=cost(
-            flops=2 * blocks * count * width * sum(widths),
-            bytes_accessed=2 * (blocks * count * (width * len(pairs) + sum(widths)) + width * columns),
-            transcendentals=0,
-        ),
-        name="weight_grad",
-    )(*operands)
 
 
 def hbm_spec():
@@ -729,7 +426,7 @@
     deep, first_ref, cotangent_ref, tokens_ref, gain_ref, qkv_halves, out_halves, feed_halves,
     qkv_spread, out_spread, cosine_ref, sine_ref,
     first_out, qkv_out, heads_out, logs_out, qkv_wide_out, out_wide_out, middle_out, second_out,
-    cotangent_out, feed_out,
+    cotangent_out, feed_out, qkv_own_out,
     first_all, qkv_buffer, out_buffer, qkv_wide, out_wide, qkv, heads, logs, keys, values,
     parts, core_parts, outgoing, incoming, middle, second,
     local_sems, row_sems, qkv_sems, out_sems, feed_sems, core_sems,
@@ -785,6 +482,7 @@
     out_kept.wait()
     feed_core.wait_recv()
     feed_kept.wait()
+    kept.append(keep_local(qkv_buffer.at[0, 0], qkv_own_out, 13))
     for shift, copy in zip(far + rest, qkv_z):
         copy.wait_recv()
         qkv_y.append(open_y(qkv_buffer, qkv_sems, shift))
@@ -919,6 +617,7 @@
         shape(4, count, width),
         shape(4, count, width),
         shape(2, deep, 2, part, feed_halves.shape[2]),
+        shape(2, part, qkv_halves.shape[2]),
     )
     scratch = [
         room(4, count, width),
@@ -937,7 +636,7 @@
         room(count, width),
         room(count, width, kind=jnp.float32),
         room(count, width),
-        pltpu.SemaphoreType.DMA((13,)),
+        pltpu.SemaphoreType.DMA((14,)),
         pltpu.SemaphoreType.DMA((2, 9)),
         pltpu.SemaphoreType.DMA((2, 2 * deep)),
         pltpu.SemaphoreType.DMA((2, 2 * deep)),
@@ -956,6 +655,688 @@
     )(first, cotangent, tokens, gain, qkv_halves, out_halves, feed_halves, *spreads, cosine, sine)
 
 
+EARLY = 6
+
+
+def ring_row(shift, deep, rows):
+    z_place = lax.rem(lax.axis_index("z").astype(jnp.int32) + shift, jnp.int32(deep))
+    return pl.multiple_of(z_place * rows, rows)
+
+
+def add_rows(target, source, step_rows=128):
+    @pl.loop(0, target.shape[0] // step_rows)
+    def _(step):
+        rows = pl.ds(pl.multiple_of(step * step_rows, step_rows), step_rows)
+        target[rows, :] = (target[rows, :].astype(jnp.float32) + source[rows, :].astype(jnp.float32)).astype(
+            jnp.bfloat16
+        )
+
+
+def pieces_of(deep):
+    return [(piece, shift) for piece in range(3) for shift in range(deep)]
+
+
+def feed_back_kernel(
+    deep, rows_hbm, grads_hbm, chunks, middle_hbm, gain_ref,
+    grad_middle_out, grad_attention_out, branch_out, sent_out, own_out, arrived_out,
+    gate, up, down, rows, grads, hidden, grad_gate, grad_up, parts, landing, incoming, middle, stage,
+    load_sems, weight_sems, store_sems, early_sems, core_sems, x_sems, y_sems,
+):
+    core_beside, x_beside, y_beside = beside()
+    greet([core_beside, x_beside, y_beside])
+    blocks, count, width = rows.shape
+    half = gate.shape[1] // 2
+    part = chunks.shape[3]
+    piece_rows = 2 * part
+    sent = []
+
+    def load(source, target, sem):
+        copy = pltpu.make_async_copy(source, target, sem)
+        copy.start()
+        return copy
+
+    def move(source, target, sems, index, where):
+        copy = send(source, target, (sems.at[0, index], sems.at[1, index]), where)
+        sent.append(copy)
+        return copy
+
+    row_loads = {}
+    for block in (3, 1):
+        row_loads[block] = [load(rows_hbm.at[block], rows.at[block], load_sems.at[0, block])]
+    weight_loads = []
+    for matrix, target in enumerate((gate, up, down)):
+        here = []
+        for side in range(2):
+            for shift in range(deep):
+                for rel in range(2):
+                    here.append(
+                        load(
+                            chunks.at[side, shift, rel, :, pl.ds(matrix * half, half)],
+                            target.at[pl.ds(grid_offset(shift, rel, deep, part), part), pl.ds(side * half, half)],
+                            weight_sems.at[matrix, side, shift, rel],
+                        )
+                    )
+        weight_loads.append(here)
+        if matrix == 0:
+            for block in (3, 1):
+                row_loads[block].append(load(grads_hbm.at[block], grads.at[block], load_sems.at[1, block]))
+    for block in (2, 0):
+        row_loads[block] = [
+            load(rows_hbm.at[block], rows.at[block], load_sems.at[0, block]),
+            load(grads_hbm.at[block], grads.at[block], load_sems.at[1, block]),
+        ]
+    middle_load = load(middle_hbm, middle, load_sems.at[0, 4])
+
+    def inner(block):
+        @pl.loop(0, gate.shape[1] // TILE)
+        def _(step):
+            lanes = pl.ds(pl.multiple_of(step * TILE, TILE), TILE)
+            gate_value = nn(rows[block], gate[:, lanes])
+            up_value = nn(rows[block], up[:, lanes])
+            grad_hidden = nn(grads[block], down[:, lanes])
+            sigmoid = 1.0 / (1.0 + jnp.exp(-gate_value))
+            swish = gate_value * sigmoid
+            slope = sigmoid + swish * (1.0 - sigmoid)
+            hidden[block, :, lanes] = (swish * up_value).astype(jnp.bfloat16)
+            grad_gate[block, :, lanes] = (grad_hidden * up_value * slope).astype(jnp.bfloat16)
+            grad_up[block, :, lanes] = (grad_hidden * swish).astype(jnp.bfloat16)
+
+    def outer(block):
+        @pl.loop(0, width // TILE)
+        def _(step):
+            lanes = pl.ds(pl.multiple_of(step * TILE, TILE), TILE)
+            parts[block, :, lanes] = (
+                times_transposed(grad_gate[block], gate[lanes, :])
+                + times_transposed(grad_up[block], up[lanes, :])
+            ).astype(jnp.bfloat16)
+
+    for position, block in enumerate((3, 1, 2, 0)):
+        for copy in row_loads[block]:
+            copy.wait()
+        if position == 0:
+            for here in weight_loads:
+                for copy in here:
+                    copy.wait()
+        inner(block)
+        outer(block)
+        if block == 3:
+            far = move(parts.at[3], landing.at[1], core_sems, 0, core_beside)
+        if block == 1:
+            far.wait_recv()
+            add_rows(parts.at[1], landing.at[1])
+            across = move(parts.at[1], incoming, x_sems, 0, x_beside)
+        if block == 2:
+            near = move(parts.at[2], landing.at[0], core_sems, 1, core_beside)
+
+    sources = ((grads, hidden), (rows, grad_gate), (rows, grad_up))
+
+    def weight_part(piece, side, shift):
+        left, right = sources[piece]
+        row = ring_row(shift, deep, piece_rows)
+        lanes = slice(side * half, (side + 1) * half)
+        product = transposed_times(
+            left[:, :, pl.ds(row, piece_rows)].reshape(blocks * count, piece_rows),
+            right[:, :, lanes].reshape(blocks * count, half),
+        )
+        stage[piece, pl.ds(row, piece_rows), :] = product.astype(jnp.bfloat16)
+
+    early = pieces_of(deep)[:EARLY]
+    arrivals, stores, pending = [], [], []
+
+    def flush():
+        for index, store, target in pending:
+            store.wait()
+            arrivals.append(move(target, arrived_out.at[index], y_sems, index, y_beside))
+        pending.clear()
+
+    for piece in range(3):
+        mine = [pair for pair in early if pair[0] == piece]
+        for pair in mine:
+            weight_part(piece, 1, pair[1])
+            flush()
+            rows_here = pl.ds(ring_row(pair[1], deep, piece_rows), piece_rows)
+            index = early.index(pair)
+            target = sent_out.at[piece, rows_here, :]
+            pending.append((index, load(stage.at[piece, rows_here, :], target, early_sems.at[index]), target))
+        for shift in range(len(mine), deep):
+            weight_part(piece, 1, shift)
+            flush()
+            rows_here = pl.ds(ring_row(shift, deep, piece_rows), piece_rows)
+            stores.append(
+                load(
+                    stage.at[piece, rows_here, :],
+                    sent_out.at[piece, rows_here, :],
+                    early_sems.at[piece * deep + shift],
+                )
+            )
+    late_stores = list(stores)
+    near.wait_recv()
+    middle_load.wait()
+    across.wait_recv()
+    step_rows = 128
+
+    @pl.loop(0, count // step_rows)
+    def _(step):
+        tile = pl.ds(pl.multiple_of(step * step_rows, step_rows), step_rows)
+        grad = (
+            parts[0, tile, :].astype(jnp.float32)
+            + landing[0, tile, :].astype(jnp.float32)
+            + incoming[tile, :].astype(jnp.float32)
+        )
+        total = grads[0, tile, :].astype(jnp.float32) + norm_back(middle[tile, :], gain_ref[...], grad)
+        middle[tile, :] = total
+        incoming[tile, :] = total.astype(jnp.bfloat16)
+
+    attention_x = move(incoming, grad_attention_out.at[1], x_sems, 1, x_beside)
+    attention_core = move(incoming, grad_attention_out.at[2], core_sems, 2, core_beside)
+    stores.append(load(incoming, grad_attention_out.at[0], store_sems.at[0]))
+    stores.append(load(middle, grad_middle_out, store_sems.at[3]))
+
+    far.wait_send()
+    across.wait_send()
+    near.wait_send()
+
+    def branch(block):
+        @pl.loop(0, width // TILE)
+        def _(step):
+            lanes = pl.ds(pl.multiple_of(step * TILE, TILE), TILE)
+            parts[block, :, lanes] = times_transposed(hidden[block], down[lanes, :]).astype(jnp.bfloat16)
+
+    branch(3)
+    attention_core.wait_recv()
+    branch_far = move(parts.at[3], landing.at[1], core_sems, 3, core_beside)
+    branch(2)
+    branch_near = move(parts.at[2], landing.at[0], core_sems, 4, core_beside)
+    branch(1)
+    branch_far.wait_recv()
+    add_rows(parts.at[1], landing.at[1])
+    stores.append(load(parts.at[1], branch_out.at[1], store_sems.at[4]))
+    branch(0)
+    stores.append(load(parts.at[0], branch_out.at[0], store_sems.at[5]))
+    branch_near.wait_recv()
+    stores.append(load(landing.at[0], branch_out.at[2], store_sems.at[6]))
+    for copy in late_stores:
+        copy.wait()
+    for piece in range(3):
+
+        @pl.loop(0, deep)
+        def _(shift, piece=piece):
+            weight_part(piece, 0, shift)
+
+        stores.append(load(stage.at[piece], own_out.at[piece], store_sems.at[7 + piece]))
+    attention_x.wait_recv()
+    attention_far = move(grad_attention_out.at[1], grad_attention_out.at[3], core_sems, 5, core_beside)
+    attention_far.wait_recv()
+    for copy in arrivals:
+        copy.wait_recv()
+    for copy in stores[len(late_stores) :]:
+        copy.wait()
+    for copy in arrivals:
+        copy.wait_send()
+    for copy in (attention_x, attention_core, branch_far, branch_near, attention_far):
+        copy.wait_send()
+
+
+def feed_back(deep, rows, grads, chunks, middle, gain):
+    blocks, count, width = rows.shape
+    half = chunks.shape[4] // 3
+    part = chunks.shape[3]
+
+    def shape(*dims, kind=jnp.bfloat16):
+        return jax.ShapeDtypeStruct(dims, kind)
+
+    def room(*dims, kind=jnp.bfloat16):
+        return pltpu.VMEM(dims, kind)
+
+    outs = (
+        shape(count, width, kind=jnp.float32),
+        shape(blocks, count, width),
+        shape(3, count, width),
+        shape(3, width, half),
+        shape(3, width, half),
+        shape(EARLY, 2 * part, half),
+    )
+    dma = pltpu.SemaphoreType.DMA
+    return pl.pallas_call(
+        functools.partial(feed_back_kernel, deep),
+        out_shape=outs,
+        in_specs=[hbm_spec()] * 4 + [vmem_spec()],
+        out_specs=(hbm_spec(),) * len(outs),
+        scratch_shapes=[room(width, 2 * half)] * 3
+        + [room(blocks, count, width)] * 2
+        + [room(blocks, count, 2 * half)] * 3
+        + [room(blocks, count, width), room(2, count, width), room(count, width)]
+        + [room(count, width, kind=jnp.float32), room(3, width, half)]
+        + [dma((2, 5)), dma((3, 2, deep, 2)), dma((10,)), dma((3 * deep,)), dma((2, 6)), dma((2, 2)), dma((2, EARLY))],
+        compiler_params=vmem_params(collective_id=2, has_side_effects=True),
+        cost_estimate=cost(flops=80 * 10**9, bytes_accessed=10**8, transcendentals=10**7),
+        name="feed_back",
+    )(rows, grads, chunks, middle, gain)
+
+
+def attend_back_pair(
+    qkv, grad_heads, heads, logs, cosine_ref, sine_ref, grad_qkv, keys, values, grad_keys, grad_values,
+    sequence, pair,
+):
+    count = qkv.shape[1]
+    x_place = lax.axis_index("x").astype(jnp.int32)
+    lane0 = pl.multiple_of(pair * 4 * LANES, 4 * LANES)
+    head0 = pl.multiple_of(pair * 2 * LANES, 2 * LANES)
+    mask = diagonal_mask()
+    factor = HD ** (-0.5)
+    scale = factor * LOG2E
+    for rel in range(2):
+        position = lax.rem(x_place + rel, jnp.int32(2))
+        rows = pl.ds(pl.multiple_of(position * count, count), count)
+        keys[rows, :] = qkv[2 * sequence + rel, :, pl.ds(lane0 + 2 * LANES, LANES)]
+        values[rows, :] = qkv[2 * sequence + rel, :, pl.ds(lane0 + 3 * LANES, LANES)]
+    grad_keys[...] = jnp.zeros_like(grad_keys)
+    grad_values[...] = jnp.zeros_like(grad_values)
+
+    def visit(rel, start, before):
+        block = 2 * sequence + rel
+        rows = slice(start, start + TILE)
+
+        def both(ref, first):
+            return jnp.concatenate(
+                [ref[block, rows, pl.ds(first, LANES)], ref[block, rows, pl.ds(first + LANES, LANES)]], axis=0
+            )
+
+        queries, grads, outs = both(qkv, lane0), both(grad_heads, head0), both(heads, head0)
+        lane = lax.broadcasted_iota(jnp.int32, (TILE, LANES), 1)
+        kept = logs[block, rows, :]
+        log = jnp.concatenate(
+            [
+                jnp.sum(jnp.where(lane == 2 * pair + head, kept, 0.0), axis=-1, keepdims=True)
+                for head in range(2)
+            ],
+            axis=0,
+        )
+        inner = jnp.sum(grads.astype(jnp.float32) * outs.astype(jnp.float32), axis=-1, keepdims=True)
+
+        def span(span_rows, masked):
+            softmax = jnp.exp2(times_transposed(queries, keys[span_rows, :]) * scale - log)
+            if masked:
+                softmax = jnp.where(mask, softmax, 0.0)
+            grad_softmax = times_transposed(grads, values[span_rows, :])
+            grad_scores = (softmax * (grad_softmax - inner)).astype(jnp.bfloat16)
+            grad_values[span_rows, :] += transposed_times(softmax.astype(jnp.bfloat16), grads)
+            grad_keys[span_rows, :] += transposed_times(grad_scores, queries)
+            return nn(grad_scores, keys[span_rows, :])
+
+        grad_queries = span(slice(before, before + TILE), True)
+        if before:
+            grad_queries = grad_queries + span(slice(0, before), False)
+        cosine, sine = cosine_ref[rel, rows, :], -sine_ref[rel, rows, :]
+        for head in range(2):
+            piece = grad_queries[head * TILE : (head + 1) * TILE] * factor
+            grad_qkv[block, rows, pl.ds(lane0 + head * LANES, LANES)] = turn(piece, cosine, sine).astype(
+                jnp.bfloat16
+            )
+
+    for rel in range(2):
+        position = lax.rem(x_place + rel, jnp.int32(2))
+        for static_position in range(2):
+
+            @pl.when(position == static_position)
+            def _(rel=rel, static_position=static_position):
+                for step in range(count // TILE):
+                    visit(rel, step * TILE, static_position * count + step * TILE)
+
+    for rel in range(2):
+        block = 2 * sequence + rel
+        position = lax.rem(x_place + rel, jnp.int32(2))
+        rows = pl.ds(pl.multiple_of(position * count, count), count)
+        grad_qkv[block, :, pl.ds(lane0 + 2 * LANES, LANES)] = turn(
+            grad_keys[rows, :] * factor, cosine_ref[rel], -sine_ref[rel]
+        ).astype(jnp.bfloat16)
+        grad_qkv[block, :, pl.ds(lane0 + 3 * LANES, LANES)] = grad_values[rows, :].astype(jnp.bfloat16)
+
+
+def heads_back_kernel(
+    deep, grad_attention_hbm, qkv_hbm, heads_hbm, logs_hbm, first_hbm, qkv_wide_hbm, out_wide_hbm,
+    branch_hbm, sent_hbm, own_hbm, early_hbm, chunks_hbm, qkv_own_hbm,
+    cosine_ref, sine_ref, qkv_spread, out_spread,
+    first_part, first_core, first_x, branch_x, feed_final, qkv_final, out_final, first_gain_out, second_gain_out,
+    grad_attention, qkv, heads, grad_heads, logs, grad_qkv, qkv_wide, out_wide, keys, values, grad_keys,
+    grad_values, landing, feed_sum, feed_y, feed_z, out_sent, out_sum, out_y, out_z, qkv_sent, qkv_sum, qkv_y,
+    qkv_z, feed_last, qkv_last, out_last, feed_weight, qkv_weight, gain_part, gain_in, gain_total,
+    load_sems, own_sems, tile_sems, core_sems, x_sems, y_sems, z_sems, gain_sems,
+):
+    blocks, count, width = grad_attention.shape
+    core_beside, x_beside, y_beside = beside()
+    core, z_place = lax.axis_index("c").astype(jnp.int32), lax.axis_index("z").astype(jnp.int32)
+    across, along = lax.axis_index("x").astype(jnp.int32), lax.axis_index("y").astype(jnp.int32)
+    ring = jnp.int32(deep)
+    z_ahead = [{"z": lax.rem(z_place + shift, ring)} for shift in range(deep)]
+    cube = {
+        (rel, up, over): {"c": (core + rel) % 2, "y": (along + up) % 2, "x": (across + over) % 2}
+        for rel in range(2)
+        for up in range(2)
+        for over in range(2)
+    }
+    far_cube = [key for key in cube if key != (0, 0, 0)]
+    greet([cube[key] for key in far_cube] + z_ahead[1:])
+    half = feed_sum.shape[3]
+    piece_rows = feed_sum.shape[2]
+    part = piece_rows // 2
+    step_rows = 128
+    sent = []
+
+    def load(source, target, sem):
+        copy = pltpu.make_async_copy(source, target, sem)
+        copy.start()
+        return copy
+
+    def move(source, target, sems, index, where):
+        copy = send(source, target, (sems.at[0, index], sems.at[1, index]), where)
+        sent.append(copy)
+        return copy
+
+    early, late = pieces_of(deep)[:EARLY], pieces_of(deep)[EARLY:]
+    attention_load = load(grad_attention_hbm, grad_attention, load_sems.at[0])
+    out_load = load(out_wide_hbm, out_wide, load_sems.at[1])
+    heads_load = load(heads_hbm, heads, load_sems.at[2])
+    late_copies = []
+    for index, (piece, shift) in enumerate(late):
+        row = ring_row(shift, deep, piece_rows)
+        late_copies.append(
+            move(
+                sent_hbm.at[piece, pl.ds(row, piece_rows), :], feed_y.at[piece, shift], y_sems, index, y_beside
+            )
+        )
+    branch_copy = move(branch_hbm.at[1], branch_x, x_sems, 0, x_beside)
+    qkv_load = load(qkv_hbm, qkv, load_sems.at[3])
+    logs_load = load(logs_hbm, logs, load_sems.at[4])
+    wide_load = load(qkv_wide_hbm, qkv_wide, load_sems.at[5])
+    own_loads = {}
+    early_loads = {}
+    for index, (piece, shift) in enumerate(pieces_of(deep)):
+        row = ring_row(shift, deep, piece_rows)
+        own_loads[piece, shift] = load(
+            own_hbm.at[piece, pl.ds(row, piece_rows), :], feed_sum.at[piece, shift], own_sems.at[0, index]
+        )
+        if (piece, shift) in early:
+            early_loads[piece, shift] = load(
+                early_hbm.at[index], feed_y.at[piece, shift], own_sems.at[1, index]
+            )
+    weight_loads = [
+        load(chunks_hbm.at[0, 0, :, :, pl.ds(0, 2 * half)], feed_weight, load_sems.at[6]),
+        load(qkv_own_hbm, qkv_weight, load_sems.at[7]),
+    ]
+
+    attention_load.wait()
+    out_load.wait()
+
+    @pl.loop(0, blocks)
+    def _(block):
+        grad_heads[block] = nn(grad_attention[block], out_wide[...]).astype(jnp.bfloat16)
+
+    heads_load.wait()
+
+    def weight_tile(left, right, spread, side):
+        size = spread.shape[1]
+        right = right[:, :, side * size : (side + 1) * size].reshape(blocks * count, size)
+        product = transposed_times(left.reshape(blocks * count, piece_rows), right)
+        return times_transposed(product.astype(jnp.bfloat16), spread[...]).astype(jnp.bfloat16)
+
+    y_index = len(late)
+    out_copies = []
+    for shift in range(deep):
+        row = ring_row(shift, deep, piece_rows)
+        out_sent[shift] = weight_tile(grad_attention[:, :, pl.ds(row, piece_rows)], heads, out_spread, 1)
+        out_copies.append(move(out_sent.at[shift], out_y.at[shift], y_sems, y_index + shift, y_beside))
+
+    @pl.loop(0, deep)
+    def _(shift):
+        row = ring_row(shift, deep, piece_rows)
+        out_sum[shift] = weight_tile(grad_attention[:, :, pl.ds(row, piece_rows)], heads, out_spread, 0)
+
+    z_copies = {}
+
+    def join_piece(name, number, total, arrived, target, shift):
+        add_rows(total.at[shift], arrived.at[shift])
+        if shift:
+            z_copies[name, shift] = move(
+                total.at[shift], target.at[shift - 1], z_sems, number * (deep - 1) + shift - 1, z_ahead[shift]
+            )
+
+    def join_feed(piece, shift):
+        own_loads[piece, shift].wait()
+        join_piece(piece, piece, feed_sum.at[piece], feed_y.at[piece], feed_z.at[piece], shift)
+
+    for pair in early:
+        early_loads[pair].wait()
+        join_feed(*pair)
+
+    qkv_load.wait()
+    logs_load.wait()
+    for sequence in range(2):
+
+        @pl.loop(0, 2)
+        def _(pair, sequence=sequence):
+            attend_back_pair(
+                qkv, grad_heads, heads, logs, cosine_ref, sine_ref, grad_qkv, keys, values, grad_keys,
+                grad_values, sequence, pair,
+            )
+
+        for index in range(sequence * 2, sequence * 2 + 2):
+            late_copies[index].wait_recv()
+            join_feed(*late[index])
+    wide_load.wait()
+
+    def first_tile(shift):
+        row = ring_row(shift, deep, piece_rows)
+        slot = (shift % 2) * 512
+        return load(
+            first_hbm.at[:, :, pl.ds(row, piece_rows)],
+            qkv.at[:, :, pl.ds(slot, piece_rows)],
+            tile_sems.at[shift],
+        )
+
+    first_loads = [first_tile(shift) for shift in range(2)]
+
+    def first_piece(block):
+        @pl.loop(0, width // 512)
+        def _(step):
+            lanes = pl.ds(pl.multiple_of(step * 512, 512), 512)
+            grad_attention[block, :, lanes] = times_transposed(grad_qkv[block], qkv_wide[lanes, :]).astype(
+                jnp.bfloat16
+            )
+
+    first_piece(3)
+    core_far = move(grad_attention.at[3], landing, core_sems, 0, core_beside)
+    first_piece(1)
+    core_far.wait_recv()
+    add_rows(grad_attention.at[1], landing)
+    x_copy = move(grad_attention.at[1], first_x, x_sems, 1, x_beside)
+    first_piece(2)
+    core_near = move(grad_attention.at[2], first_core, core_sems, 1, core_beside)
+    first_piece(0)
+    first_store = load(grad_attention.at[0], first_part, load_sems.at[8])
+
+    qkv_copies = []
+    y_index += deep
+    for shift in range(deep):
+        first_loads[shift].wait()
+        slot = (shift % 2) * 512
+        left = qkv[:, :, slot : slot + piece_rows]
+        qkv_sent[shift] = weight_tile(left, grad_qkv, qkv_spread, 1)
+        qkv_copies.append(move(qkv_sent.at[shift], qkv_y.at[shift], y_sems, y_index + shift, y_beside))
+        qkv_sum[shift] = weight_tile(left, grad_qkv, qkv_spread, 0)
+        if shift + 2 < deep:
+            first_loads.append(first_tile(shift + 2))
+
+    for index in range(4, len(late)):
+        late_copies[index].wait_recv()
+        join_feed(*late[index])
+    for shift in range(deep):
+        out_copies[shift].wait_recv()
+        join_piece("out", 3, out_sum, out_y, out_z, shift)
+
+    finals = []
+
+    def finish(name, number, total, arrived, last, final, weights):
+        for shift in range(1, deep):
+            z_copies[name, shift].wait_recv()
+        size = total.shape[2]
+        sums = []
+        for rel in range(2):
+            row = pl.multiple_of(lax.rem(core + rel, jnp.int32(2)) * part, part)
+            value = total[0, pl.ds(row, part), :].astype(jnp.float32)
+            for shift in range(deep - 1):
+                value = value + arrived[shift, pl.ds(row, part), :].astype(jnp.float32)
+            last[rel] = value
+            if weights is not None:
+                product = value * weights[rel].astype(jnp.float32)
+                sums.append(sum(product[:, i * LANES : (i + 1) * LANES] for i in range(size // LANES)))
+        finals.append(load(last.at[0], final.at[core], own_sems.at[1, 12 + number]))
+        finals.append(move(last.at[1], final.at[core], core_sems, 2 + number, core_beside))
+        return sums
+
+    def gain_exchange(which, sums):
+        slots = {}
+        for rel in range(2):
+            gain_part[which, rel] = sums[rel]
+        piece = part // 4
+        for number, key in enumerate(far_cube):
+            rel, up, over = key
+            target = ((along + up) % 2) * 2 + (across + over) % 2
+            row = pl.multiple_of(target * piece, 8)
+            slots[key] = move(
+                gain_part.at[which, rel, pl.ds(row, piece), :],
+                gain_in.at[which, number],
+                gain_sems,
+                which * len(far_cube) + number,
+                cube[key],
+            )
+        return slots
+
+    def gain_finish(which, slots, output):
+        piece = part // 4
+        row = pl.multiple_of((along * 2 + across) * piece, 8)
+        value = gain_part[which, 0, pl.ds(row, piece), :]
+        for number, key in enumerate(far_cube):
+            slots[key].wait_recv()
+            value = value + gain_in[which, number]
+        gain_total[which] = value
+        return load(gain_total.at[which], output, load_sems.at[9 + which])
+
+    for copy in weight_loads:
+        copy.wait()
+    finish(0, 0, feed_sum.at[0], feed_z.at[0], feed_last.at[0], feed_final.at[0], None)
+    gate_sums = finish(
+        1, 1, feed_sum.at[1], feed_z.at[1], feed_last.at[1], feed_final.at[1], feed_weight.at[:, :, pl.ds(0, half)]
+    )
+    for shift in range(deep):
+        qkv_copies[shift].wait_recv()
+        join_piece("qkv", 4, qkv_sum, qkv_y, qkv_z, shift)
+    up_sums = finish(
+        2, 2, feed_sum.at[2], feed_z.at[2], feed_last.at[2], feed_final.at[2],
+        feed_weight.at[:, :, pl.ds(half, half)],
+    )
+    second_slots = gain_exchange(1, [one + two for one, two in zip(gate_sums, up_sums)])
+    finish("out", 3, out_sum, out_z, out_last, out_final, None)
+    sums = finish("qkv", 4, qkv_sum, qkv_z, qkv_last, qkv_final, qkv_weight)
+    first_slots = gain_exchange(0, sums)
+    second_store = gain_finish(1, second_slots, second_gain_out)
+    first_gain_store = gain_finish(0, first_slots, first_gain_out)
+    for copy in (branch_copy, x_copy, core_near):
+        copy.wait_recv()
+    for number in range(5):
+        finals[2 * number].wait()
+        finals[2 * number + 1].wait_recv()
+    for copy in (first_store, second_store, first_gain_store):
+        copy.wait()
+    for copy in sent:
+        copy.wait_send()
+
+
+def heads_back(
+    deep, grad_attention, qkv, heads, logs, first, qkv_wide, out_wide, branch, sent, own, early, chunks, qkv_own,
+    cosine, sine, spreads,
+):
+    blocks, count, width = grad_attention.shape
+    part, half = chunks.shape[3], chunks.shape[4] // 3
+    qkv_half, out_half = spreads[0].shape[0], spreads[1].shape[0]
+    rows = 2 * part
+
+    def shape(*dims, kind=jnp.bfloat16):
+        return jax.ShapeDtypeStruct(dims, kind)
+
+    def room(*dims, kind=jnp.bfloat16):
+        return pltpu.VMEM(dims, kind)
+
+    wide = jnp.float32
+    outs = (
+        shape(count, width),
+        shape(count, width),
+        shape(count, width),
+        shape(count, width),
+        shape(3, 2, part, half, kind=wide),
+        shape(2, part, qkv_half, kind=wide),
+        shape(2, part, out_half, kind=wide),
+        shape(part // 4, LANES, kind=wide),
+        shape(part // 4, LANES, kind=wide),
+    )
+    dma = pltpu.SemaphoreType.DMA
+    scratch = [
+        room(blocks, count, width),
+        room(*qkv.shape),
+        room(*heads.shape),
+        room(*heads.shape),
+        room(*logs.shape, kind=wide),
+        room(*qkv.shape),
+        room(*qkv_wide.shape),
+        room(*out_wide.shape),
+        room(2 * count, LANES),
+        room(2 * count, LANES),
+        room(2 * count, LANES, kind=wide),
+        room(2 * count, LANES, kind=wide),
+        room(count, width),
+        room(3, deep, rows, half),
+        room(3, deep, rows, half),
+        room(3, deep - 1, rows, half),
+        room(deep, rows, out_half),
+        room(deep, rows, out_half),
+        room(deep, rows, out_half),
+        room(deep - 1, rows, out_half),
+        room(deep, rows, qkv_half),
+        room(deep, rows, qkv_half),
+        room(deep, rows, qkv_half),
+        room(deep - 1, rows, qkv_half),
+        room(3, 2, part, half, kind=wide),
+        room(2, part, qkv_half, kind=wide),
+        room(2, part, out_half, kind=wide),
+        room(2, part, 2 * half),
+        room(2, part, qkv_half),
+        room(2, 2, part, LANES, kind=wide),
+        room(2, 7, part // 4, LANES, kind=wide),
+        room(2, part // 4, LANES, kind=wide),
+        dma((11,)),
+        dma((2, max(3 * deep, 17))),
+        dma((deep,)),
+        dma((2, 7)),
+        dma((2, 2)),
+        dma((2, 5 * deep)),
+        dma((2, 5 * (deep - 1))),
+        dma((2, 14)),
+    ]
+    return pl.pallas_call(
+        functools.partial(heads_back_kernel, deep),
+        out_shape=outs,
+        in_specs=[hbm_spec()] * 13 + [vmem_spec()] * 4,
+        out_specs=(hbm_spec(),) * len(outs),
+        scratch_shapes=scratch,
+        compiler_params=vmem_params(collective_id=3, has_side_effects=True),
+        cost_estimate=cost(flops=30 * 10**9, bytes_accessed=10**8, transcendentals=10**7),
+        name="heads_back",
+    )(
+        grad_attention, qkv, heads, logs, first, qkv_wide, out_wide, branch, sent, own, early, chunks, qkv_own,
+        cosine, sine, *spreads,
+    )
+
+
 def tables(rows, x_place):
     lane = np.arange(LANES)
     entry = lane % (LANES // 2)
@@ -982,40 +1363,14 @@
     return factor * scaled - rows * factor**3 * jnp.mean(scaled * rows, axis=-1, keepdims=True)
 
 
-def spread_blocks(own):
-    beside = swap(own, "x")
-    return [own, beside, swap(own, "c"), swap(beside, "c")]
-
-
-def sum_blocks(parts):
-    beside = parts[1].astype(jnp.float32) + swap(parts[3], "c").astype(jnp.float32)
-    arrived = swap(beside.astype(jnp.bfloat16), "x")
-    own = parts[0].astype(jnp.float32) + swap(parts[2], "c").astype(jnp.float32)
-    return own + arrived.astype(jnp.float32)
-
-
-def finish_grad(summed, core, part):
-    mine = lax.psum_scatter(summed, "z", scatter_dimension=0, tiled=True)
-    keep = lax.dynamic_slice_in_dim(mine, core * part, part, axis=0)
-    send = lax.dynamic_slice_in_dim(mine, (1 - core) * part, part, axis=0)
-    recv = swap(send, "c")
-    first = jnp.where(core == 0, keep, recv).astype(jnp.float32)
-    second = jnp.where(core == 0, recv, keep).astype(jnp.float32)
-    return first, second
-
-
-def join(first, second, start, stop):
-    return jnp.concatenate([first[:, start:stop], second[:, start:stop]], axis=1)
-
-
-def gain_grad(columns, gain, depth_place, part):
-    rows = sum(jnp.sum(grad * weight.astype(jnp.float32), axis=1) for grad, weight in columns)
-    rows = rows / lax.dynamic_slice_in_dim(gain, depth_place * part, part)
-    rows = rows + swap(rows, "x")
-    rows = rows + swap(rows, "y")
-    piece = part // 4
-    place = lax.axis_index("y") * 2 + lax.axis_index("x")
-    return lax.dynamic_slice_in_dim(rows, place * piece, piece)
+def join(halves):
+    return jnp.concatenate([halves[0], halves[1]], axis=1)
+
+
+def gain_grad(lanes, gain, depth_place):
+    piece = lanes.shape[0]
+    start = (depth_place * 4 + lax.axis_index("y") * 2 + lax.axis_index("x")) * piece
+    return jnp.sum(lanes, axis=1) / lax.dynamic_slice_in_dim(gain, start, piece)
 
 
 def fast_local(
@@ -1033,9 +1388,7 @@
 ):
     deep = lax.axis_size("z")
     z_place, core, x_place = (lax.axis_index(name).astype(jnp.int32) for name in ("z", "c", "x"))
-    place = jnp.stack([z_place, core, x_place])
     rows = tokens.shape[0]
-    part = gate_weight.shape[0]
     depth_place = z_place * 2 + core
     own_rows = tokens.astype(jnp.float32)
     first_normed = (own_rows * norm_factor(own_rows) * first_gain).astype(jnp.bfloat16)
@@ -1051,11 +1404,10 @@
             result.append(jnp.concatenate(pieces, axis=1))
         return result
 
-    spread = spread_heads(3, 3)
     spreads = (spread_heads(3, 1), spread_heads(0, 2))
     cosine, sine = tables(rows, x_place)
     (
-        first_all, qkv_all, heads_all, logs_all, qkv_weight, out_wide, middle, second_all, cotangent_all, chunks,
+        first_all, qkv_all, heads_all, logs_all, qkv_weight, out_wide, middle, second_all, cotangent_all, chunks, qkv_own,
     ) = forward(
         deep,
         first_normed,
@@ -1069,72 +1421,36 @@
         cosine,
         sine,
     )
-    first_blocks, cotangent_blocks, second_blocks, qkv, heads, logs = (
-        [stack[i] for i in range(4)]
-        for stack in (first_all, cotangent_all, second_all, qkv_all, heads_all, logs_all)
-    )
-    fed = [None] * 4
-    for pair in ((1, 3), (0, 2)):
-        outs = feed(place, second_all, cotangent_all, chunks, pair)
-        for i, out in zip(pair, outs):
-            fed[i] = out
-    hidden, grad_gate, grad_up, branches, grads_second = ([block[i] for block in fed] for i in range(5))
-    grad_second = sum_blocks(grads_second)
-    grad_middle = cotangent.astype(jnp.float32) + norm_back(middle, second_gain, grad_second)
-    grad_attention = spread_blocks(grad_middle.astype(jnp.bfloat16))
-    result = (middle + sum_blocks(branches)).astype(jnp.bfloat16)
-
-    down_sent = swap(weight_grad([(cotangent_blocks, hidden)], 1), "y")
-    wide_sent = swap(weight_grad([(second_blocks, grad_gate), (second_blocks, grad_up)], 1), "y")
-    down_grads = finish_grad(weight_grad([(cotangent_blocks, hidden)], 0, added=down_sent), core, part)
-    wide_grads = finish_grad(
-        weight_grad([(second_blocks, grad_gate), (second_blocks, grad_up)], 0, added=wide_sent), core, part
-    )
-
-    grad_heads = [nn(block, out_wide).astype(jnp.bfloat16) for block in grad_attention]
-    grad_qkv = []
-    for sequence in range(2):
-        chosen = slice(2 * sequence, 2 * sequence + 2)
-        grad_qkv += attend_back(
-            place, qkv[chosen], grad_heads[chosen], heads[chosen], logs[chosen], cosine, sine
+    grad_middle, grad_attention, branch, sent, own, early = feed_back(
+        deep, second_all, cotangent_all, chunks, middle, second_gain[None]
+    )
+    first_part, first_core, first_x, branch_x, feed_final, qkv_final, out_final, first_lanes, second_lanes = (
+        heads_back(
+            deep, grad_attention, qkv_all, heads_all, logs_all, first_all, qkv_weight, out_wide, branch, sent,
+            own, early, chunks, qkv_own, cosine, sine, spreads,
         )
-    grad_first = sum_blocks([times_transposed(block, qkv_weight).astype(jnp.bfloat16) for block in grad_qkv])
+    )
+
+    def total(*parts):
+        return sum(piece.astype(jnp.float32) for piece in parts)
+
+    result = (middle + total(branch[0], branch[2], branch_x)).astype(jnp.bfloat16)
+    grad_first = total(first_part, first_core, first_x)
     tokens_grad = grad_middle + norm_back(own_rows, first_gain, grad_first)
-    head_pairs = [(first_blocks, grad_qkv), (grad_attention, heads)]
-    heads_sent = swap(weight_grad(head_pairs, 1, spread=spread), "y")
-    heads_grads = finish_grad(
-        weight_grad(head_pairs, 0, spread=spread, added=heads_sent), core, part
-    )
-
-    sizes = [weight.shape[1] // 2 for weight in (query_weight, key_weight, value_weight, out_turned)]
-    starts = np.cumsum([0] + sizes)
-    query_grad, key_grad, value_grad, out_grad = (
-        join(*heads_grads, int(starts[i]), int(starts[i + 1])) for i in range(4)
-    )
-    half = gate_weight.shape[1] // 2
-    gate_grad, up_grad = (join(*wide_grads, i * half, (i + 1) * half) for i in range(2))
-    down_grad = join(*down_grads, 0, half)
-    first_gain_grad = gain_grad(
-        ((query_grad, query_weight), (key_grad, key_weight), (value_grad, value_weight)),
-        first_gain,
-        depth_place,
-        part,
-    )
-    second_gain_grad = gain_grad(
-        ((gate_grad, gate_weight), (up_grad, up_weight)), second_gain, depth_place, part
-    )
+    query_end = query_weight.shape[1] // 2
+    key_end = query_end + key_weight.shape[1] // 2
     return (
         result,
         tokens_grad,
-        query_grad,
-        key_grad,
-        value_grad,
-        out_grad.T,
-        gate_grad,
-        up_grad,
-        down_grad.T,
-        first_gain_grad,
-        second_gain_grad,
+        join(qkv_final[:, :, :query_end]),
+        join(qkv_final[:, :, query_end:key_end]),
+        join(qkv_final[:, :, key_end:]),
+        join(out_final).T,
+        join(feed_final[1]),
+        join(feed_final[2]),
+        join(feed_final[0]).T,
+        gain_grad(first_lanes, first_gain, depth_place),
+        gain_grad(second_lanes, second_gain, depth_place),
     )
 
 

time: 627 us -> 515 us (0.82)
  the two profiles are of different devices: /device:TPU:0 before, /device:TPU:13 now
where the time goes in v3:
time: 515 us; the launch traced here: 506 us
  Pallas kernels  470 us (91%)
  other arithmetic  28.8 us (6%)
  local copies, waits for them, and re-layouts  6.06 us (1%)
    pallas_call x1, Pallas kernels, heads_back(): pl.pallas_call(functools.partial(heads_back_kernel, deep), out_shape=outs...  182 us
    pallas_call x1, Pallas kernels, forward(): pl.pallas_call(functools.partial(forward_kernel, deep), out_shape=outs, i...  179 us
    pallas_call x1, Pallas kernels, feed_back(): pl.pallas_call(functools.partial(feed_back_kernel, deep), out_shape=outs,...  108 us

profile of v3, /device:TPU:13, one launch (start us, length us, event | category | flops | bytes accessed | tf_op | source)
XLA Modules:
  0.0 505.6 jit_solution(6875641042682273695)
XLA Ops:
  0.7 1.9 fusion
  2.6 1.3 broadcast_in_dim.2.gain_ref
  3.9 1.1 fusion.13
  5.0 1.1 fusion.14
  6.0 1.1 fusion.12
  7.1 0.2 maximum_bitcast_fusion.4
  7.3 0.8 pad_maximum_fusion.4.qkv_halves
  8.1 0.7 pad_maximum_fusion.6.out_halves
  9.1 1.1 pad_maximum_fusion.feed_halves
  10.2 0.2 broadcast_multiply_fusion.1
  10.4 2.7 sine_multiply_fusion
  13.1 1.6 fusion.2.first_ref
  14.7 179.2 %forward.1 = (bf16[4,512,1536]{2,1,0:T(8,128)(2,1)}, bf16[4,512,1024]{2,1,0:T(8,128)(2,1)}, bf16[4,512,512]{2,1,0:T(8,128)(2,1)}, f32[4,512,128]{2,1,0:T(8,128)}...) custom-call(bf16[512,1536]{1,0:T(8,128)(2,1)} %fusion.2.first_ref, ...), custom_call_target="tpu_custom_call" | custom-call | flops 1000000000 | bytes 5000000 | tf_op jit(solution)/shard_map/forward/pallas_call | solution.py:646
  193.9 108.1 %feed_back.1 = (f32[512,1536]{1,0:T(8,128)}, bf16[4,512,1536]{2,1,0:T(8,128)(2,1)}, bf16[3,512,1536]{2,1,0:T(8,128)(2,1)}, bf16[3,1536,512]{2,1,0:T(8,128)(2,1)}...) custom-call(bf16[4,512,1536]{2,1,0:T(8,128)(2,1)} %get-tuple-element.38.rows_hbm, ...), custom_call_target="tpu_custom_call" | custom-call | flops 4000000000 | bytes 5000000 | tf_op jit(solution)/shard_map/feed_back/pallas_call | solution.py:900
  302.0 182.4 %heads_back.1 = (bf16[512,1536]{1,0:T(8,128)(2,1)}, bf16[512,1536]{1,0:T(8,128)(2,1)}, bf16[512,1536]{1,0:T(8,128)(2,1)}, bf16[512,1536]{1,0:T(8,128)(2,1)}, f32...) custom-call(bf16[4,512,1536]{2,1,0:T(8,128)(2,1)} %get-tuple-element, ...), custom_call_target="tpu_custom_call" | custom-call | flops 1500000000 | bytes 5000000 | tf_op jit(solution)/shard_map/heads_back/pallas_call | solution.py:1325
  484.4 5.4 %fusion.8 = bf16[512,1536]{1,0:T(8,128)(2,1)} fusion(f32[512,1536]{1,0:T(8,128)} %get-tuple-element.37.middle_hbm, bf16[512,1536]{1,0:T(8,128)(2,1)} %get-tuple-element.53, bf16[3,512,1536]{2,1,0:T(8,128)(2,1)} %get-tuple-element.41.branch_hbm), kind=kLoop, calls=%fused_computation.13 | loop fusion | flops 5505024 | bytes 9437184 | tf_op jit(solution)/shard_map/convert_element_type | solution.py:1437
  489.8 0.1 reduce_sum.42
  489.9 0.1 reduce_sum.43
  490.0 1.3 dynamic-slice_divide_fusion
  491.3 0.6 dynamic-slice_divide_fusion.1
  492.0 3.0 fusion.6
  495.0 0.7 copy-done.5
  495.7 3.0 fusion.5
  498.8 0.2 slice_bitcast_fusion.13
  499.0 0.8 pad_maximum_fusion.5
  499.8 0.8 pad_maximum_fusion.8
  500.6 0.8 pad_maximum_fusion.7
  501.4 0.8 maximum_bitcast_fusion.3
  502.3 0.4 slice_bitcast_fusion.1
  502.6 0.9 maximum_bitcast_fusion
  503.6 0.9 pad_maximum_fusion.2
  504.5 0.9 pad_maximum_fusion.1
  (47 shorter events, 0.4 us)
Async XLA Ops:
  0.6 8.3 %copy-start.10 = (bf16[1024,192]{0,1:T(8,128)(2,1)S(1)}, bf16[1024,192]{0,1:T(8,128)(2,1)}, u32[]{:S(2)}) copy-start(bf16[1024,192]{0,1:T(8,128)(2,1)} %param.26) | copy-start | bytes 1179652
  0.7 8.2 %copy-start.9 = (bf16[192,1024]{1,0:T(8,128)(2,1)S(1)}, bf16[192,1024]{1,0:T(8,128)(2,1)}, u32[]{:S(2)}) copy-start(bf16[192,1024]{1,0:T(8,128)(2,1)} %param.25) | copy-start | bytes 1179652
  0.7 8.2 %copy-start.8 = (bf16[192,1024]{1,0:T(8,128)(2,1)S(1)}, bf16[192,1024]{1,0:T(8,128)(2,1)}, u32[]{:S(2)}) copy-start(bf16[192,1024]{1,0:T(8,128)(2,1)} %param.24) | copy-start | bytes 1179652
  0.7 7.3 %copy-start.12 = (bf16[384,192]{0,1:T(8,128)(2,1)S(1)}, bf16[384,192]{0,1:T(8,128)(2,1)}, u32[]{:S(2)}) copy-start(bf16[384,192]{0,1:T(8,128)(2,1)} %param.22) | copy-start | bytes 442372
  8.9 1.4 copy-start.18
  8.9 1.5 copy-start.16
  8.9 1.5 copy-start.17
  9.0 4.1 copy-start
  9.0 4.1 copy-start.13
  484.4 5.4 %copy-start.15 = (f32[48,128]{1,0:T(8,128)S(1)}, f32[48,128]{1,0:T(8,128)}, u32[]{:S(2)}) copy-start(f32[48,128]{1,0:T(8,128)} %get-tuple-element.61) | copy-start | bytes 73732
  484.4 5.5 %copy-start.14 = (f32[48,128]{1,0:T(8,128)S(1)}, f32[48,128]{1,0:T(8,128)}, u32[]{:S(2)}) copy-start(f32[48,128]{1,0:T(8,128)} %get-tuple-element.62) | copy-start | bytes 73732
  484.4 7.5 %copy-start.1 = (bf16[512,1536]{1,0:T(8,128)(2,1)S(1)}, bf16[512,1536]{1,0:T(8,128)(2,1)}, u32[]{:S(2)}) copy-start(bf16[512,1536]{1,0:T(8,128)(2,1)} %tokens_ref.1) | copy-start | bytes 4718596
  484.4 7.5 %copy-start.2 = (bf16[512,1536]{1,0:T(8,128)(2,1)S(1)}, bf16[512,1536]{1,0:T(8,128)(2,1)}, u32[]{:S(2)}) copy-start(bf16[512,1536]{1,0:T(8,128)(2,1)} %get-tuple-element.55) | copy-start | bytes 4718596
  491.9 3.0 copy-start.3
  491.9 3.1 copy-start.4
  491.9 3.8 copy-start.5
  495.7 3.0 copy-start.7
  498.7 2.6 copy-start.11
  498.8 3.5 copy-start.6

commit v4 on v3

--- a/solution.py
+++ b/solution.py
@@ -18,7 +18,7 @@
 LOG2E = 1.4426950408889634
 LANES = 128
 SHARE = 20
-VMEM_BYTES = 60 * 2**20
+VMEM_BYTES = 63 * 2**20
 
 
 def normed(inputs, gain):
@@ -423,7 +423,7 @@
 
 
 def forward_kernel(
-    deep, first_ref, cotangent_ref, tokens_ref, gain_ref, qkv_halves, out_halves, feed_halves,
+    deep, cotangent_ref, tokens_ref, gains_ref, all_halves,
     qkv_spread, out_spread, cosine_ref, sine_ref,
     first_out, qkv_out, heads_out, logs_out, qkv_wide_out, out_wide_out, middle_out, second_out,
     cotangent_out, feed_out, qkv_own_out,
@@ -433,10 +433,16 @@
 ):
     core, z_place = lax.axis_index("c").astype(jnp.int32), lax.axis_index("z").astype(jnp.int32)
     core_beside, x_beside, y_beside = beside()
-    count = first_ref.shape[0]
+    count = tokens_ref.shape[0]
     ring = jnp.int32(deep)
-    z_beside = [{"z": lax.rem(z_place + deep - shift, ring)} for shift in range(deep)]
-    greet([core_beside, x_beside, y_beside] + z_beside[1:])
+    feed_lanes, qkv_lanes, out_lanes = (
+        buffer.shape[-1] for buffer in (feed_out, qkv_buffer, out_buffer)
+    )
+    feed_halves = all_halves.at[:, :, pl.ds(0, feed_lanes)]
+    qkv_halves = all_halves.at[:, :, pl.ds(feed_lanes, qkv_lanes)]
+    out_halves = all_halves.at[:, :, pl.ds(feed_lanes + qkv_lanes, out_lanes)]
+    z_beside = {way: {"z": lax.rem(z_place + deep + way, ring)} for way in (-1, 1)}
+    greet([core_beside, x_beside, y_beside, z_beside[-1], z_beside[1]])
 
     kept = []
     sent = []
@@ -456,55 +462,125 @@
 
     qkv_core = move(qkv_halves.at[1 - core], qkv_buffer.at[0, 0, 1], qkv_sems, 0, core_beside)
     qkv_kept = keep_local(qkv_halves.at[core], qkv_buffer.at[0, 0, 0], 0)
-    first_x = move(first_ref, first_all.at[1], row_sems, 0, x_beside)
+    step_rows = 128
+
+    @pl.loop(0, count // step_rows)
+    def _(step):
+        rows = pl.ds(pl.multiple_of(step * step_rows, step_rows), step_rows)
+        value = tokens_ref[rows, :].astype(jnp.float32)
+        first_all[0, rows, :] = (value * norm_factor(value) * gains_ref[0:1, :]).astype(jnp.bfloat16)
+
+    first_x = move(first_all.at[0], first_all.at[1], row_sems, 0, x_beside)
     out_core = move(out_halves.at[1 - core], out_buffer.at[0, 0, 1], out_sems, 0, core_beside)
     out_kept = keep_local(out_halves.at[core], out_buffer.at[0, 0, 0], 1)
     feed_core = move(feed_halves.at[1 - core], feed_out.at[0, 0, 1], feed_sems, 0, core_beside)
     feed_kept = keep_local(feed_halves.at[core], feed_out.at[0, 0, 0], 2)
-    first_core = move(first_ref, first_all.at[2], row_sems, 1, core_beside)
-    first_kept = keep_local(first_ref, first_all.at[0], 3)
+    first_core = move(first_all.at[0], first_all.at[2], row_sems, 1, core_beside)
     cotangent_kept = keep_local(cotangent_ref, cotangent_out.at[0], 4)
 
-    def open_z(buffer, sems, shifts):
-        return [move(buffer.at[0, 0], buffer.at[0, shift], sems, shift, z_beside[shift]) for shift in shifts]
-
-    def open_y(buffer, sems, shift):
-        return move(buffer.at[0, shift], buffer.at[1, shift], sems, deep + shift, y_beside)
-
-    far = [shift for shift in range(1, deep) if shift in (1, deep - 1)]
-    rest = [shift for shift in range(1, deep) if shift not in far]
-
+    last = deep - 1
+
+    def z_copy(buffer, sems, upward, step, rel):
+        source, target = ((deep - step) % deep, last - step) if upward else (step, step + 1)
+        return pltpu.make_async_remote_copy(
+            src_ref=buffer.at[0, source, rel],
+            dst_ref=buffer.at[0, target, rel],
+            send_sem=sems.at[0, 2 * (1 + upward * last + step) + rel],
+            recv_sem=sems.at[1, 2 * target + rel],
+            device_id=z_beside[1 if upward else -1],
+            device_id_type=pl.DeviceIdType.MESH,
+        )
+
+    def z_sends(upward, step):
+        if upward:
+            return (z_place <= last - 1) & (z_place - step >= 0)
+        return (z_place >= 1) & (z_place + step <= last)
+
+    def z_start(buffer, sems, upward, step, rel):
+        @pl.when(z_sends(upward, step))
+        def _():
+            z_copy(buffer, sems, upward, step, rel).start()
+
+    def open_z(buffer, sems):
+        for rel in range(2):
+            z_start(buffer, sems, False, 0, rel)
+            z_start(buffer, sems, True, 0, rel)
+
+    def y_copy(buffer, sems, slot, rel):
+        return pltpu.make_async_remote_copy(
+            src_ref=buffer.at[0, slot, rel],
+            dst_ref=buffer.at[1, slot, rel],
+            send_sem=sems.at[0, 2 * (2 * deep + slot) + rel],
+            recv_sem=sems.at[1, 2 * (2 * deep + slot) + rel],
+            device_id=y_beside,
+            device_id_type=pl.DeviceIdType.MESH,
+        )
+
+    def open_y(buffer, sems):
+        for rel in range(2):
+            y_copy(buffer, sems, 0, rel).start()
+
+    def z_part(buffer, sems, step, rel):
+        for upward in (False, True):
+            slot = last - step if upward else step + 1
+            arrives = z_place - step - 1 >= 0 if upward else z_place + step + 1 <= last
+
+            @pl.when(arrives)
+            def _(upward=upward, slot=slot):
+                z_copy(buffer, sems, upward, step, rel).wait_recv()
+                if step + 1 < last:
+                    z_start(buffer, sems, upward, step + 1, rel)
+                y_copy(buffer, sems, slot, rel).start()
+
+    def z_step(buffer, sems, step):
+        for rel in range(2):
+            z_part(buffer, sems, step, rel)
+
+    def y_wait(buffer, sems):
+        for slot in range(deep):
+            for rel in range(2):
+                y_copy(buffer, sems, slot, rel).wait_recv()
+
+    def close(buffer, sems):
+        for rel in range(2):
+            for slot in range(deep):
+                y_copy(buffer, sems, slot, rel).wait_send()
+            for upward in (False, True):
+                for step in range(last):
+
+                    @pl.when(z_sends(upward, step))
+                    def _(upward=upward, step=step, rel=rel):
+                        z_copy(buffer, sems, upward, step, rel).wait_send()
+
+    qkv_z, out_z, feed_z = (qkv_buffer, qkv_sems), (out_buffer, out_sems), (feed_out, feed_sems)
     qkv_core.wait_recv()
     qkv_kept.wait()
-    qkv_z = open_z(qkv_buffer, qkv_sems, far + rest)
-    qkv_y = [open_y(qkv_buffer, qkv_sems, 0)]
+    open_z(*qkv_z)
+    open_y(*qkv_z)
     out_core.wait_recv()
     out_kept.wait()
     feed_core.wait_recv()
     feed_kept.wait()
     kept.append(keep_local(qkv_buffer.at[0, 0], qkv_own_out, 13))
-    for shift, copy in zip(far + rest, qkv_z):
-        copy.wait_recv()
-        qkv_y.append(open_y(qkv_buffer, qkv_sems, shift))
-    out_z = open_z(out_buffer, out_sems, far + rest)
-    out_y = [open_y(out_buffer, out_sems, 0)]
+    for step in range(last):
+        z_step(*qkv_z, step)
+        if step == last - 2:
+            open_z(*out_z)
+    open_y(*out_z)
+    for step in range(last):
+        z_step(*out_z, step)
+    open_z(*feed_z)
+    open_y(*feed_z)
     first_x.wait_recv()
     first_far = move(first_all.at[1], first_all.at[3], row_sems, 2, core_beside)
     cotangent_x = move(cotangent_ref, cotangent_out.at[1], row_sems, 3, x_beside)
     cotangent_core = move(cotangent_ref, cotangent_out.at[2], row_sems, 4, core_beside)
-    feed_z = open_z(feed_out, feed_sems, far)
-    for copy in qkv_y:
-        copy.wait_recv()
-    for shift, copy in zip(far + rest, out_z):
-        copy.wait_recv()
-        out_y.append(open_y(out_buffer, out_sems, shift))
-    feed_y = [open_y(feed_out, feed_sems, 0)]
+    y_wait(*qkv_z)
 
     spread_weight(qkv_buffer, qkv_spread, qkv_wide, deep)
     kept.append(keep_local(qkv_wide, qkv_wide_out, 5))
     first_core.wait_recv()
     first_far.wait_recv()
-    first_kept.wait()
     kept.append(keep_local(first_all, first_out, 6))
 
     @pl.loop(0, 8)
@@ -512,8 +588,8 @@
         block, pair = step // 2, lax.rem(step, jnp.int32(2))
         lane0 = pl.multiple_of(pair * 4 * LANES, 4 * LANES)
         product = nn(first_all[block], qkv_wide[:, pl.ds(lane0, 4 * LANES)])
-        rel = lax.rem(block, jnp.int32(2))
-        cosine, sine = cosine_ref[rel], sine_ref[rel]
+        position = lax.rem(lax.axis_index("x").astype(jnp.int32) + block, jnp.int32(2))
+        cosine, sine = cosine_ref[position], sine_ref[position]
         for head in range(4):
             part = product[:, head * LANES : (head + 1) * LANES]
             if head < 3:
@@ -521,16 +597,20 @@
             qkv[block, :, pl.ds(lane0 + head * LANES, LANES)] = part.astype(jnp.bfloat16)
 
     kept.append(keep_local(qkv, qkv_out, 7))
+    z_part(*feed_z, 0, 0)
     logs[...] = jnp.zeros_like(logs)
-
-    @pl.loop(0, 4)
-    def _(step):
-        attend_pair(qkv, heads, logs, keys, values, step // 2, lax.rem(step, jnp.int32(2)))
+    for sequence in range(2):
+
+        @pl.loop(0, 2)
+        def _(pair, sequence=sequence):
+            attend_pair(qkv, heads, logs, keys, values, sequence, pair)
+
+        if sequence == 0:
+            z_part(*feed_z, 0, 1)
 
     kept.append(keep_local(heads, heads_out, 8))
     kept.append(keep_local(logs, logs_out, 9))
-    for copy in out_y:
-        copy.wait_recv()
+    y_wait(*out_z)
     spread_weight(out_buffer, out_spread, out_wide, deep)
     kept.append(keep_local(out_wide, out_wide_out, 10))
 
@@ -544,7 +624,6 @@
     core_far = move(parts.at[3], core_parts.at[1], core_sems, 0, core_beside)
     out_part(1)
     core_far.wait_recv()
-    step_rows = 128
 
     @pl.loop(0, count // step_rows)
     def _(step):
@@ -557,11 +636,8 @@
     out_part(2)
     core_near = move(parts.at[2], core_parts.at[0], core_sems, 2, core_beside)
     out_part(0)
-    for shift, copy in zip(far, feed_z):
-        copy.wait_recv()
-        feed_y.append(open_y(feed_out, feed_sems, shift))
-    feed_z = open_z(feed_out, feed_sems, rest)
     core_near.wait_recv()
+    z_step(*feed_z, 1)
     branch_x.wait_recv()
 
     @pl.loop(0, count // step_rows)
@@ -574,7 +650,7 @@
             + incoming[rows, :].astype(jnp.float32)
         )
         middle[rows, :] = total
-        second[rows, :] = (total * norm_factor(total) * gain_ref[...]).astype(jnp.bfloat16)
+        second[rows, :] = (total * norm_factor(total) * gains_ref[1:2, :]).astype(jnp.bfloat16)
 
     kept.append(keep_local(middle, middle_out, 11))
     kept.append(keep_local(second, second_out.at[0], 12))
@@ -582,22 +658,24 @@
     second_core = move(second, second_out.at[2], row_sems, 6, core_beside)
     cotangent_x.wait_recv()
     cotangent_far = move(cotangent_out.at[1], cotangent_out.at[3], row_sems, 7, core_beside)
-    for shift, copy in zip(rest, feed_z):
-        copy.wait_recv()
-        feed_y.append(open_y(feed_out, feed_sems, shift))
+    z_step(*feed_z, 2)
     second_x.wait_recv()
     second_far = move(second_out.at[1], second_out.at[3], row_sems, 8, core_beside)
-    for copy in [second_core, second_far, cotangent_core, cotangent_far] + feed_y:
+    for copy in (second_core, second_far, cotangent_core, cotangent_far):
         copy.wait_recv()
+    y_wait(*feed_z)
     for copy in kept + [cotangent_kept]:
         copy.wait()
     for copy in sent:
         copy.wait_send()
-
-
-def forward(deep, first, cotangent, tokens, gain, qkv_halves, out_halves, feed_halves, spreads, cosine, sine):
-    count, width = first.shape
-    part = feed_halves.shape[1]
+    for which in (qkv_z, out_z, feed_z):
+        close(*which)
+
+
+def forward(deep, cotangent, tokens, gains, halves, sizes, spreads, cosine, sine):
+    count, width = tokens.shape
+    part = halves.shape[1]
+    feed_size, qkv_size, out_size = sizes
 
     def shape(*dims, kind=jnp.bfloat16):
         return jax.ShapeDtypeStruct(dims, kind)
@@ -616,13 +694,13 @@
         shape(count, width, kind=jnp.float32),
         shape(4, count, width),
         shape(4, count, width),
-        shape(2, deep, 2, part, feed_halves.shape[2]),
-        shape(2, part, qkv_halves.shape[2]),
+        shape(2, deep, 2, part, feed_size),
+        shape(2, part, qkv_size),
     )
     scratch = [
         room(4, count, width),
-        room(2, deep, 2, part, qkv_halves.shape[2]),
-        room(2, deep, 2, part, out_halves.shape[2]),
+        room(2, deep, 2, part, qkv_size),
+        room(2, deep, 2, part, out_size),
         room(width, qkv_lanes),
         room(width, out_lanes),
         room(4, count, qkv_lanes),
@@ -638,21 +716,21 @@
         room(count, width),
         pltpu.SemaphoreType.DMA((14,)),
         pltpu.SemaphoreType.DMA((2, 9)),
-        pltpu.SemaphoreType.DMA((2, 2 * deep)),
-        pltpu.SemaphoreType.DMA((2, 2 * deep)),
-        pltpu.SemaphoreType.DMA((2, 2 * deep)),
+        pltpu.SemaphoreType.DMA((2, 6 * deep)),
+        pltpu.SemaphoreType.DMA((2, 6 * deep)),
+        pltpu.SemaphoreType.DMA((2, 6 * deep)),
         pltpu.SemaphoreType.DMA((2, 3)),
     ]
     return pl.pallas_call(
         functools.partial(forward_kernel, deep),
         out_shape=outs,
-        in_specs=[vmem_spec(), hbm_spec()] + [vmem_spec()] * 2 + [hbm_spec()] * 3 + [vmem_spec()] * 4,
+        in_specs=[hbm_spec(), vmem_spec(), vmem_spec(), hbm_spec()] + [vmem_spec()] * 4,
         out_specs=(hbm_spec(),) * len(outs),
         scratch_shapes=scratch,
         compiler_params=vmem_params(collective_id=1, has_side_effects=True),
         cost_estimate=cost(flops=20 * 10**9, bytes_accessed=10**8, transcendentals=10**7),
         name="forward",
-    )(first, cotangent, tokens, gain, qkv_halves, out_halves, feed_halves, *spreads, cosine, sine)
+    )(cotangent, tokens, gains, halves, *spreads, cosine, sine)
 
 
 EARLY = 6
@@ -672,18 +750,24 @@
         )
 
 
+def ahead(deep):
+    z_place = lax.axis_index("z").astype(jnp.int32)
+    return [{"z": lax.rem(z_place + shift, jnp.int32(deep))} for shift in range(deep)]
+
+
 def pieces_of(deep):
     return [(piece, shift) for piece in range(3) for shift in range(deep)]
 
 
 def feed_back_kernel(
     deep, rows_hbm, grads_hbm, chunks, middle_hbm, gain_ref,
-    grad_middle_out, grad_attention_out, branch_out, sent_out, own_out, arrived_out,
+    grad_middle_out, grad_attention_out, branch_out, sent_out, own_out, sum_out, arrived_out,
     gate, up, down, rows, grads, hidden, grad_gate, grad_up, parts, landing, incoming, middle, stage,
-    load_sems, weight_sems, store_sems, early_sems, core_sems, x_sems, y_sems,
+    early_y, load_sems, weight_sems, store_sems, sum_sems, early_sems, core_sems, x_sems, y_sems, z_sems,
 ):
     core_beside, x_beside, y_beside = beside()
-    greet([core_beside, x_beside, y_beside])
+    z_ahead = ahead(deep)
+    greet([core_beside, x_beside, y_beside] + z_ahead[1:])
     blocks, count, width = rows.shape
     half = gate.shape[1] // 2
     part = chunks.shape[3]
@@ -758,15 +842,14 @@
                 for copy in here:
                     copy.wait()
         inner(block)
-        outer(block)
+        if block in (3, 1):
+            outer(block)
         if block == 3:
             far = move(parts.at[3], landing.at[1], core_sems, 0, core_beside)
         if block == 1:
             far.wait_recv()
             add_rows(parts.at[1], landing.at[1])
             across = move(parts.at[1], incoming, x_sems, 0, x_beside)
-        if block == 2:
-            near = move(parts.at[2], landing.at[0], core_sems, 1, core_beside)
 
     sources = ((grads, hidden), (rows, grad_gate), (rows, grad_up))
 
@@ -774,11 +857,14 @@
         left, right = sources[piece]
         row = ring_row(shift, deep, piece_rows)
         lanes = slice(side * half, (side + 1) * half)
-        product = transposed_times(
+        return transposed_times(
             left[:, :, pl.ds(row, piece_rows)].reshape(blocks * count, piece_rows),
             right[:, :, lanes].reshape(blocks * count, half),
         )
-        stage[piece, pl.ds(row, piece_rows), :] = product.astype(jnp.bfloat16)
+
+    def weight_stage(piece, side, shift):
+        row = ring_row(shift, deep, piece_rows)
+        stage[piece, pl.ds(row, piece_rows), :] = weight_part(piece, side, shift).astype(jnp.bfloat16)
 
     early = pieces_of(deep)[:EARLY]
     arrivals, stores, pending = [], [], []
@@ -786,29 +872,29 @@
     def flush():
         for index, store, target in pending:
             store.wait()
-            arrivals.append(move(target, arrived_out.at[index], y_sems, index, y_beside))
+            arrivals.append(move(target, early_y.at[index], y_sems, index, y_beside))
         pending.clear()
 
-    for piece in range(3):
-        mine = [pair for pair in early if pair[0] == piece]
-        for pair in mine:
-            weight_part(piece, 1, pair[1])
-            flush()
-            rows_here = pl.ds(ring_row(pair[1], deep, piece_rows), piece_rows)
-            index = early.index(pair)
-            target = sent_out.at[piece, rows_here, :]
-            pending.append((index, load(stage.at[piece, rows_here, :], target, early_sems.at[index]), target))
-        for shift in range(len(mine), deep):
-            weight_part(piece, 1, shift)
+    def send_piece(piece):
+        for shift in range(deep):
+            weight_stage(piece, 1, shift)
             flush()
             rows_here = pl.ds(ring_row(shift, deep, piece_rows), piece_rows)
-            stores.append(
-                load(
-                    stage.at[piece, rows_here, :],
-                    sent_out.at[piece, rows_here, :],
-                    early_sems.at[piece * deep + shift],
-                )
-            )
+            target = sent_out.at[piece, rows_here, :]
+            store = load(stage.at[piece, rows_here, :], target, early_sems.at[piece * deep + shift])
+            if (piece, shift) in early:
+                pending.append((early.index((piece, shift)), store, target))
+            else:
+                stores.append(store)
+
+    send_piece(0)
+    outer(2)
+    flush()
+    near = move(parts.at[2], landing.at[0], core_sems, 1, core_beside)
+    outer(0)
+    send_piece(1)
+    send_piece(2)
+    flush()
     late_stores = list(stores)
     near.wait_recv()
     middle_load.wait()
@@ -823,7 +909,7 @@
             + landing[0, tile, :].astype(jnp.float32)
             + incoming[tile, :].astype(jnp.float32)
         )
-        total = grads[0, tile, :].astype(jnp.float32) + norm_back(middle[tile, :], gain_ref[...], grad)
+        total = grads[0, tile, :].astype(jnp.float32) + norm_back(middle[tile, :], gain_ref[1:2, :], grad)
         middle[tile, :] = total
         incoming[tile, :] = total.astype(jnp.bfloat16)
 
@@ -832,6 +918,22 @@
     stores.append(load(incoming, grad_attention_out.at[0], store_sems.at[0]))
     stores.append(load(middle, grad_middle_out, store_sems.at[3]))
 
+    hops = []
+
+    def join_early(pairs):
+        for piece, shift in pairs:
+            index = early.index((piece, shift))
+            product = weight_part(piece, 0, shift)
+            arrivals[index].wait_recv()
+            early_y[index] = (product + early_y[index].astype(jnp.float32)).astype(jnp.bfloat16)
+            if piece == 0 and shift:
+                hops.append(
+                    move(early_y.at[index], arrived_out.at[shift - 1], z_sems, shift, z_ahead[shift])
+                )
+            else:
+                stores.append(load(early_y.at[index], sum_out.at[index], sum_sems.at[index]))
+
+    join_early(early[:-2])
     far.wait_send()
     across.wait_send()
     near.wait_send()
@@ -850,28 +952,34 @@
     branch(1)
     branch_far.wait_recv()
     add_rows(parts.at[1], landing.at[1])
-    stores.append(load(parts.at[1], branch_out.at[1], store_sems.at[4]))
+    stores.append(load(parts.at[1], branch_out.at[1], store_sems.at[7]))
     branch(0)
-    stores.append(load(parts.at[0], branch_out.at[0], store_sems.at[5]))
+    stores.append(load(parts.at[0], branch_out.at[0], store_sems.at[8]))
     branch_near.wait_recv()
-    stores.append(load(landing.at[0], branch_out.at[2], store_sems.at[6]))
+    stores.append(load(landing.at[0], branch_out.at[2], store_sems.at[9]))
     for copy in late_stores:
         copy.wait()
     for piece in range(3):
-
-        @pl.loop(0, deep)
-        def _(shift, piece=piece):
-            weight_part(piece, 0, shift)
-
-        stores.append(load(stage.at[piece], own_out.at[piece], store_sems.at[7 + piece]))
+        for shift in range(deep):
+            if (piece, shift) not in early:
+                weight_stage(piece, 0, shift)
+                rows_here = pl.ds(ring_row(shift, deep, piece_rows), piece_rows)
+                stores.append(
+                    load(
+                        stage.at[piece, rows_here, :],
+                        own_out.at[piece, rows_here, :],
+                        early_sems.at[(3 + piece) * deep + shift],
+                    )
+                )
+    join_early(early[-2:])
     attention_x.wait_recv()
     attention_far = move(grad_attention_out.at[1], grad_attention_out.at[3], core_sems, 5, core_beside)
     attention_far.wait_recv()
-    for copy in arrivals:
+    for copy in hops:
         copy.wait_recv()
     for copy in stores[len(late_stores) :]:
         copy.wait()
-    for copy in arrivals:
+    for copy in arrivals + hops:
         copy.wait_send()
     for copy in (attention_x, attention_core, branch_far, branch_near, attention_far):
         copy.wait_send()
@@ -895,6 +1003,7 @@
         shape(3, width, half),
         shape(3, width, half),
         shape(EARLY, 2 * part, half),
+        shape(deep - 1, 2 * part, half),
     )
     dma = pltpu.SemaphoreType.DMA
     return pl.pallas_call(
@@ -906,8 +1015,8 @@
         + [room(blocks, count, width)] * 2
         + [room(blocks, count, 2 * half)] * 3
         + [room(blocks, count, width), room(2, count, width), room(count, width)]
-        + [room(count, width, kind=jnp.float32), room(3, width, half)]
-        + [dma((2, 5)), dma((3, 2, deep, 2)), dma((10,)), dma((3 * deep,)), dma((2, 6)), dma((2, 2)), dma((2, EARLY))],
+        + [room(count, width, kind=jnp.float32), room(3, width, half), room(EARLY, 2 * part, half)]
+        + [dma((2, 5)), dma((3, 2, deep, 2)), dma((10,)), dma((EARLY,)), dma((6 * deep,)), dma((2, 6)), dma((2, 2)), dma((2, EARLY)), dma((2, EARLY))],
         compiler_params=vmem_params(collective_id=2, has_side_effects=True),
         cost_estimate=cost(flops=80 * 10**9, bytes_accessed=10**8, transcendentals=10**7),
         name="feed_back",
@@ -967,7 +1076,8 @@
         grad_queries = span(slice(before, before + TILE), True)
         if before:
             grad_queries = grad_queries + span(slice(0, before), False)
-        cosine, sine = cosine_ref[rel, rows, :], -sine_ref[rel, rows, :]
+        position, table_rows = before // count, slice(before % count, before % count + TILE)
+        cosine, sine = cosine_ref[position, table_rows, :], -sine_ref[position, table_rows, :]
         for head in range(2):
             piece = grad_queries[head * TILE : (head + 1) * TILE] * factor
             grad_qkv[block, rows, pl.ds(lane0 + head * LANES, LANES)] = turn(piece, cosine, sine).astype(
@@ -988,27 +1098,26 @@
         position = lax.rem(x_place + rel, jnp.int32(2))
         rows = pl.ds(pl.multiple_of(position * count, count), count)
         grad_qkv[block, :, pl.ds(lane0 + 2 * LANES, LANES)] = turn(
-            grad_keys[rows, :] * factor, cosine_ref[rel], -sine_ref[rel]
+            grad_keys[rows, :] * factor, cosine_ref[position], -sine_ref[position]
         ).astype(jnp.bfloat16)
         grad_qkv[block, :, pl.ds(lane0 + 3 * LANES, LANES)] = grad_values[rows, :].astype(jnp.bfloat16)
 
 
 def heads_back_kernel(
     deep, grad_attention_hbm, qkv_hbm, heads_hbm, logs_hbm, first_hbm, qkv_wide_hbm, out_wide_hbm,
-    branch_hbm, sent_hbm, own_hbm, early_hbm, chunks_hbm, qkv_own_hbm,
+    branch_hbm, sent_hbm, own_hbm, sum_hbm, arrived_hbm, chunks_hbm, qkv_own_hbm,
     cosine_ref, sine_ref, qkv_spread, out_spread,
     first_part, first_core, first_x, branch_x, feed_final, qkv_final, out_final, first_gain_out, second_gain_out,
     grad_attention, qkv, heads, grad_heads, logs, grad_qkv, qkv_wide, out_wide, keys, values, grad_keys,
-    grad_values, landing, feed_sum, feed_y, feed_z, out_sent, out_sum, out_y, out_z, qkv_sent, qkv_sum, qkv_y,
+    grad_values, slots, landing, feed_sum, feed_y, feed_z, out_sent, out_sum, out_y, out_z, qkv_sent, qkv_sum, qkv_y,
     qkv_z, feed_last, qkv_last, out_last, feed_weight, qkv_weight, gain_part, gain_in, gain_total,
     load_sems, own_sems, tile_sems, core_sems, x_sems, y_sems, z_sems, gain_sems,
 ):
     blocks, count, width = grad_attention.shape
     core_beside, x_beside, y_beside = beside()
-    core, z_place = lax.axis_index("c").astype(jnp.int32), lax.axis_index("z").astype(jnp.int32)
+    core = lax.axis_index("c").astype(jnp.int32)
     across, along = lax.axis_index("x").astype(jnp.int32), lax.axis_index("y").astype(jnp.int32)
-    ring = jnp.int32(deep)
-    z_ahead = [{"z": lax.rem(z_place + shift, ring)} for shift in range(deep)]
+    z_ahead = ahead(deep)
     cube = {
         (rel, up, over): {"c": (core + rel) % 2, "y": (along + up) % 2, "x": (across + over) % 2}
         for rel in range(2)
@@ -1033,7 +1142,7 @@
         sent.append(copy)
         return copy
 
-    early, late = pieces_of(deep)[:EARLY], pieces_of(deep)[EARLY:]
+    late = pieces_of(deep)[EARLY:]
     attention_load = load(grad_attention_hbm, grad_attention, load_sems.at[0])
     out_load = load(out_wide_hbm, out_wide, load_sems.at[1])
     heads_load = load(heads_hbm, heads, load_sems.at[2])
@@ -1049,16 +1158,27 @@
     qkv_load = load(qkv_hbm, qkv, load_sems.at[3])
     logs_load = load(logs_hbm, logs, load_sems.at[4])
     wide_load = load(qkv_wide_hbm, qkv_wide, load_sems.at[5])
-    own_loads = {}
-    early_loads = {}
+    own_loads, z_copies = {}, {}
+    early_loads = []
     for index, (piece, shift) in enumerate(pieces_of(deep)):
-        row = ring_row(shift, deep, piece_rows)
-        own_loads[piece, shift] = load(
-            own_hbm.at[piece, pl.ds(row, piece_rows), :], feed_sum.at[piece, shift], own_sems.at[0, index]
-        )
-        if (piece, shift) in early:
-            early_loads[piece, shift] = load(
-                early_hbm.at[index], feed_y.at[piece, shift], own_sems.at[1, index]
+        if (piece, shift) in late:
+            row = ring_row(shift, deep, piece_rows)
+            own_loads[piece, shift] = load(
+                own_hbm.at[piece, pl.ds(row, piece_rows), :], feed_sum.at[piece, shift], own_sems.at[0, index]
+            )
+        elif shift == 0:
+            early_loads.append(load(sum_hbm.at[index], feed_sum.at[piece, 0], own_sems.at[1, index]))
+        elif piece == 0:
+            early_loads.append(
+                load(arrived_hbm.at[shift - 1], feed_z.at[piece, shift - 1], own_sems.at[1, index])
+            )
+        else:
+            z_copies[piece, shift] = move(
+                sum_hbm.at[index],
+                feed_z.at[piece, shift - 1],
+                z_sems,
+                piece * (deep - 1) + shift - 1,
+                z_ahead[shift],
             )
     weight_loads = [
         load(chunks_hbm.at[0, 0, :, :, pl.ds(0, 2 * half)], feed_weight, load_sems.at[6]),
@@ -1079,20 +1199,6 @@
         right = right[:, :, side * size : (side + 1) * size].reshape(blocks * count, size)
         product = transposed_times(left.reshape(blocks * count, piece_rows), right)
         return times_transposed(product.astype(jnp.bfloat16), spread[...]).astype(jnp.bfloat16)
-
-    y_index = len(late)
-    out_copies = []
-    for shift in range(deep):
-        row = ring_row(shift, deep, piece_rows)
-        out_sent[shift] = weight_tile(grad_attention[:, :, pl.ds(row, piece_rows)], heads, out_spread, 1)
-        out_copies.append(move(out_sent.at[shift], out_y.at[shift], y_sems, y_index + shift, y_beside))
-
-    @pl.loop(0, deep)
-    def _(shift):
-        row = ring_row(shift, deep, piece_rows)
-        out_sum[shift] = weight_tile(grad_attention[:, :, pl.ds(row, piece_rows)], heads, out_spread, 0)
-
-    z_copies = {}
 
     def join_piece(name, number, total, arrived, target, shift):
         add_rows(total.at[shift], arrived.at[shift])
@@ -1105,24 +1211,20 @@
         own_loads[piece, shift].wait()
         join_piece(piece, piece, feed_sum.at[piece], feed_y.at[piece], feed_z.at[piece], shift)
 
-    for pair in early:
-        early_loads[pair].wait()
-        join_feed(*pair)
+    def join_feed_late(index):
+        late_copies[index].wait_recv()
+        join_feed(*late[index])
 
     qkv_load.wait()
     logs_load.wait()
     for sequence in range(2):
 
-        @pl.loop(0, 2)
-        def _(pair, sequence=sequence):
+        for pair in range(2):
             attend_back_pair(
                 qkv, grad_heads, heads, logs, cosine_ref, sine_ref, grad_qkv, keys, values, grad_keys,
                 grad_values, sequence, pair,
             )
-
-        for index in range(sequence * 2, sequence * 2 + 2):
-            late_copies[index].wait_recv()
-            join_feed(*late[index])
+            join_feed_late(2 * sequence + pair)
     wide_load.wait()
 
     def first_tile(shift):
@@ -1140,20 +1242,36 @@
         @pl.loop(0, width // 512)
         def _(step):
             lanes = pl.ds(pl.multiple_of(step * 512, 512), 512)
-            grad_attention[block, :, lanes] = times_transposed(grad_qkv[block], qkv_wide[lanes, :]).astype(
+            slots[block % 3, :, lanes] = times_transposed(grad_qkv[block], qkv_wide[lanes, :]).astype(
                 jnp.bfloat16
             )
 
     first_piece(3)
-    core_far = move(grad_attention.at[3], landing, core_sems, 0, core_beside)
+    core_far = move(slots.at[0], landing, core_sems, 0, core_beside)
     first_piece(1)
     core_far.wait_recv()
-    add_rows(grad_attention.at[1], landing)
-    x_copy = move(grad_attention.at[1], first_x, x_sems, 1, x_beside)
+    add_rows(slots.at[1], landing)
+    x_copy = move(slots.at[1], first_x, x_sems, 1, x_beside)
     first_piece(2)
-    core_near = move(grad_attention.at[2], first_core, core_sems, 1, core_beside)
+    core_near = move(slots.at[2], first_core, core_sems, 1, core_beside)
+    core_far.wait_send()
+    sent[:] = [copy for copy in sent if copy is not core_far]
     first_piece(0)
-    first_store = load(grad_attention.at[0], first_part, load_sems.at[8])
+    first_store = load(slots.at[0], first_part, load_sems.at[8])
+    join_feed_late(4)
+    y_index = len(late)
+    out_copies = []
+    for shift in range(deep):
+        row = ring_row(shift, deep, piece_rows)
+        out_sent[shift] = weight_tile(grad_attention[:, :, pl.ds(row, piece_rows)], heads, out_spread, 1)
+        out_copies.append(move(out_sent.at[shift], out_y.at[shift], y_sems, y_index + shift, y_beside))
+
+    @pl.loop(0, deep)
+    def _(shift):
+        row = ring_row(shift, deep, piece_rows)
+        out_sum[shift] = weight_tile(grad_attention[:, :, pl.ds(row, piece_rows)], heads, out_spread, 0)
+
+    join_feed_late(5)
 
     qkv_copies = []
     y_index += deep
@@ -1167,9 +1285,6 @@
         if shift + 2 < deep:
             first_loads.append(first_tile(shift + 2))
 
-    for index in range(4, len(late)):
-        late_copies[index].wait_recv()
-        join_feed(*late[index])
     for shift in range(deep):
         out_copies[shift].wait_recv()
         join_piece("out", 3, out_sum, out_y, out_z, shift)
@@ -1178,7 +1293,8 @@
 
     def finish(name, number, total, arrived, last, final, weights):
         for shift in range(1, deep):
-            z_copies[name, shift].wait_recv()
+            if (name, shift) in z_copies:
+                z_copies[name, shift].wait_recv()
         size = total.shape[2]
         sums = []
         for rel in range(2):
@@ -1222,7 +1338,7 @@
         gain_total[which] = value
         return load(gain_total.at[which], output, load_sems.at[9 + which])
 
-    for copy in weight_loads:
+    for copy in weight_loads + early_loads:
         copy.wait()
     finish(0, 0, feed_sum.at[0], feed_z.at[0], feed_last.at[0], feed_final.at[0], None)
     gate_sums = finish(
@@ -1253,8 +1369,8 @@
 
 
 def heads_back(
-    deep, grad_attention, qkv, heads, logs, first, qkv_wide, out_wide, branch, sent, own, early, chunks, qkv_own,
-    cosine, sine, spreads,
+    deep, grad_attention, qkv, heads, logs, first, qkv_wide, out_wide, branch, sent, own, sums, arrived, chunks,
+    qkv_own, cosine, sine, spreads,
 ):
     blocks, count, width = grad_attention.shape
     part, half = chunks.shape[3], chunks.shape[4] // 3
@@ -1293,6 +1409,7 @@
         room(2 * count, LANES),
         room(2 * count, LANES, kind=wide),
         room(2 * count, LANES, kind=wide),
+        room(3, count, width),
         room(count, width),
         room(3, deep, rows, half),
         room(3, deep, rows, half),
@@ -1325,32 +1442,28 @@
     return pl.pallas_call(
         functools.partial(heads_back_kernel, deep),
         out_shape=outs,
-        in_specs=[hbm_spec()] * 13 + [vmem_spec()] * 4,
+        in_specs=[hbm_spec()] * 14 + [vmem_spec()] * 4,
         out_specs=(hbm_spec(),) * len(outs),
         scratch_shapes=scratch,
         compiler_params=vmem_params(collective_id=3, has_side_effects=True),
         cost_estimate=cost(flops=30 * 10**9, bytes_accessed=10**8, transcendentals=10**7),
         name="heads_back",
     )(
-        grad_attention, qkv, heads, logs, first, qkv_wide, out_wide, branch, sent, own, early, chunks, qkv_own,
-        cosine, sine, *spreads,
-    )
-
-
-def tables(rows, x_place):
+        grad_attention, qkv, heads, logs, first, qkv_wide, out_wide, branch, sent, own, sums, arrived, chunks,
+        qkv_own, cosine, sine, *spreads,
+    )
+
+
+def tables(rows):
     lane = np.arange(LANES)
     entry = lane % (LANES // 2)
-    live = (entry < HD // 2).astype(np.float32)
-    sign = np.where(lane < LANES // 2, -1.0, 1.0).astype(np.float32) * live
-    pair_entry = np.where(entry < HD // 2, entry, 0).astype(np.float32)
-    inverse = THETA ** (-2.0 * jnp.asarray(pair_entry) / HD)
-    both = []
-    for rel in range(2):
-        first = lax.rem(x_place + rel, jnp.int32(2)) * rows
-        position = (first + jnp.arange(rows, dtype=jnp.int32)).astype(jnp.float32)
-        both.append(position[:, None] * inverse[None, :])
-    angles = jnp.stack(both)
-    return jnp.cos(angles) * live, jnp.sin(angles) * sign
+    live = (entry < HD // 2).astype(np.float64)
+    sign = np.where(lane < LANES // 2, -1.0, 1.0) * live
+    inverse = np.where(live > 0, THETA ** (-2.0 * entry / HD), 0.0).astype(np.float32)
+    position = np.arange(2 * rows, dtype=np.float32)
+    angles = (position[:, None] * inverse[None, :]).astype(np.float32).astype(np.float64)
+    both = (np.cos(angles) * live, np.sin(angles) * sign)
+    return tuple(jnp.asarray(table.astype(np.float32).reshape(2, rows, LANES)) for table in both)
 
 
 def norm_factor(rows):
@@ -1387,11 +1500,10 @@
     down_weight,
 ):
     deep = lax.axis_size("z")
-    z_place, core, x_place = (lax.axis_index(name).astype(jnp.int32) for name in ("z", "c", "x"))
+    z_place, core = (lax.axis_index(name).astype(jnp.int32) for name in ("z", "c"))
     rows = tokens.shape[0]
     depth_place = z_place * 2 + core
     own_rows = tokens.astype(jnp.float32)
-    first_normed = (own_rows * norm_factor(own_rows) * first_gain).astype(jnp.bfloat16)
     out_turned, down_turned = out_weight.T, down_weight.T
 
     def halves(*weights):
@@ -1405,29 +1517,34 @@
         return result
 
     spreads = (spread_heads(3, 1), spread_heads(0, 2))
-    cosine, sine = tables(rows, x_place)
+    cosine, sine = tables(rows)
+    gains = jnp.stack([first_gain, second_gain])
     (
         first_all, qkv_all, heads_all, logs_all, qkv_weight, out_wide, middle, second_all, cotangent_all, chunks, qkv_own,
     ) = forward(
         deep,
-        first_normed,
         cotangent,
         tokens,
-        second_gain[None],
-        jnp.stack(halves(query_weight, key_weight, value_weight)),
-        jnp.stack(halves(out_turned)),
-        jnp.stack(halves(gate_weight, up_weight, down_turned)),
+        gains,
+        jnp.stack(
+            halves(gate_weight, up_weight, down_turned, query_weight, key_weight, value_weight, out_turned)
+        ),
+        (
+            gate_weight.shape[1] * 3 // 2,
+            query_weight.shape[1] // 2 + key_weight.shape[1],
+            out_turned.shape[1] // 2,
+        ),
         spreads,
         cosine,
         sine,
     )
-    grad_middle, grad_attention, branch, sent, own, early = feed_back(
-        deep, second_all, cotangent_all, chunks, middle, second_gain[None]
+    grad_middle, grad_attention, branch, sent, own, sums, arrived = feed_back(
+        deep, second_all, cotangent_all, chunks, middle, gains
     )
     first_part, first_core, first_x, branch_x, feed_final, qkv_final, out_final, first_lanes, second_lanes = (
         heads_back(
             deep, grad_attention, qkv_all, heads_all, logs_all, first_all, qkv_weight, out_wide, branch, sent,
-            own, early, chunks, qkv_own, cosine, sine, spreads,
+            own, sums, arrived, chunks, qkv_own, cosine, sine, spreads,
         )
     )
 
@@ -1468,7 +1585,7 @@
     def run(tokens, cotangent, *weights):
         fits = (
             width == 4
-            and depth % 2 == 0
+            and depth == 8
             and tokens.shape[0] * 2 == SEQ_LEN * depth * width
             and weights[2].shape[1] == 2 * width * HD
             and weights[1].shape[1] == 4 * width * HD

time: 515 us -> 435 us (0.84)
  the two profiles are of different devices: /device:TPU:13 before, /device:TPU:11 now
where the time goes in v4:
time: 435 us; the launch traced here: 428 us
  Pallas kernels  404 us (93%)
  other arithmetic  15.7 us (4%)
  local copies, waits for them, and re-layouts  7.71 us (2%)
    pallas_call x1, Pallas kernels, forward(): pl.pallas_call(functools.partial(forward_kernel, deep), out_shape=outs, i...  167 us
    pallas_call x1, Pallas kernels, heads_back(): pl.pallas_call(functools.partial(heads_back_kernel, deep), out_shape=outs...  128 us
    pallas_call x1, Pallas kernels, feed_back(): pl.pallas_call(functools.partial(feed_back_kernel, deep), out_shape=outs,...  109 us

profile of v4, /device:TPU:11, one launch (start us, length us, event | category | flops | bytes accessed | tf_op | source)
XLA Modules:
  0.0 428.5 jit_solution(5091583922298781986)
XLA Ops:
  0.6 1.3 fusion.7
  1.9 1.2 fusion.10
  3.1 1.1 fusion.12
  4.2 1.1 fusion.9
  5.2 0.0 copy-start.9
  5.2 0.0 copy-start.12
  5.2 0.3 concatenate.27
  5.6 0.3 concatenate.28
  5.9 1.4 pad_maximum_fusion.all_halves
  7.3 0.6 pad_maximum_fusion.6.gains_ref.gain_ref
  7.9 166.8 %forward.1 = (bf16[4,512,1536]{2,1,0:T(8,128)(2,1)}, bf16[4,512,1024]{2,1,0:T(8,128)(2,1)}, bf16[4,512,512]{2,1,0:T(8,128)(2,1)}, f32[4,512,128]{2,1,0:T(8,128)}...) custom-call(bf16[512,1536]{1,0:T(8,128)(2,1)} %cotangent_ref.1, ...), custom_call_target="tpu_custom_call" | custom-call | flops 1000000000 | bytes 5000000 | tf_op jit(solution)/shard_map/forward/pallas_call | solution.py:724
  174.7 109.0 %feed_back.1 = (f32[512,1536]{1,0:T(8,128)}, bf16[4,512,1536]{2,1,0:T(8,128)(2,1)}, bf16[3,512,1536]{2,1,0:T(8,128)(2,1)}, bf16[3,1536,512]{2,1,0:T(8,128)(2,1)}...) custom-call(bf16[4,512,1536]{2,1,0:T(8,128)(2,1)} %get-tuple-element.39.rows_hbm, ...), custom_call_target="tpu_custom_call" | custom-call | flops 4000000000 | bytes 5000000 | tf_op jit(solution)/shard_map/feed_back/pallas_call | solution.py:1009
  283.7 128.2 %heads_back.1 = (bf16[512,1536]{1,0:T(8,128)(2,1)}, bf16[512,1536]{1,0:T(8,128)(2,1)}, bf16[512,1536]{1,0:T(8,128)(2,1)}, bf16[512,1536]{1,0:T(8,128)(2,1)}, f32...) custom-call(bf16[4,512,1536]{2,1,0:T(8,128)(2,1)} %get-tuple-element, ...), custom_call_target="tpu_custom_call" | custom-call | flops 1500000000 | bytes 5000000 | tf_op jit(solution)/shard_map/heads_back/pallas_call | solution.py:1442
  412.0 1.8 slice_bitcast_fusion.1
  413.8 0.9 maximum_bitcast_fusion
  414.8 0.9 pad_maximum_fusion.2
  415.7 0.9 pad_maximum_fusion.1
  416.7 0.8 maximum_bitcast_fusion.1
  417.5 0.2 slice_bitcast_fusion.11
  417.7 0.8 pad_maximum_fusion.5
  418.5 0.8 pad_maximum_fusion.4
  419.3 0.8 pad_maximum_fusion.3
  420.2 0.0 slice-start
  420.2 1.3 fusion
  421.5 0.0 slice-start.1
  421.5 3.0 fusion.3
  424.5 0.4 copy-done.6
  424.9 2.0 fusion.6
  426.9 0.1 reduce_sum.39
  427.0 0.6 dynamic-slice_divide_fusion
  427.6 0.1 reduce_sum.38
  427.7 0.6 dynamic-slice_divide_fusion.1
  (32 shorter events, 0.1 us)
Async XLA Ops:
  5.2 2.0 copy-start.9
  5.2 2.0 copy-start.12
  413.8 2.9 copy-start.8
  413.8 3.7 copy-start.7
  414.8 5.4 %copy-start.4 = (bf16[512,1536]{1,0:T(8,128)(2,1)S(1)}, bf16[512,1536]{1,0:T(8,128)(2,1)}, u32[]{:S(2)}) copy-start(bf16[512,1536]{1,0:T(8,128)(2,1)} %get-tuple-element.59) | copy-start | bytes 4718596
  415.7 4.5 %copy-start = (bf16[512,1536]{1,0:T(8,128)(2,1)S(1)}, bf16[512,1536]{1,0:T(8,128)(2,1)}, u32[]{:S(2)}) copy-start(bf16[512,1536]{1,0:T(8,128)(2,1)} %tokens_ref.1) | copy-start | bytes 4718596
  415.7 4.5 %copy-start.2 = (bf16[512,1536]{1,0:T(8,128)(2,1)S(1)}, bf16[512,1536]{1,0:T(8,128)(2,1)}, u32[]{:S(2)}) copy-start(bf16[512,1536]{1,0:T(8,128)(2,1)} %get-tuple-element.57) | copy-start | bytes 4718596
  415.7 4.5 %copy-start.3 = (bf16[512,1536]{1,0:T(8,128)(2,1)S(1)}, bf16[512,1536]{1,0:T(8,128)(2,1)}, u32[]{:S(2)}) copy-start(bf16[512,1536]{1,0:T(8,128)(2,1)} %get-tuple-element.58) | copy-start | bytes 4718596
  419.3 2.2 copy-start.5
  420.2 4.3 %slice-start = ((s8[4718592]{0:T(1024)(128)(4,1)}), s8[4194304]{0:T(1024)(128)(4,1)S(1)}, s32[]{:S(2)}) async-start(s8[4718592]{0:T(1024)(128)(4,1)} %bitcast.42), calls=%async_computation | async-start | bytes 8388608
  421.5 3.0 slice-start.1
  421.5 3.0 copy-start.1
  421.5 3.4 copy-start.6
  424.9 2.0 copy-start.11
  424.9 2.7 copy-start.10

commit v5 on v4

--- a/solution.py
+++ b/solution.py
@@ -313,6 +313,7 @@
 
 
 TILE = 256
+WIDE = 768
 
 
 def diagonal_mask():
@@ -375,14 +376,13 @@
     lane0 = pl.multiple_of(pair * 4 * LANES, 4 * LANES)
     mask = diagonal_mask()
     scale = HD ** (-0.5) * LOG2E
-    for rel in range(2):
-        position = lax.rem(x_place + rel, jnp.int32(2))
-        rows = pl.ds(pl.multiple_of(position * count, count), count)
-        keys[rows, :] = qkv[2 * sequence + rel, :, pl.ds(lane0 + 2 * LANES, LANES)]
-        values[rows, :] = qkv[2 * sequence + rel, :, pl.ds(lane0 + 3 * LANES, LANES)]
-
-    def visit(rel, start, before):
-        block = 2 * sequence + rel
+    places = [2 * sequence + lax.rem(x_place + position, jnp.int32(2)) for position in range(2)]
+    for position, block in enumerate(places):
+        rows = slice(position * count, (position + 1) * count)
+        keys[rows, :] = qkv[block, :, pl.ds(lane0 + 2 * LANES, LANES)]
+        values[rows, :] = qkv[block, :, pl.ds(lane0 + 3 * LANES, LANES)]
+
+    def visit(block, start, before):
         rows = slice(start, start + TILE)
         queries = jnp.concatenate(
             [qkv[block, rows, pl.ds(lane0, LANES)], qkv[block, rows, pl.ds(lane0 + LANES, LANES)]], axis=0
@@ -412,14 +412,9 @@
             kept = jnp.where(lane == 2 * pair + head, log[part], kept)
         logs[block, rows, :] = kept
 
-    for rel in range(2):
-        position = lax.rem(x_place + rel, jnp.int32(2))
-        for static_position in range(2):
-
-            @pl.when(position == static_position)
-            def _(rel=rel, static_position=static_position):
-                for step in range(count // TILE):
-                    visit(rel, step * TILE, static_position * count + step * TILE)
+    for position, block in enumerate(places):
+        for step in range(count // TILE):
+            visit(block, step * TILE, position * count + step * TILE)
 
 
 def forward_kernel(
@@ -615,9 +610,9 @@
     kept.append(keep_local(out_wide, out_wide_out, 10))
 
     def out_part(block):
-        @pl.loop(0, out_wide.shape[0] // 512)
+        @pl.loop(0, out_wide.shape[0] // WIDE)
         def _(step):
-            lanes = pl.ds(pl.multiple_of(step * 512, 512), 512)
+            lanes = pl.ds(pl.multiple_of(step * WIDE, WIDE), WIDE)
             parts[block, :, lanes] = times_transposed(heads[block], out_wide[lanes, :]).astype(jnp.bfloat16)
 
     out_part(3)
@@ -733,7 +728,9 @@
     )(cotangent, tokens, gains, halves, *spreads, cosine, sine)
 
 
-EARLY = 6
+EARLY = 7
+ORDER = (1, 3, 2, 0)
+HOPS = {(0, 1): 0, (0, 3): 1, (0, 2): 2, (1, 1): 3}
 
 
 def ring_row(shift, deep, rows):
@@ -756,7 +753,7 @@
 
 
 def pieces_of(deep):
-    return [(piece, shift) for piece in range(3) for shift in range(deep)]
+    return [(piece, shift) for piece in range(3) for shift in ORDER[:deep]]
 
 
 def feed_back_kernel(
@@ -787,10 +784,10 @@
     row_loads = {}
     for block in (3, 1):
         row_loads[block] = [load(rows_hbm.at[block], rows.at[block], load_sems.at[0, block])]
-    weight_loads = []
-    for matrix, target in enumerate((gate, up, down)):
+    weight_loads = {}
+    for side in range(2):
         here = []
-        for side in range(2):
+        for matrix, target in enumerate((gate, up, down)):
             for shift in range(deep):
                 for rel in range(2):
                     here.append(
@@ -800,8 +797,8 @@
                             weight_sems.at[matrix, side, shift, rel],
                         )
                     )
-        weight_loads.append(here)
-        if matrix == 0:
+        weight_loads[side] = here
+        if side == 0:
             for block in (3, 1):
                 row_loads[block].append(load(grads_hbm.at[block], grads.at[block], load_sems.at[1, block]))
     for block in (2, 0):
@@ -812,9 +809,10 @@
     middle_load = load(middle_hbm, middle, load_sems.at[0, 4])
 
     def inner(block):
-        @pl.loop(0, gate.shape[1] // TILE)
-        def _(step):
-            lanes = pl.ds(pl.multiple_of(step * TILE, TILE), TILE)
+        for side in range(2):
+            for copy in weight_loads.pop(side, ()):
+                copy.wait()
+            lanes = slice(side * half, (side + 1) * half)
             gate_value = nn(rows[block], gate[:, lanes])
             up_value = nn(rows[block], up[:, lanes])
             grad_hidden = nn(grads[block], down[:, lanes])
@@ -826,21 +824,17 @@
             grad_up[block, :, lanes] = (grad_hidden * swish).astype(jnp.bfloat16)
 
     def outer(block):
-        @pl.loop(0, width // TILE)
+        @pl.loop(0, width // WIDE)
         def _(step):
-            lanes = pl.ds(pl.multiple_of(step * TILE, TILE), TILE)
+            lanes = pl.ds(pl.multiple_of(step * WIDE, WIDE), WIDE)
             parts[block, :, lanes] = (
                 times_transposed(grad_gate[block], gate[lanes, :])
                 + times_transposed(grad_up[block], up[lanes, :])
             ).astype(jnp.bfloat16)
 
-    for position, block in enumerate((3, 1, 2, 0)):
+    for block in (3, 1, 2, 0):
         for copy in row_loads[block]:
             copy.wait()
-        if position == 0:
-            for here in weight_loads:
-                for copy in here:
-                    copy.wait()
         inner(block)
         if block in (3, 1):
             outer(block)
@@ -866,6 +860,18 @@
         row = ring_row(shift, deep, piece_rows)
         stage[piece, pl.ds(row, piece_rows), :] = weight_part(piece, side, shift).astype(jnp.bfloat16)
 
+    def weight_whole(piece, side):
+        left, right = sources[piece]
+        lanes = slice(side * half, (side + 1) * half)
+
+        @pl.loop(0, width // WIDE)
+        def _(step):
+            row = pl.multiple_of(step * WIDE, WIDE)
+            stage[piece, pl.ds(row, WIDE), :] = transposed_times(
+                left[:, :, pl.ds(row, WIDE)].reshape(blocks * count, WIDE),
+                right[:, :, lanes].reshape(blocks * count, half),
+            ).astype(jnp.bfloat16)
+
     early = pieces_of(deep)[:EARLY]
     arrivals, stores, pending = [], [], []
 
@@ -876,9 +882,13 @@
         pending.clear()
 
     def send_piece(piece):
-        for shift in range(deep):
-            weight_stage(piece, 1, shift)
+        if piece:
+            weight_whole(piece, 1)
             flush()
+        for shift in ORDER:
+            if not piece:
+                weight_stage(piece, 1, shift)
+                flush()
             rows_here = pl.ds(ring_row(shift, deep, piece_rows), piece_rows)
             target = sent_out.at[piece, rows_here, :]
             store = load(stage.at[piece, rows_here, :], target, early_sems.at[piece * deep + shift])
@@ -896,6 +906,23 @@
     send_piece(2)
     flush()
     late_stores = list(stores)
+    hops = []
+
+    def join_early(pairs):
+        for piece, shift in pairs:
+            index = early.index((piece, shift))
+            product = weight_part(piece, 0, shift)
+            arrivals[index].wait_recv()
+            early_y[index] = (product + early_y[index].astype(jnp.float32)).astype(jnp.bfloat16)
+            if (piece, shift) in HOPS:
+                number = HOPS[piece, shift]
+                hops.append(
+                    move(early_y.at[index], arrived_out.at[number], z_sems, number, z_ahead[shift])
+                )
+            else:
+                stores.append(load(early_y.at[index], sum_out.at[index], sum_sems.at[index]))
+
+    join_early(early[:2])
     near.wait_recv()
     middle_load.wait()
     across.wait_recv()
@@ -918,30 +945,15 @@
     stores.append(load(incoming, grad_attention_out.at[0], store_sems.at[0]))
     stores.append(load(middle, grad_middle_out, store_sems.at[3]))
 
-    hops = []
-
-    def join_early(pairs):
-        for piece, shift in pairs:
-            index = early.index((piece, shift))
-            product = weight_part(piece, 0, shift)
-            arrivals[index].wait_recv()
-            early_y[index] = (product + early_y[index].astype(jnp.float32)).astype(jnp.bfloat16)
-            if piece == 0 and shift:
-                hops.append(
-                    move(early_y.at[index], arrived_out.at[shift - 1], z_sems, shift, z_ahead[shift])
-                )
-            else:
-                stores.append(load(early_y.at[index], sum_out.at[index], sum_sems.at[index]))
-
-    join_early(early[:-2])
+    join_early(early[2:4])
     far.wait_send()
     across.wait_send()
     near.wait_send()
 
     def branch(block):
-        @pl.loop(0, width // TILE)
+        @pl.loop(0, width // WIDE)
         def _(step):
-            lanes = pl.ds(pl.multiple_of(step * TILE, TILE), TILE)
+            lanes = pl.ds(pl.multiple_of(step * WIDE, WIDE), WIDE)
             parts[block, :, lanes] = times_transposed(hidden[block], down[lanes, :]).astype(jnp.bfloat16)
 
     branch(3)
@@ -960,9 +972,13 @@
     for copy in late_stores:
         copy.wait()
     for piece in range(3):
+        whole = piece not in [pair[0] for pair in early]
+        if whole:
+            weight_whole(piece, 0)
         for shift in range(deep):
             if (piece, shift) not in early:
-                weight_stage(piece, 0, shift)
+                if not whole:
+                    weight_stage(piece, 0, shift)
                 rows_here = pl.ds(ring_row(shift, deep, piece_rows), piece_rows)
                 stores.append(
                     load(
@@ -971,7 +987,7 @@
                         early_sems.at[(3 + piece) * deep + shift],
                     )
                 )
-    join_early(early[-2:])
+    join_early(early[4:])
     attention_x.wait_recv()
     attention_far = move(grad_attention_out.at[1], grad_attention_out.at[3], core_sems, 5, core_beside)
     attention_far.wait_recv()
@@ -1003,7 +1019,7 @@
         shape(3, width, half),
         shape(3, width, half),
         shape(EARLY, 2 * part, half),
-        shape(deep - 1, 2 * part, half),
+        shape(len(HOPS), 2 * part, half),
     )
     dma = pltpu.SemaphoreType.DMA
     return pl.pallas_call(
@@ -1034,16 +1050,15 @@
     mask = diagonal_mask()
     factor = HD ** (-0.5)
     scale = factor * LOG2E
-    for rel in range(2):
-        position = lax.rem(x_place + rel, jnp.int32(2))
-        rows = pl.ds(pl.multiple_of(position * count, count), count)
-        keys[rows, :] = qkv[2 * sequence + rel, :, pl.ds(lane0 + 2 * LANES, LANES)]
-        values[rows, :] = qkv[2 * sequence + rel, :, pl.ds(lane0 + 3 * LANES, LANES)]
+    places = [2 * sequence + lax.rem(x_place + position, jnp.int32(2)) for position in range(2)]
+    for position, block in enumerate(places):
+        rows = slice(position * count, (position + 1) * count)
+        keys[rows, :] = qkv[block, :, pl.ds(lane0 + 2 * LANES, LANES)]
+        values[rows, :] = qkv[block, :, pl.ds(lane0 + 3 * LANES, LANES)]
     grad_keys[...] = jnp.zeros_like(grad_keys)
     grad_values[...] = jnp.zeros_like(grad_values)
 
-    def visit(rel, start, before):
-        block = 2 * sequence + rel
+    def visit(block, start, before):
         rows = slice(start, start + TILE)
 
         def both(ref, first):
@@ -1084,19 +1099,12 @@
                 jnp.bfloat16
             )
 
-    for rel in range(2):
-        position = lax.rem(x_place + rel, jnp.int32(2))
-        for static_position in range(2):
-
-            @pl.when(position == static_position)
-            def _(rel=rel, static_position=static_position):
-                for step in range(count // TILE):
-                    visit(rel, step * TILE, static_position * count + step * TILE)
-
-    for rel in range(2):
-        block = 2 * sequence + rel
-        position = lax.rem(x_place + rel, jnp.int32(2))
-        rows = pl.ds(pl.multiple_of(position * count, count), count)
+    for position, block in enumerate(places):
+        for step in range(count // TILE):
+            visit(block, step * TILE, position * count + step * TILE)
+
+    for position, block in enumerate(places):
+        rows = slice(position * count, (position + 1) * count)
         grad_qkv[block, :, pl.ds(lane0 + 2 * LANES, LANES)] = turn(
             grad_keys[rows, :] * factor, cosine_ref[position], -sine_ref[position]
         ).astype(jnp.bfloat16)
@@ -1110,8 +1118,8 @@
     first_part, first_core, first_x, branch_x, feed_final, qkv_final, out_final, first_gain_out, second_gain_out,
     grad_attention, qkv, heads, grad_heads, logs, grad_qkv, qkv_wide, out_wide, keys, values, grad_keys,
     grad_values, slots, landing, feed_sum, feed_y, feed_z, out_sent, out_sum, out_y, out_z, qkv_sent, qkv_sum, qkv_y,
-    qkv_z, feed_last, qkv_last, out_last, feed_weight, qkv_weight, gain_part, gain_in, gain_total,
-    load_sems, own_sems, tile_sems, core_sems, x_sems, y_sems, z_sems, gain_sems,
+    qkv_z, feed_pass, out_pass, qkv_pass, feed_last, qkv_last, out_last, feed_weight, qkv_weight, gain_part, gain_in, gain_total,
+    load_sems, own_sems, tile_sems, core_sems, x_sems, y_sems, z_sems, pass_sems, gain_sems,
 ):
     blocks, count, width = grad_attention.shape
     core_beside, x_beside, y_beside = beside()
@@ -1168,9 +1176,9 @@
             )
         elif shift == 0:
             early_loads.append(load(sum_hbm.at[index], feed_sum.at[piece, 0], own_sems.at[1, index]))
-        elif piece == 0:
+        elif (piece, shift) in HOPS:
             early_loads.append(
-                load(arrived_hbm.at[shift - 1], feed_z.at[piece, shift - 1], own_sems.at[1, index])
+                load(arrived_hbm.at[HOPS[piece, shift]], feed_z.at[piece, shift - 1], own_sems.at[1, index])
             )
         else:
             z_copies[piece, shift] = move(
@@ -1200,16 +1208,69 @@
         product = transposed_times(left.reshape(blocks * count, piece_rows), right)
         return times_transposed(product.astype(jnp.bfloat16), spread[...]).astype(jnp.bfloat16)
 
-    def join_piece(name, number, total, arrived, target, shift):
+    guarded = []
+    z_place = lax.axis_index("z").astype(jnp.int32)
+    last = deep - 1
+    inside = (z_place > 0) & (z_place < last)
+    inward = {"z": jnp.where(z_place == 0, jnp.int32(1), jnp.int32(last - 1))}
+
+    def remote(source, target, sems, index, where):
+        return pltpu.make_async_remote_copy(
+            src_ref=source,
+            dst_ref=target,
+            send_sem=sems.at[0, index],
+            recv_sem=sems.at[1, index],
+            device_id=where,
+            device_id_type=pl.DeviceIdType.MESH,
+        )
+
+    def begin(copy, condition):
+        pl.when(condition)(copy.start)
+        guarded.append((copy, condition))
+
+    def clear(target):
+        @pl.when(z_place == 0)
+        def _():
+            target[0] = jnp.zeros(target.shape[1:], target.dtype)
+
+        @pl.when(z_place == last)
+        def _():
+            target[last - 1] = jnp.zeros(target.shape[1:], target.dtype)
+
+    def join_piece(name, number, total, arrived, target, passing, shift):
         add_rows(total.at[shift], arrived.at[shift])
-        if shift:
-            z_copies[name, shift] = move(
-                total.at[shift], target.at[shift - 1], z_sems, number * (deep - 1) + shift - 1, z_ahead[shift]
-            )
+        if not shift:
+            return
+        direct = remote(total.at[shift], target.at[shift - 1], z_sems, number * last + shift - 1, z_ahead[shift])
+        if passing is None:
+            direct.start()
+            sent.append(direct)
+        else:
+            far = z_place == (last if shift == 1 else 0)
+            through = remote(total.at[shift], passing, pass_sems, number, inward)
+            if shift == 2:
+
+                @pl.when(inside)
+                def _():
+                    through.wait_recv()
+                    add_rows(total.at[shift], passing)
+
+                direct.start()
+                sent.append(direct)
+            else:
+                begin(through, far)
+                begin(direct, jnp.logical_not(far))
+        z_copies[name, shift] = direct
 
     def join_feed(piece, shift):
         own_loads[piece, shift].wait()
-        join_piece(piece, piece, feed_sum.at[piece], feed_y.at[piece], feed_z.at[piece], shift)
+        join_piece(
+            piece, piece, feed_sum.at[piece], feed_y.at[piece], feed_z.at[piece],
+            feed_pass if piece == 2 else None, shift,
+        )
+
+    for target in (feed_z.at[2], out_z, qkv_z):
+        clear(target)
 
     def join_feed_late(index):
         late_copies[index].wait_recv()
@@ -1224,24 +1285,24 @@
                 qkv, grad_heads, heads, logs, cosine_ref, sine_ref, grad_qkv, keys, values, grad_keys,
                 grad_values, sequence, pair,
             )
-            join_feed_late(2 * sequence + pair)
+        join_feed_late(sequence)
     wide_load.wait()
 
-    def first_tile(shift):
-        row = ring_row(shift, deep, piece_rows)
-        slot = (shift % 2) * 512
+    def first_tile(order):
+        row = ring_row(ORDER[order], deep, piece_rows)
+        slot = (order % 2) * 512
         return load(
             first_hbm.at[:, :, pl.ds(row, piece_rows)],
             qkv.at[:, :, pl.ds(slot, piece_rows)],
-            tile_sems.at[shift],
+            tile_sems.at[order],
         )
 
-    first_loads = [first_tile(shift) for shift in range(2)]
+    first_loads = [first_tile(order) for order in range(2)]
 
     def first_piece(block):
-        @pl.loop(0, width // 512)
+        @pl.loop(0, width // WIDE)
         def _(step):
-            lanes = pl.ds(pl.multiple_of(step * 512, 512), 512)
+            lanes = pl.ds(pl.multiple_of(step * WIDE, WIDE), WIDE)
             slots[block % 3, :, lanes] = times_transposed(grad_qkv[block], qkv_wide[lanes, :]).astype(
                 jnp.bfloat16
             )
@@ -1258,43 +1319,48 @@
     sent[:] = [copy for copy in sent if copy is not core_far]
     first_piece(0)
     first_store = load(slots.at[0], first_part, load_sems.at[8])
-    join_feed_late(4)
+    join_feed_late(2)
     y_index = len(late)
-    out_copies = []
-    for shift in range(deep):
+    out_copies = {}
+    for shift in ORDER:
         row = ring_row(shift, deep, piece_rows)
         out_sent[shift] = weight_tile(grad_attention[:, :, pl.ds(row, piece_rows)], heads, out_spread, 1)
-        out_copies.append(move(out_sent.at[shift], out_y.at[shift], y_sems, y_index + shift, y_beside))
+        out_copies[shift] = move(out_sent.at[shift], out_y.at[shift], y_sems, y_index + shift, y_beside)
 
     @pl.loop(0, deep)
     def _(shift):
         row = ring_row(shift, deep, piece_rows)
         out_sum[shift] = weight_tile(grad_attention[:, :, pl.ds(row, piece_rows)], heads, out_spread, 0)
 
-    join_feed_late(5)
-
-    qkv_copies = []
+    join_feed_late(3)
+
+    qkv_copies = {}
     y_index += deep
-    for shift in range(deep):
-        first_loads[shift].wait()
-        slot = (shift % 2) * 512
+    for order, shift in enumerate(ORDER):
+        first_loads[order].wait()
+        slot = (order % 2) * 512
         left = qkv[:, :, slot : slot + piece_rows]
         qkv_sent[shift] = weight_tile(left, grad_qkv, qkv_spread, 1)
-        qkv_copies.append(move(qkv_sent.at[shift], qkv_y.at[shift], y_sems, y_index + shift, y_beside))
+        qkv_copies[shift] = move(qkv_sent.at[shift], qkv_y.at[shift], y_sems, y_index + shift, y_beside)
         qkv_sum[shift] = weight_tile(left, grad_qkv, qkv_spread, 0)
-        if shift + 2 < deep:
-            first_loads.append(first_tile(shift + 2))
-
-    for shift in range(deep):
+        if order + 2 < deep:
+            first_loads.append(first_tile(order + 2))
+
+    join_feed_late(4)
+    for shift in ORDER:
         out_copies[shift].wait_recv()
-        join_piece("out", 3, out_sum, out_y, out_z, shift)
+        join_piece("out", 3, out_sum, out_y, out_z, out_pass, shift)
 
     finals = []
 
     def finish(name, number, total, arrived, last, final, weights):
         for shift in range(1, deep):
-            if (name, shift) in z_copies:
+            if (name, shift) not in z_copies:
+                continue
+            if name in (0, 1) or shift == 2:
                 z_copies[name, shift].wait_recv()
+            else:
+                pl.when(z_place != (0 if shift == 1 else deep - 1))(z_copies[name, shift].wait_recv)
         size = total.shape[2]
         sums = []
         for rel in range(2):
@@ -1344,9 +1410,9 @@
     gate_sums = finish(
         1, 1, feed_sum.at[1], feed_z.at[1], feed_last.at[1], feed_final.at[1], feed_weight.at[:, :, pl.ds(0, half)]
     )
-    for shift in range(deep):
+    for shift in ORDER:
         qkv_copies[shift].wait_recv()
-        join_piece("qkv", 4, qkv_sum, qkv_y, qkv_z, shift)
+        join_piece("qkv", 4, qkv_sum, qkv_y, qkv_z, qkv_pass, shift)
     up_sums = finish(
         2, 2, feed_sum.at[2], feed_z.at[2], feed_last.at[2], feed_final.at[2],
         feed_weight.at[:, :, pl.ds(half, half)],
@@ -1366,6 +1432,8 @@
         copy.wait()
     for copy in sent:
         copy.wait_send()
+    for copy, condition in guarded:
+        pl.when(condition)(copy.wait_send)
 
 
 def heads_back(
@@ -1422,6 +1490,9 @@
         room(deep, rows, qkv_half),
         room(deep, rows, qkv_half),
         room(deep - 1, rows, qkv_half),
+        room(rows, half),
+        room(rows, out_half),
+        room(rows, qkv_half),
         room(3, 2, part, half, kind=wide),
         room(2, part, qkv_half, kind=wide),
         room(2, part, out_half, kind=wide),
@@ -1437,6 +1508,7 @@
         dma((2, 2)),
         dma((2, 5 * deep)),
         dma((2, 5 * (deep - 1))),
+        dma((2, 5)),
         dma((2, 14)),
     ]
     return pl.pallas_call(

time: 435 us -> 411 us (0.945)
  the two profiles are of different devices: /device:TPU:11 before, /device:TPU:0 now
where the time goes in v5:
time: 411 us; the launch traced here: 403 us
  Pallas kernels  378 us (92%)
  other arithmetic  15.7 us (4%)
  local copies, waits for them, and re-layouts  7.71 us (2%)
    pallas_call x1, Pallas kernels, forward(): pl.pallas_call(functools.partial(forward_kernel, deep), out_shape=outs, i...  167 us
    pallas_call x1, Pallas kernels, feed_back(): pl.pallas_call(functools.partial(feed_back_kernel, deep), out_shape=outs,...  107 us
    pallas_call x1, Pallas kernels, heads_back(): pl.pallas_call(functools.partial(heads_back_kernel, deep), out_shape=outs...  104 us

profile of v5, /device:TPU:0, one launch (start us, length us, event | category | flops | bytes accessed | tf_op | source)
XLA Modules:
  0.0 403.1 jit_solution(3650340417149127193)
XLA Ops:
  0.6 1.3 fusion.7
  1.9 1.2 fusion.10
  3.1 1.1 fusion.12
  4.2 1.1 fusion.9
  5.2 0.0 copy-start.9
  5.2 0.0 copy-start.12
  5.2 0.3 concatenate.27
  5.6 0.3 concatenate.28
  5.9 1.4 pad_maximum_fusion.all_halves
  7.3 0.6 pad_maximum_fusion.6.gains_ref.gain_ref
  7.9 167.4 %forward.1 = (bf16[4,512,1536]{2,1,0:T(8,128)(2,1)}, bf16[4,512,1024]{2,1,0:T(8,128)(2,1)}, bf16[4,512,512]{2,1,0:T(8,128)(2,1)}, f32[4,512,128]{2,1,0:T(8,128)}...) custom-call(bf16[512,1536]{1,0:T(8,128)(2,1)} %cotangent_ref.1, ...), custom_call_target="tpu_custom_call" | custom-call | flops 1000000000 | bytes 5000000 | tf_op jit(solution)/shard_map/forward/pallas_call | solution.py:719
  175.4 106.7 %feed_back.1 = (f32[512,1536]{1,0:T(8,128)}, bf16[4,512,1536]{2,1,0:T(8,128)(2,1)}, bf16[3,512,1536]{2,1,0:T(8,128)(2,1)}, bf16[3,1536,512]{2,1,0:T(8,128)(2,1)}...) custom-call(bf16[4,512,1536]{2,1,0:T(8,128)(2,1)} %get-tuple-element.39.rows_hbm, ...), custom_call_target="tpu_custom_call" | custom-call | flops 4000000000 | bytes 5000000 | tf_op jit(solution)/shard_map/feed_back/pallas_call | solution.py:1025
  282.0 104.2 %heads_back.1 = (bf16[512,1536]{1,0:T(8,128)(2,1)}, bf16[512,1536]{1,0:T(8,128)(2,1)}, bf16[512,1536]{1,0:T(8,128)(2,1)}, bf16[512,1536]{1,0:T(8,128)(2,1)}, f32...) custom-call(bf16[4,512,1536]{2,1,0:T(8,128)(2,1)} %get-tuple-element, ...), custom_call_target="tpu_custom_call" | custom-call | flops 1500000000 | bytes 5000000 | tf_op jit(solution)/shard_map/heads_back/pallas_call | solution.py:1514
  386.3 1.8 slice_bitcast_fusion.1
  388.2 0.9 maximum_bitcast_fusion
  389.1 0.9 pad_maximum_fusion.2
  390.1 0.9 pad_maximum_fusion.1
  391.0 0.8 maximum_bitcast_fusion.1
  391.9 0.2 slice_bitcast_fusion.11
  392.0 0.8 pad_maximum_fusion.5
  392.8 0.8 pad_maximum_fusion.4
  393.7 0.8 pad_maximum_fusion.3
  394.5 0.0 slice-start
  394.5 1.3 fusion
  395.8 0.0 slice-start.1
  395.9 3.0 fusion.3
  398.8 0.4 copy-done.6
  399.2 2.0 fusion.6
  401.2 0.1 reduce_sum.39
  401.3 0.6 dynamic-slice_divide_fusion
  401.9 0.1 reduce_sum.38
  402.0 0.6 dynamic-slice_divide_fusion.1
  (32 shorter events, 0.1 us)
Async XLA Ops:
  5.2 2.0 copy-start.9
  5.2 2.0 copy-start.12
  388.1 2.9 copy-start.8
  388.2 3.7 copy-start.7
  389.1 5.4 %copy-start.4 = (bf16[512,1536]{1,0:T(8,128)(2,1)S(1)}, bf16[512,1536]{1,0:T(8,128)(2,1)}, u32[]{:S(2)}) copy-start(bf16[512,1536]{1,0:T(8,128)(2,1)} %get-tuple-element.59) | copy-start | bytes 4718596
  390.0 4.5 %copy-start = (bf16[512,1536]{1,0:T(8,128)(2,1)S(1)}, bf16[512,1536]{1,0:T(8,128)(2,1)}, u32[]{:S(2)}) copy-start(bf16[512,1536]{1,0:T(8,128)(2,1)} %tokens_ref.1) | copy-start | bytes 4718596
  390.1 4.5 %copy-start.2 = (bf16[512,1536]{1,0:T(8,128)(2,1)S(1)}, bf16[512,1536]{1,0:T(8,128)(2,1)}, u32[]{:S(2)}) copy-start(bf16[512,1536]{1,0:T(8,128)(2,1)} %get-tuple-element.57) | copy-start | bytes 4718596
  390.1 4.5 %copy-start.3 = (bf16[512,1536]{1,0:T(8,128)(2,1)S(1)}, bf16[512,1536]{1,0:T(8,128)(2,1)}, u32[]{:S(2)}) copy-start(bf16[512,1536]{1,0:T(8,128)(2,1)} %get-tuple-element.58) | copy-start | bytes 4718596
  393.7 2.2 copy-start.5
  394.5 4.3 %slice-start = ((s8[4718592]{0:T(1024)(128)(4,1)}), s8[4194304]{0:T(1024)(128)(4,1)S(1)}, s32[]{:S(2)}) async-start(s8[4718592]{0:T(1024)(128)(4,1)} %bitcast.42), calls=%async_computation | async-start | bytes 8388608
  395.8 3.0 slice-start.1
  395.8 3.0 copy-start.1
  395.9 3.4 copy-start.6
  399.2 2.0 copy-start.11
  399.2 2.7 copy-start.10
